TPU v7x, 512 devices: a whole 4x4x16 slice. The times are simulated.
512 devices in a mesh: fsdp: 32 (over z, core), tensor: 16 (over x, y).
Axes of the slice: x: 4, y: 4, z: 16, core: 2. Of those that a mesh axis runs over, the one named last changes fastest.
Arguments:
- weights: bfloat16 [8192, 14336], P('fsdp', 'tensor'), may hold values from -6 to 6
- momentum: float32 [8192, 14336], P('fsdp', 'tensor'), may hold values from -40 to 40
- gradient: bfloat16 [8192, 14336], P('fsdp', 'tensor'), may hold values from -20 to 20
- warm_basis: float32 [512, 14336], P('fsdp', 'tensor'), may hold values from -6 to 6
Outputs:
- new_weights: bfloat16 [8192, 14336], P('fsdp', 'tensor')
- new_momentum: float32 [8192, 14336], P('fsdp', 'tensor')
- new_basis: float32 [512, 14336], P('fsdp', 'tensor')
All inputs are finite; a program needn't handle non-finite values.
Results may differ from a plain program's by a relative error of at most 0.001.
Values sent between devices are 32-bit elements; how exact they have to be, the bound alone decides.
No kernel may reach another device: no remote copies, remote signals or barrier semaphores. Data moves between devices by JAX's collectives and lax.ppermute only.
A program may use at most 64 MiB of HBM per device.

v0:
```python
import math

import jax
import jax.numpy as jnp
from jax import lax
from jax.sharding import PartitionSpec as P

D = 8192
FF = 14336


momentum_decay = 0.95
step_size = 2.0
epsilon = 1e-06


def highest_dot(left_side, right_side, contract_left, contract_right):
    return lax.dot_general(
        left_side,
        right_side,
        (((contract_left,), (contract_right,)), ((), ())),
        precision=lax.Precision.HIGHEST,
        preferred_element_type=jnp.float32,
    )


def orthonormalize(projected, gram):
    factor = jnp.linalg.cholesky(gram)
    return lax.linalg.triangular_solve(
        factor, projected, left_side=False, lower=True, transpose_a=True
    )


def on_device(weights, momentum, gradient, warm_basis):
    owned = warm_basis.shape[0]
    blended = momentum + gradient.astype(jnp.float32)
    partial_projection = highest_dot(
        blended, lax.all_gather(warm_basis, "fsdp", axis=0, tiled=True), 1, 1
    )
    projected = lax.psum(partial_projection, "tensor")
    gram = lax.psum(highest_dot(projected, projected, 0, 0), "fsdp")
    orthonormal = orthonormalize(projected, gram)
    coefficients = lax.psum(highest_dot(orthonormal, blended, 0, 0), "fsdp")
    energy = lax.psum(jnp.sum(coefficients * coefficients, axis=1), "tensor")
    full_basis = coefficients * lax.rsqrt(energy / FF + epsilon)[:, None]
    feedback = highest_dot(orthonormal, coefficients, 1, 0)
    update = highest_dot(orthonormal, full_basis, 1, 0)
    new_basis = lax.dynamic_slice_in_dim(full_basis, lax.axis_index("fsdp") * owned, owned, 0)
    new_momentum = blended - (1.0 - momentum_decay) * feedback
    new_weights = (weights.astype(jnp.float32) - step_size * math.sqrt(D / FF) * update).astype(
        jnp.bfloat16
    )
    return (new_weights, new_momentum, new_basis)


def solution(mesh):
    in_specs = (P("fsdp", "tensor"), P("fsdp", "tensor"), P("fsdp", "tensor"), P("fsdp", "tensor"))
    out_specs = (P("fsdp", "tensor"), P("fsdp", "tensor"), P("fsdp", "tensor"))
    return jax.shard_map(
        on_device, mesh=mesh, in_specs=in_specs, out_specs=out_specs, check_vma=False
    )
```

profile of v0, /device:TPU:1, one launch (start us, length us, event | category | flops | bytes accessed | tf_op | source)
XLA Modules:
  0.0 823.4 jit_solution(674419299690827047)
XLA Ops:
  7.9 79.5 %all-gather.2.cloned.1.call-done = f32[512,896]{1,0:T(8,128)} async-done(((f32[16,896]{1,0:T(8,128)}), f32[512,896]{1,0:T(8,128)}) %all-gather.2.cloned.1.call-update) | async-done | bytes 1835024 | tf_op jit(solution)/shard_map/all_gather | solution.py:38
  87.4 4.6 fusion.10
  92.2 111.2 %all-reduce.5.cloned.1.call-done = f32[256,512]{1,0:T(8,128)} async-done(((f32[256,512]{1,0:T(8,128)}), f32[256,512]{1,0:T(8,128)}) %all-reduce.5.cloned.1.call-update) | async-done | bytes 524304 | tf_op jit(solution)/shard_map/psum | solution.py:40
  203.4 3.3 fusion.39
  207.2 210.9 %all-reduce.7.cloned.1.call-done = f32[512,512]{0,1:T(8,128)} async-done(((f32[512,512]{0,1:T(8,128)}), f32[512,512]{0,1:T(8,128)}) %all-reduce.7.cloned.1.call-update) | async-done | bytes 1048592 | tf_op jit(solution)/shard_map/psum | solution.py:41
  420.1 11.7 %cholesky.104 = f32[128,128]{1,0:T(8,128)S(1)} custom-call(f32[128,128]{1,0:T(8,128)S(1)} %cholesky.266), custom_call_target="Cholesky" | custom-call | tf_op jit(solution)/shard_map/jit(cholesky)/cholesky | solution.py:28
  431.8 9.8 %custom-call.30 = f32[1,128,128]{1,2,0:T(8,128)S(1)} custom-call(f32[1,128,128]{2,1,0:T(8,128)S(1)} %get-tuple-element.30), custom_call_target="InvertDiagBlocksLowerTriangular" | custom-call | tf_op jit(solution)/shard_map/jit(cholesky)/cholesky | solution.py:28
  442.4 11.7 %cholesky.217 = f32[128,128]{1,0:T(8,128)S(1)} custom-call(f32[128,128]{1,0:T(8,128)S(1)} %cholesky.270), custom_call_target="Cholesky" | custom-call | tf_op jit(solution)/shard_map/jit(cholesky)/cholesky | solution.py:28
  454.2 10.0 %custom-call.31 = f32[1,128,128]{1,2,0:T(8,128)S(1)} custom-call(f32[1,128,128]{2,1,0:T(8,128)S(1)} %get-tuple-element.27), custom_call_target="InvertDiagBlocksLowerTriangular" | custom-call | tf_op jit(solution)/shard_map/jit(cholesky)/cholesky | solution.py:28
  464.8 11.7 %cholesky.238 = f32[128,128]{1,0:T(8,128)S(1)} custom-call(f32[128,128]{1,0:T(8,128)S(1)} %cholesky.275), custom_call_target="Cholesky" | custom-call | tf_op jit(solution)/shard_map/jit(cholesky)/cholesky | solution.py:28
  477.3 9.8 %custom-call.32 = f32[1,128,128]{1,2,0:T(8,128)S(1)} custom-call(f32[1,128,128]{2,1,0:T(8,128)S(1)} %get-tuple-element.24), custom_call_target="InvertDiagBlocksLowerTriangular" | custom-call | tf_op jit(solution)/shard_map/jit(cholesky)/cholesky | solution.py:28
  487.7 11.7 %cholesky.255 = f32[128,128]{1,0:T(8,128)S(1)} custom-call(f32[128,128]{1,0:T(8,128)S(1)} %convolution_subtract_fusion.5), custom_call_target="Cholesky" | custom-call | tf_op jit(solution)/shard_map/jit(cholesky)/cholesky | solution.py:28
  503.6 10.9 %while.1 = (s32[]{:T(128)}, f32[512,512]{1,0:T(8,128)S(1)}, s32[4,2]{0,1:T(2,128)S(1)}, f32[4,128,128]{2,1,0:T(8,128)}, s32[]{:T(128)}) while((s32[]{:T(128)}, f32[512,512]{1,0:T(8,128)S(1)}, s32[4,2]{0,1:T(2,128)S(1)}, f32[4,128,128]{2,1,0:T(8,128)}, s32[]{:T(128)}) %tuple.31), condition=%wide.while_cond, body=%wide.while_body.sunk | while | flops 2 | bytes 132705 | solution.py:29
  504.3 2.1 bitcast_dynamic-update-slice_fusion.2
  507.0 2.1 bitcast_dynamic-update-slice_fusion.2
  509.8 2.1 bitcast_dynamic-update-slice_fusion.2
  512.5 2.1 bitcast_dynamic-update-slice_fusion.2
  514.6 40.2 %custom-call.33 = f32[4,128,128]{1,2,0:T(8,128)S(1)} custom-call(f32[4,128,128]{2,1,0:T(8,128)} %get-tuple-element.10), custom_call_target="InvertDiagBlocksLowerTriangular" | custom-call | tf_op jit(solution)/shard_map/triangular_solve | solution.py:29
  558.0 3.1 fusion.9
  561.1 213.1 %all-reduce.9.cloned.1.call-done = f32[512,896]{1,0:T(8,128)} async-done(((f32[512,896]{1,0:T(8,128)}), f32[512,896]{1,0:T(8,128)}) %all-reduce.9.cloned.1.call-update) | async-done | bytes 1835024 | tf_op jit(solution)/shard_map/psum | solution.py:43
  774.2 1.8 multiply_reduce_fusion
  776.0 33.3 %psum.31 = f32[512]{0:T(512)S(1)} all-reduce(f32[512]{0:T(512)S(1)} %multiply_reduce_fusion), channel_id=1, replica_groups=mesh['fsdp'=32,'tensor'=16] {'tensor'}, use_global_device_ids=true, to_apply=%region_12.13 | all-reduce | flops 512 | bytes 4096 | tf_op jit(solution)/shard_map/psum | solution.py:44
  810.5 2.7 fusion.2
  813.8 2.9 fusion
  (67 shorter events, 15.2 us)
Async XLA Ops:
  7.2 80.3 %all-gather.2.cloned.1.call-start = ((), (), s32[]{:S(2)}) async-start(), calls=%async_computation | async-start | bytes 1892352 | tf_op jit(solution)/shard_map/all_gather | solution.py:38
  7.9 195.5 %all-reduce.5.cloned.1.call-start = ((), (), s32[]{:S(2)}) async-start(), calls=%async_computation.1 | async-start | bytes 1048576 | tf_op jit(solution)/shard_map/psum | solution.py:40
  92.1 326.1 %all-reduce.7.cloned.1.call-start = ((), (), s32[]{:S(2)}) async-start(), calls=%async_computation.2 | async-start | bytes 2097152 | tf_op jit(solution)/shard_map/psum | solution.py:41
  206.7 567.5 %all-reduce.9.cloned.1.call-start = ((), (), s32[]{:S(2)}) async-start(), calls=%async_computation.3 | async-start | bytes 3670016 | tf_op jit(solution)/shard_map/psum | solution.py:43
  418.2 1.7 copy-start.3
  476.6 78.2 %copy-start.2 = (f32[256,512]{1,0:T(8,128)S(1)}, f32[256,512]{1,0:T(8,128)}, u32[]{:S(2)}) copy-start(f32[256,512]{1,0:T(8,128)} %all-reduce.5.cloned.1.call-done) | copy-start | bytes 1572868
  514.6 43.4 %copy-start.1 = (f32[256,896]{1,0:T(8,128)S(1)}, f32[256,896]{1,0:T(8,128)}, u32[]{:S(2)}) copy-start(f32[256,896]{1,0:T(8,128)} %param.5) | copy-start | bytes 2752516
  514.6 43.4 %copy-start.4 = (bf16[256,896]{1,0:T(8,128)(2,1)S(1)}, bf16[256,896]{1,0:T(8,128)(2,1)}, u32[]{:S(2)}) copy-start(bf16[256,896]{1,0:T(8,128)(2,1)} %param.6) | copy-start | bytes 1376260
  556.8 1.2 copy-start.6
  774.2 35.2 %copy-start = (f32[512,896]{1,0:T(8,128)S(1)}, f32[512,896]{1,0:T(8,128)}, u32[]{:S(2)}) copy-start(f32[512,896]{1,0:T(8,128)} %all-reduce.9.cloned.1.call-done) | copy-start | bytes 5505028
  809.4 0.9 copy-start.7
  809.4 1.1 copy-start.8
  810.5 3.3 copy-start.5
Sparse Core Ops, SparseCore 0:
  10.1 77.2 all-gather.1
  92.2 111.1 all-reduce.4
  206.8 211.2 all-reduce.6
  561.2 212.9 all-reduce.8
where the time goes:
time: 830 us; the launch traced here: 823 us
  waiting for transfers between devices  615 us (74%)
  other arithmetic  121 us (15%)
  blocking collectives  33.3 us (4%)
  matrix products  21.5 us (3%)
  between operations  16.8 us (2%)
  local copies, waits for them, and re-layouts  14.2 us (2%)
    psum x1, waiting for transfers between devices, on_device(): coefficients = lax.psum(highest_dot(orthonormal, blended, 0, 0), 'fsdp')  213 us
    psum x1, waiting for transfers between devices, on_device(): gram = lax.psum(highest_dot(projected, projected, 0, 0), 'fsdp')  211 us
    psum x1, waiting for transfers between devices, on_device(): projected = lax.psum(partial_projection, 'tensor')  111 us
    all_gather x1, waiting for transfers between devices, on_device(): lax.all_gather(warm_basis, 'fsdp', axis=0, tiled=True)  79.5 us
    another operation x14, other arithmetic, orthonormalize(): factor = jnp.linalg.cholesky(gram)  78.6 us
    another operation x3, other arithmetic, orthonormalize(): lax.linalg.triangular_solve(factor, projected, left_side=False, lower=Tru...  40.6 us
    psum x1, blocking collectives, on_device(): energy = lax.psum(jnp.sum(coefficients * coefficients, axis=1), 'tensor')  33.3 us
  transfers between devices with their start and end apart: 4, of which 4 were waited for; matrix products, arithmetic and copies ran while one was open for 0% of the time, Pallas kernels for 0%

commit v1 on v0

v1 whole, which is shorter than its diff:
```python
import math

import jax
import jax.numpy as jnp
from jax import lax
from jax.sharding import Mesh, PartitionSpec as P

D = 8192
FF = 14336

momentum_decay = 0.95
step_size = 2.0
epsilon = 1e-06

PLANE = ("core", "x", "y")
COLUMN_BLOCKS = ("x", "y")
SWAP = [(0, 1), (1, 0)]


def dot(left_side, right_side, contract_left, contract_right, precision=lax.Precision.HIGHEST):
    return lax.dot_general(
        left_side,
        right_side,
        (((contract_left,), (contract_right,)), ((), ())),
        precision=precision,
        preferred_element_type=jnp.float32,
    )


def exchange(array, axes):
    return lax.all_to_all(array, axes, 0, 0, tiled=True)


def spread(array, axes, count):
    return exchange(
        jnp.broadcast_to(array[None], (count,) + array.shape).reshape(
            (count * array.shape[0],) + array.shape[1:]
        ),
        axes,
    )


def inverse_factor(gram):
    factor = jnp.linalg.cholesky(gram)
    return lax.linalg.triangular_solve(
        factor, jnp.eye(gram.shape[0], dtype=jnp.float32), left_side=True, lower=True
    )


def on_device(weights, momentum, gradient, warm_basis):
    rows, columns = momentum.shape
    owned = warm_basis.shape[0]
    depth = lax.axis_size("z")
    plane = lax.axis_size(PLANE)
    blocks = lax.axis_size(COLUMN_BLOCKS)
    rank = owned * depth * 2
    core = lax.axis_index("core")
    place = lax.axis_index("z")

    blended = momentum + gradient.astype(jnp.float32)
    partner = lax.ppermute(blended, "core", SWAP)
    basis = lax.all_gather(warm_basis, "z", axis=0, tiled=True)
    mine = dot(blended, basis, 1, 1)
    theirs = dot(partner, basis, 1, 1)
    partial = jnp.where(
        core == 0, jnp.stack([mine, theirs]), jnp.stack([theirs, mine])
    ).reshape(2 * rows, rank // 2)
    pieces = exchange(partial, PLANE).reshape(2, blocks, 2 * rows // plane, depth, owned)
    part = jnp.sum(pieces, axis=1).transpose(1, 2, 0, 3).reshape(2 * rows // plane, rank)
    projected = spread(part, PLANE, plane)

    share = rank // plane
    mine_at = lax.axis_index(PLANE) * share
    gram_part = dot(lax.dynamic_slice_in_dim(projected, mine_at, share, 1), projected, 0, 0)
    gram_row = jnp.sum(exchange(gram_part, "z").reshape(depth, share // depth, rank), axis=0)
    gram_share = spread(gram_row, "z", depth)
    gram = spread(gram_share, PLANE, plane)

    half = lax.dynamic_slice_in_dim(projected, core * (rank // 2), rank // 2, 1)
    own_rows = lax.dynamic_slice_in_dim(half, core * rows, rows, 0)
    partner_rows = lax.dynamic_slice_in_dim(half, (1 - core) * rows, rows, 0)
    moved = dot(own_rows, blended, 0, 0) + dot(partner_rows, partner, 0, 0)
    moved = lax.psum_scatter(moved, "z", scatter_dimension=0, tiled=True)
    moved = lax.all_gather(moved, "z", axis=0, tiled=True)
    moved = spread(moved, "core", 2)

    inverse = inverse_factor(gram)
    own_projected = lax.dynamic_slice_in_dim(projected, core * rows, rows, 0)
    orthonormal = dot(own_projected, inverse, 1, 1)
    coefficients = dot(inverse, moved, 1, 0)
    energy = jnp.sum(coefficients * coefficients, axis=1).reshape(rank // 128, 128)
    energy = jnp.sum(
        spread(energy, COLUMN_BLOCKS, blocks).reshape(blocks, rank // 128, 128), axis=0
    ).reshape(rank)
    scale = lax.rsqrt(energy / FF + epsilon)
    feedback = dot(orthonormal, coefficients, 1, 0)
    new_momentum = blended - (1.0 - momentum_decay) * feedback
    update = dot(orthonormal * scale[None, :], coefficients, 1, 0)
    first = (place * 2 + core) * owned
    new_basis = (
        lax.dynamic_slice_in_dim(coefficients, first, owned, 0)
        * lax.dynamic_slice_in_dim(scale, first, owned, 0)[:, None]
    )
    new_weights = (weights.astype(jnp.float32) - step_size * math.sqrt(D / FF) * update).astype(
        jnp.bfloat16
    )
    return (new_weights, new_momentum, new_basis)


def solution(mesh):
    devices = mesh.devices
    split = Mesh(
        devices.reshape(devices.shape[0] // 2, 2, 4, devices.shape[1] // 4),
        ("z", "core", "x", "y"),
    )
    spec = P(("z", "core"), ("x", "y"))
    return jax.shard_map(
        on_device, mesh=split, in_specs=(spec,) * 4, out_specs=(spec,) * 3, check_vma=False
    )
```

time: 830 us -> 390 us (0.47)
  waiting for transfers between devices: 615 us -> 30.7 us
  blocking collectives: 33.3 us -> 124 us
  starting transfers between devices: 0.62 us -> 25.1 us
  matrix products: 21.5 us -> 32.2 us
  local copies, waits for them, and re-layouts: 14.2 us -> 24 us
  other arithmetic: 121 us -> 130 us
    psum x3 -> x0, waiting for transfers between devices: 535 us -> none  [the longest x1 213 us: on_device(): coefficients = lax.psum(highest_dot(orthonormal, blended, 0, 0), 'fsdp')]
    all_gather x1 -> x0, waiting for transfers between devices: 79.5 us -> none  [on_device(): lax.all_gather(warm_basis, 'fsdp', axis=0, tiled=True)]
    all_to_all x0 -> x4, blocking collectives: none -> 69.3 us  [exchange(): return lax.all_to_all(array, axes, 0, 0, tiled=True)]
    all_gather x0 -> x2, blocking collectives: none -> 54.9 us  [the longest x1 29 us: on_device(): basis = lax.all_gather(warm_basis, 'z', axis=0, tiled=True)]
    psum x1 -> x0, blocking collectives: 33.3 us -> none  [on_device(): energy = lax.psum(jnp.sum(coefficients * coefficients, axis=1), 'tensor')]
    all_to_all x0 -> x3, waiting for transfers between devices: none -> 30.7 us  [exchange(): return lax.all_to_all(array, axes, 0, 0, tiled=True)]
    all_to_all x0 -> x3, starting transfers between devices: none -> 15.8 us  [exchange(): return lax.all_to_all(array, axes, 0, 0, tiled=True)]
    ppermute x0 -> x1, starting transfers between devices: none -> 8.79 us  [on_device(): partner = lax.ppermute(blended, 'core', SWAP)]
  transfers between devices with their start and end apart: 4 -> 5, of which waited for: 4 -> 3; matrix products, arithmetic and copies ran while one was open for 0% -> 43% of each run, Pallas kernels for 0% -> 0%
where the time goes in v1:
time: 390 us; the launch traced here: 383 us
  other arithmetic  130 us (33%)
  blocking collectives  124 us (32%)
  matrix products  32.2 us (8%)
  waiting for transfers between devices  30.7 us (8%)
  starting transfers between devices  25.1 us (6%)
  local copies, waits for them, and re-layouts  24 us (6%)
  between operations  17.1 us (4%)
    another operation x14, other arithmetic, inverse_factor(): factor = jnp.linalg.cholesky(gram)  81 us
    all_to_all x4, blocking collectives, exchange(): return lax.all_to_all(array, axes, 0, 0, tiled=True)  69.3 us
    another operation x3, other arithmetic, inverse_factor(): lax.linalg.triangular_solve(factor, jnp.eye(gram.shape[0], dtype=jnp.floa...  41.9 us
    all_to_all x3, waiting for transfers between devices, exchange(): return lax.all_to_all(array, axes, 0, 0, tiled=True)  30.7 us
    all_gather x1, blocking collectives, on_device(): basis = lax.all_gather(warm_basis, 'z', axis=0, tiled=True)  29 us
    all_gather x1, blocking collectives, on_device(): moved = lax.all_gather(moved, 'z', axis=0, tiled=True)  25.8 us
    dot_general x9, matrix products, dot(): lax.dot_general(left_side, right_side, (((contract_left,), (contract_righ...  19 us
    all_to_all x3, starting transfers between devices, exchange(): return lax.all_to_all(array, axes, 0, 0, tiled=True)  15.8 us
  transfers between devices with their start and end apart: 5, of which 3 were waited for; matrix products, arithmetic and copies ran while one was open for 43% of the time, Pallas kernels for 0%

profile of v1, /device:TPU:1, one launch (start us, length us, event | category | flops | bytes accessed | tf_op | source)
XLA Modules:
  0.0 383.5 jit_solution(13313510969681970904)
XLA Ops:
  8.6 8.8 %collective-permute-start = (f32[256,896]{1,0:T(8,128)S(1)}, f32[256,896]{1,0:T(8,128)S(1)}, u32[]{:S(2)}, u32[]{:S(2)}) collective-permute-start(f32[256,896]{1,0:T(8,128)S(1)} %convert_add_fusion), channel_id=1, source_target_pairs={{0,16},{16,0},{1,17},{17,1},{2,18},{18,2},{3,19},{19,3},{4,20},{20... | collective-permute-start | bytes 2752520 | tf_op jit(solution)/shard_map/ppermute | solution.py:61
  17.4 29.0 %all_gather.6 = f32[256,896]{1,0:T(8,128)S(1)} all-gather(f32[16,896]{1,0:T(8,128)S(1)} %copy-done.10), channel_id=1, replica_groups=mesh['z'=16,'core'=2,'x'=4,'y'=4] {'z'}, dimensions={0}, use_global_device_ids=true | all-gather | bytes 974848 | tf_op jit(solution)/shard_map/all_gather | solution.py:62
  48.5 24.5 %all_to_all.54 = f32[32,16,256]{2,1,0:T(8,128)S(1)} all-to-all(f32[32,16,256]{2,1,0:T(8,128)S(1)} %bitcast.83), channel_id=1, replica_groups=mesh['z'=16,'core'=2,'x'=4,'y'=4] {'core','x','y'}, dimensions={0} | all-to-all | bytes 1048576 | tf_op jit(solution)/shard_map/all_to_all | solution.py:31
  79.8 4.7 %all-to-all-start.1 = ((f32[32,16,512]{2,1,0:T(8,128)}), f32[32,16,512]{2,1,0:T(8,128)S(1)}, u32[]{:S(2)}, u32[]{:S(2)}) async-start(f32[32,16,512]{2,1,0:T(8,128)} %broadcast_in_dim.17), calls=%async_computation.1 | async-start | bytes 2097152 | tf_op jit(solution)/shard_map/all_to_all | solution.py:31
  84.5 16.6 %all-to-all-done.1 = f32[32,16,512]{2,1,0:T(8,128)S(1)} async-done(((f32[32,16,512]{2,1,0:T(8,128)}), f32[32,16,512]{2,1,0:T(8,128)S(1)}, u32[]{:S(2)}, u32[]{:S(2)}) %all-to-all-start.1) | async-done | bytes 1048608 | tf_op jit(solution)/shard_map/all_to_all | solution.py:31
  101.9 17.9 %all_to_all.55 = f32[16,1,512]{2,1,0:T(1,128)S(1)} all-to-all(f32[16,1,512]{2,1,0:T(1,128)S(1)} %copy.16), channel_id=1, replica_groups=mesh['z'=16,'core'=2,'x'=4,'y'=4] {'z'}, dimensions={0} | all-to-all | bytes 65536 | tf_op jit(solution)/shard_map/all_to_all | solution.py:31
  119.9 14.0 %all_to_all.56 = f32[16,1,512]{2,1,0:T(1,128)S(1)} all-to-all(f32[16,1,512]{2,1,0:T(1,128)S(1)} %reshape.108), channel_id=1, replica_groups=mesh['z'=16,'core'=2,'x'=4,'y'=4] {'z'}, dimensions={0} | all-to-all | bytes 65536 | tf_op jit(solution)/shard_map/all_to_all | solution.py:31
  135.0 7.3 %all-to-all-start.4 = ((f32[32,16,512]{2,1,0:T(8,128)}), f32[32,16,512]{2,1,0:T(8,128)S(1)}, u32[]{:S(2)}, u32[]{:S(2)}) async-start(f32[32,16,512]{2,1,0:T(8,128)} %broadcast_in_dim.19), calls=%async_computation.4 | async-start | bytes 2097152 | tf_op jit(solution)/shard_map/all_to_all | solution.py:31
  147.4 11.6 %all-to-all-done.4 = f32[32,16,512]{2,1,0:T(8,128)S(1)} async-done(((f32[32,16,512]{2,1,0:T(8,128)}), f32[32,16,512]{2,1,0:T(8,128)S(1)}, u32[]{:S(2)}, u32[]{:S(2)}) %all-to-all-start.4) | async-done | bytes 1048608 | tf_op jit(solution)/shard_map/all_to_all | solution.py:31
  162.8 11.7 %cholesky.104 = f32[128,128]{1,0:T(8,128)S(1)} custom-call(f32[128,128]{1,0:T(8,128)S(1)} %cholesky.266), custom_call_target="Cholesky" | custom-call | tf_op jit(solution)/shard_map/jit(cholesky)/cholesky | solution.py:44
  174.7 9.8 %custom-call.30 = f32[1,128,128]{1,2,0:T(8,128)S(1)} custom-call(f32[1,128,128]{2,1,0:T(8,128)S(1)} %get-tuple-element.30), custom_call_target="InvertDiagBlocksLowerTriangular" | custom-call | tf_op jit(solution)/shard_map/jit(cholesky)/cholesky | solution.py:44
  187.6 12.7 %cholesky.217 = f32[128,128]{1,0:T(8,128)S(1)} custom-call(f32[128,128]{1,0:T(8,128)} %cholesky.270), custom_call_target="Cholesky" | custom-call | tf_op jit(solution)/shard_map/jit(cholesky)/cholesky | solution.py:44
  201.0 10.6 %custom-call.31 = f32[1,128,128]{1,2,0:T(8,128)S(1)} custom-call(f32[1,128,128]{2,1,0:T(8,128)} %get-tuple-element.27), custom_call_target="InvertDiagBlocksLowerTriangular" | custom-call | tf_op jit(solution)/shard_map/jit(cholesky)/cholesky | solution.py:44
  213.2 11.7 %cholesky.238 = f32[128,128]{1,0:T(8,128)S(1)} custom-call(f32[128,128]{1,0:T(8,128)S(1)} %cholesky.275), custom_call_target="Cholesky" | custom-call | tf_op jit(solution)/shard_map/jit(cholesky)/cholesky | solution.py:44
  225.6 9.8 %custom-call.32 = f32[1,128,128]{1,2,0:T(8,128)S(1)} custom-call(f32[1,128,128]{2,1,0:T(8,128)S(1)} %get-tuple-element.24), custom_call_target="InvertDiagBlocksLowerTriangular" | custom-call | tf_op jit(solution)/shard_map/jit(cholesky)/cholesky | solution.py:44
  236.9 11.9 %cholesky.255 = f32[128,128]{1,0:T(8,128)S(1)} custom-call(f32[128,128]{1,0:T(8,128)S(1)} %convolution_subtract_fusion.5), custom_call_target="Cholesky" | custom-call | tf_op jit(solution)/shard_map/jit(cholesky)/cholesky | solution.py:44
  253.7 13.8 %while.1 = (s32[]{:T(128)}, f32[512,512]{1,0:T(8,128)}, s32[4,2]{0,1:T(2,128)S(1)}, f32[4,128,128]{2,1,0:T(8,128)}, s32[]{:T(128)}) while((s32[]{:T(128)}, f32[512,512]{1,0:T(8,128)}, s32[4,2]{0,1:T(2,128)S(1)}, f32[4,128,128]{2,1,0:T(8,128)}, s32[]{:T(128)}) %tuple.32), condition=%wide.while_cond, body=%wide.while_body.sunk | while | flops 2 | bytes 132705 | solution.py:45
  267.5 40.7 %custom-call.33 = f32[4,128,128]{1,2,0:T(8,128)} custom-call(f32[4,128,128]{2,1,0:T(8,128)} %get-tuple-element.10), custom_call_target="InvertDiagBlocksLowerTriangular" | custom-call | tf_op jit(solution)/shard_map/triangular_solve | solution.py:45
  318.6 25.8 %all_gather.7 = f32[256,896]{1,0:T(8,128)S(1)} all-gather(f32[16,896]{1,0:T(8,128)} %reduce-scatter.2.cloned.1.call-done), channel_id=1, replica_groups=mesh['z'=16,'core'=2,'x'=4,'y'=4] {'z'}, dimensions={0}, use_global_device_ids=true | all-gather | bytes 974848 | tf_op jit(solution)/shard_map/all_gather | solution.py:84
  344.5 12.9 %all_to_all.57 = f32[2,256,896]{2,1,0:T(8,128)S(1)} all-to-all(f32[2,256,896]{2,1,0:T(8,128)S(1)} %broadcast_in_dim.20), channel_id=1, replica_groups=mesh['z'=16,'core'=2,'x'=4,'y'=4] {'core'}, dimensions={0} | all-to-all | bytes 3670016 | tf_op jit(solution)/shard_map/all_to_all | solution.py:31
  357.4 3.6 multiply_reduce_fusion
  361.7 3.7 all-to-all-start.6
  365.5 3.9 %fusion = f32[256,896]{1,0:T(8,128)} fusion(f32[256,896]{1,0:T(8,128)S(1)} %convert_add_fusion, f32[256,512]{1,0:T(8,128)} %fusion.10, f32[512,896]{1,0:T(8,128)S(1)} %get-tuple-element.34), kind=kOutput, calls=%fused_computation.4 | convolution fusion | flops 1409744896 | bytes 4194304 | tf_op jit(solution)/shard_map/dot_general | solution.py:21
  372.7 3.7 fusion.2
  (95 shorter events, 59.2 us)
Async XLA Ops:
  7.2 10.2 %copy-start.10 = (f32[16,896]{1,0:T(8,128)S(1)}, f32[16,896]{1,0:T(8,128)}, u32[]{:S(2)}) copy-start(f32[16,896]{1,0:T(8,128)} %param.7) | copy-start | bytes 172036
  8.6 38.9 %collective-permute-start = (f32[256,896]{1,0:T(8,128)S(1)}, f32[256,896]{1,0:T(8,128)S(1)}, u32[]{:S(2)}, u32[]{:S(2)}) collective-permute-start(f32[256,896]{1,0:T(8,128)S(1)} %convert_add_fusion), channel_id=1, source_target_pairs={{0,16},{16,0},{1,17},{17,1},{2,18},{18,2},{3,19},{19,3},{4,20},{20... | collective-permute-start | bytes 2752520 | tf_op jit(solution)/shard_map/ppermute | solution.py:61
  47.5 25.6 %copy-start = (f32[256,896]{1,0:T(8,128)}, f32[256,896]{1,0:T(8,128)S(1)}, u32[]{:S(2)}) copy-start(f32[256,896]{1,0:T(8,128)S(1)} %collective-permute-done) | copy-start | bytes 2752516
  79.8 21.3 %all-to-all-start.1 = ((f32[32,16,512]{2,1,0:T(8,128)}), f32[32,16,512]{2,1,0:T(8,128)S(1)}, u32[]{:S(2)}, u32[]{:S(2)}) async-start(f32[32,16,512]{2,1,0:T(8,128)} %broadcast_in_dim.17), calls=%async_computation.1 | async-start | bytes 2097152 | tf_op jit(solution)/shard_map/all_to_all | solution.py:31
  135.0 24.0 %all-to-all-start.4 = ((f32[32,16,512]{2,1,0:T(8,128)}), f32[32,16,512]{2,1,0:T(8,128)S(1)}, u32[]{:S(2)}, u32[]{:S(2)}) async-start(f32[32,16,512]{2,1,0:T(8,128)} %broadcast_in_dim.19), calls=%async_computation.4 | async-start | bytes 2097152 | tf_op jit(solution)/shard_map/all_to_all | solution.py:31
  142.4 176.2 %reduce-scatter.2.cloned.1.call-start = ((), (), s32[]{:S(2)}) async-start(), calls=%async_computation.8 | async-start | bytes 974848 | tf_op jit(solution)/shard_map/reduce_scatter | solution.py:83
  143.0 2.4 copy-start.1
  161.8 1.0 copy-start.3
  253.7 58.4 %copy-start.2 = (f32[512,512]{1,0:T(8,128)S(1)}, f32[512,512]{1,0:T(8,128)}, u32[]{:S(2)}) copy-start(f32[512,512]{1,0:T(8,128)} %fusion.16) | copy-start | bytes 3145732
  308.3 5.2 %copy-start.9 = (f32[4,128,128]{1,2,0:T(8,128)S(1)}, f32[4,128,128]{1,2,0:T(8,128)}, u32[]{:S(2)}) copy-start(f32[4,128,128]{1,2,0:T(8,128)} %custom-call.33) | copy-start | bytes 786436
  313.9 2.1 copy-start.4
  316.0 0.7 copy-start.7
  344.5 12.9 %copy-start.5 = (f32[128,512]{1,0:T(8,128)S(1)}, f32[128,512]{1,0:T(8,128)}, u32[]{:S(2)}) copy-start(f32[128,512]{1,0:T(8,128)} %copy-done.4) | copy-start | bytes 786436
  344.5 12.9 %copy-start.8 = (f32[128,512]{1,0:T(8,128)S(1)}, f32[128,512]{1,0:T(8,128)}, u32[]{:S(2)}) copy-start(f32[128,512]{1,0:T(8,128)} %copy-done.7) | copy-start | bytes 786436
  361.7 10.2 %all-to-all-start.6 = ((f32[16,4,128]{2,1,0:T(4,128)}), f32[16,4,128]{2,1,0:T(4,128)S(1)}, u32[]{:S(2)}, u32[]{:S(2)}) async-start(f32[16,4,128]{2,1,0:T(4,128)} %broadcast_in_dim.42), calls=%async_computation.7 | async-start | bytes 65536 | tf_op jit(solution)/shard_map/all_to_all | solution.py:31
  365.5 7.2 %copy-start.6 = (f32[256,512]{1,0:T(8,128)S(1)}, f32[256,512]{1,0:T(8,128)}, u32[]{:S(2)}) copy-start(f32[256,512]{1,0:T(8,128)} %fusion.10) | copy-start | bytes 1572868
Sparse Core Ops, SparseCore 0:
  147.6 51.3 reduce-scatter.1

commit v2 on v1

--- a/solution.py
+++ b/solution.py
@@ -3,6 +3,8 @@
 import jax
 import jax.numpy as jnp
 from jax import lax
+from jax.experimental import pallas as pl
+from jax.experimental.pallas import tpu as pltpu
 from jax.sharding import Mesh, PartitionSpec as P
 
 D = 8192
@@ -40,11 +42,100 @@
     )
 
 
+SUB = 8
+TILE = 128
+
+
+def factor_step(work, wide, at):
+    lane = lax.broadcasted_iota(jnp.int32,(SUB,TILE),1)
+    sub = lax.broadcasted_iota(jnp.int32,(SUB,TILE),0)
+    own = (lane>=at)&(lane<at+SUB)
+    block = work[at:at+SUB,:]
+    for j in range(SUB):
+        wide[j] = jnp.broadcast_to(block[:,at+j:at+j+1],(SUB,TILE))
+    work[at:at+SUB,:] = jnp.where(own, jnp.where(lane-at==sub,1.0,0.0), block)
+    spread = lambda ref_row: jnp.broadcast_to(ref_row,(SUB,TILE))
+    gram = [[spread(wide[j,i:i+1,:]) for j in range(i+1)] for i in range(SUB)]
+    low = [[None]*SUB for _ in range(SUB)]
+    inv = [None]*SUB
+    rows = [None]*SUB
+    for j in range(SUB):
+        inv[j] = lax.rsqrt(gram[j][j])
+        for i in range(j+1,SUB):
+            low[i][j] = gram[i][j]*inv[j]
+        for i in range(j+1,SUB):
+            for m in range(j+1,i+1):
+                gram[i][m] = gram[i][m]-low[i][j]*low[m][j]
+        row = spread(work[at+j:at+j+1,:])
+        for m in range(j):
+            row = row - low[j][m]*rows[m]
+        rows[j] = row*inv[j]
+    out = rows[SUB-1]
+    for i in range(SUB-1):
+        out = jnp.where(sub==i, rows[i], out)
+    work[at:at+SUB,:] = out
+    nxt = at+SUB
+    if nxt < TILE:
+        block = work[nxt:nxt+SUB,:]
+        left=[]
+        total = jnp.where(own,0.0,block)
+        for j in range(SUB):
+            col = jnp.broadcast_to(block[:,at+j:at+j+1],(SUB,TILE))
+            for m in range(j):
+                col = col - left[m]*low[j][m]
+            left.append(col*inv[j])
+            total = total - left[j]*rows[j]
+        work[nxt:nxt+SUB,:] = total
+    far = nxt+SUB
+    if far < TILE:
+        prod = dot(out,out,0,0)
+        rest = work[far:,:]
+        lanes = lax.broadcasted_iota(jnp.int32,rest.shape,1)
+        work[far:,:] = jnp.where((lanes>=at)&(lanes<at+SUB),0.0,rest) - prod[far:,:]
+
+
+def inverse_factor_kernel(gram_ref, out_ref, work, wide):
+    n = gram_ref.shape[0]; tiles = n//TILE
+    out_ref[...] = gram_ref[...]
+    def panel(p, carry):
+        at = pl.multiple_of(p*TILE,TILE)
+        work[...] = out_ref[pl.ds(at,TILE),pl.ds(at,TILE)]
+        for k in range(TILE//SUB):
+            factor_step(work, wide.at[k%2], k*SUB)
+        r = lax.broadcasted_iota(jnp.int32,(TILE,TILE),0); c = lax.broadcasted_iota(jnp.int32,(TILE,TILE),1)
+        inverse = jnp.where(r>=c, work[...], 0.0)
+        out_ref[pl.ds(at,TILE),pl.ds(at,TILE)] = jnp.where(r==c,1.0,0.0)
+        new = dot(inverse, out_ref[pl.ds(at,TILE),:],1,0)
+        out_ref[pl.ds(at,TILE),:] = new
+        for q in range(1,tiles):
+            @pl.when(q>p)
+            def _():
+                out_ref[q*TILE:(q+1)*TILE,pl.ds(at,TILE)] = jnp.zeros((TILE,TILE),jnp.float32)
+                out_ref[q*TILE:(q+1)*TILE,:] = out_ref[q*TILE:(q+1)*TILE,:] - dot(
+                    new[:,q*TILE:(q+1)*TILE],new,0,0
+                )
+        return carry
+    lax.fori_loop(0,tiles,panel,0)
+    for q in range(tiles-1):
+        out_ref[q*TILE:(q+1)*TILE,(q+1)*TILE:] = jnp.zeros((TILE,n-(q+1)*TILE),jnp.float32)
+
+
 def inverse_factor(gram):
-    factor = jnp.linalg.cholesky(gram)
-    return lax.linalg.triangular_solve(
-        factor, jnp.eye(gram.shape[0], dtype=jnp.float32), left_side=True, lower=True
-    )
+    size = gram.shape[0]
+    return pl.pallas_call(
+        inverse_factor_kernel,
+        out_shape=jax.ShapeDtypeStruct((size, size), jnp.float32),
+        in_specs=[pl.BlockSpec(memory_space=pltpu.VMEM)],
+        out_specs=pl.BlockSpec(memory_space=pltpu.VMEM),
+        scratch_shapes=[
+            pltpu.VMEM((TILE, TILE), jnp.float32),
+            pltpu.VMEM((2, SUB, SUB, TILE), jnp.float32),
+        ],
+        cost_estimate=pl.CostEstimate(
+            flops=200_000_000, bytes_accessed=4 * size * size * 2, transcendentals=size
+        ),
+        name="inverse_factor",
+    )(gram)
 
 
 def on_device(weights, momentum, gradient, warm_basis):
@@ -65,22 +156,29 @@
     partial = jnp.where(
         core == 0, jnp.stack([mine, theirs]), jnp.stack([theirs, mine])
     ).reshape(2 * rows, rank // 2)
-    pieces = exchange(partial, PLANE).reshape(2, blocks, 2 * rows // plane, depth, owned)
-    part = jnp.sum(pieces, axis=1).transpose(1, 2, 0, 3).reshape(2 * rows // plane, rank)
+    pieces = exchange(partial, PLANE).reshape(2, blocks, 2 * rows // plane, rank // 2)
+    pieces = jnp.sum(pieces, axis=1)
+    gathered = lax.broadcasted_iota(jnp.int32, (rank // 2, rank), 0)
+    ranks = lax.broadcasted_iota(jnp.int32, (rank // 2, rank), 1)
+    even = gathered // owned * (2 * owned) + gathered % owned
+    part = dot(pieces[0], (ranks == even).astype(jnp.float32), 1, 0) + dot(
+        pieces[1], (ranks == even + owned).astype(jnp.float32), 1, 0
+    )
     projected = spread(part, PLANE, plane)
-
-    share = rank // plane
-    mine_at = lax.axis_index(PLANE) * share
-    gram_part = dot(lax.dynamic_slice_in_dim(projected, mine_at, share, 1), projected, 0, 0)
-    gram_row = jnp.sum(exchange(gram_part, "z").reshape(depth, share // depth, rank), axis=0)
-    gram_share = spread(gram_row, "z", depth)
-    gram = spread(gram_share, PLANE, plane)
 
     half = lax.dynamic_slice_in_dim(projected, core * (rank // 2), rank // 2, 1)
     own_rows = lax.dynamic_slice_in_dim(half, core * rows, rows, 0)
     partner_rows = lax.dynamic_slice_in_dim(half, (1 - core) * rows, rows, 0)
     moved = dot(own_rows, blended, 0, 0) + dot(partner_rows, partner, 0, 0)
+    tie = moved[0, 0] * 0.0
     moved = lax.psum_scatter(moved, "z", scatter_dimension=0, tiled=True)
+    share = rank // plane
+    mine_at = lax.axis_index(PLANE) * share
+    gram_part = dot(lax.dynamic_slice_in_dim(projected, mine_at, share, 1), projected, 0, 0) + tie
+    gram_row = jnp.sum(exchange(gram_part, "z").reshape(depth, share // depth, rank), axis=0)
+    gram_share = spread(gram_row, "z", depth)
+    gram = spread(gram_share, PLANE, plane)
+
     moved = lax.all_gather(moved, "z", axis=0, tiled=True)
     moved = spread(moved, "core", 2)
 

time: 390 us -> 253 us (0.65); the launches traced: 383 us -> 252 us
  other arithmetic: 130 us -> 3.04 us
  Pallas kernels: 0 us -> 24.1 us
  blocking collectives: 124 us -> 100 us
  local copies, waits for them, and re-layouts: 24 us -> 5.29 us
  waiting for transfers between devices: 30.7 us -> 48 us
  matrix products: 32.2 us -> 19.3 us
  starting transfers between devices: 25.1 us -> 37.9 us
    another operation x17 -> x0, other arithmetic: 123 us -> none  [the longest x14 81 us: inverse_factor(): factor = jnp.linalg.cholesky(gram)]
    pallas_call x0 -> x1, Pallas kernels: none -> 24.1 us  [inverse_factor(): pl.pallas_call(inverse_factor_kernel, out_shape=jax.ShapeDtypeStruct((siz...]
    all_to_all x4 -> x3, blocking collectives: 69.3 us -> 45.2 us  [exchange(): return lax.all_to_all(array, axes, 0, 0, tiled=True)]
    all_to_all x3 -> x4, waiting for transfers between devices: 30.7 us -> 47.9 us  [exchange(): return lax.all_to_all(array, axes, 0, 0, tiled=True)]
    another operation x17 -> x0, local copies, waits for them, and re-layouts: 14.6 us -> none
    all_to_all x3 -> x4, starting transfers between devices: 15.8 us -> 29.1 us  [exchange(): return lax.all_to_all(array, axes, 0, 0, tiled=True)]
    another operation x13 -> x0, matrix products: 13.1 us -> none  [the longest x7 7.66 us: inverse_factor(): lax.linalg.triangular_solve(factor, jnp.eye(gram.shape[0], dtype=jnp.floa...]
    dot_general x9 -> x11, matrix products: 19 us -> 19.3 us  [dot(): lax.dot_general(left_side, right_side, (((contract_left,), (contract_righ...]
  transfers between devices with their start and end apart: 5 -> 6, of which waited for: 3 -> 4; matrix products, arithmetic and copies ran while one was open for 43% -> 4% of each run, Pallas kernels for 0% -> 10%
where the time goes in v2:
time: 253 us; the launch traced here: 252 us
  blocking collectives  100 us (40%)
  waiting for transfers between devices  48 us (19%)
  starting transfers between devices  37.9 us (15%)
  Pallas kernels  24.1 us (10%)
  matrix products  19.3 us (8%)
  between operations  14.9 us (6%)
  local copies, waits for them, and re-layouts  5.29 us (2%)
  other arithmetic  3.04 us (1%)
    all_to_all x4, waiting for transfers between devices, exchange(): return lax.all_to_all(array, axes, 0, 0, tiled=True)  47.9 us
    all_to_all x3, blocking collectives, exchange(): return lax.all_to_all(array, axes, 0, 0, tiled=True)  45.2 us
    all_to_all x4, starting transfers between devices, exchange(): return lax.all_to_all(array, axes, 0, 0, tiled=True)  29.1 us
    all_gather x1, blocking collectives, on_device(): basis = lax.all_gather(warm_basis, 'z', axis=0, tiled=True)  29 us
    all_gather x1, blocking collectives, on_device(): moved = lax.all_gather(moved, 'z', axis=0, tiled=True)  25.8 us
    pallas_call x1, Pallas kernels, inverse_factor(): pl.pallas_call(inverse_factor_kernel, out_shape=jax.ShapeDtypeStruct((siz...  24.1 us
    dot_general x11, matrix products, dot(): lax.dot_general(left_side, right_side, (((contract_left,), (contract_righ...  19.3 us
    ppermute x1, starting transfers between devices, on_device(): partner = lax.ppermute(blended, 'core', SWAP)  8.79 us
  transfers between devices with their start and end apart: 6, of which 4 were waited for; matrix products, arithmetic and copies ran while one was open for 4% of the time, Pallas kernels for 10%

profile of v2, /device:TPU:1, one launch (start us, length us, event | category | flops | bytes accessed | tf_op | source)
XLA Modules:
  0.0 252.5 jit_solution(8230875891191978893)
XLA Ops:
  7.2 1.4 convert_add_fusion
  8.6 8.8 %collective-permute-start = (f32[256,896]{1,0:T(8,128)S(1)}, f32[256,896]{1,0:T(8,128)S(1)}, u32[]{:S(2)}, u32[]{:S(2)}) collective-permute-start(f32[256,896]{1,0:T(8,128)S(1)} %convert_add_fusion), channel_id=1, source_target_pairs={{0,16},{16,0},{1,17},{17,1},{2,18},{18,2},{3,19},{19,3},{4,20},{20... | collective-permute-start | bytes 2752520 | tf_op jit(solution)/shard_map/ppermute | solution.py:152
  17.4 29.0 %all_gather.6 = f32[256,896]{1,0:T(8,128)S(1)} all-gather(f32[16,896]{1,0:T(8,128)S(1)} %copy-done.2), channel_id=1, replica_groups=mesh['z'=16,'core'=2,'x'=4,'y'=4] {'z'}, dimensions={0}, use_global_device_ids=true | all-gather | bytes 974848 | tf_op jit(solution)/shard_map/all_gather | solution.py:153
  49.3 13.5 %all-to-all-start = ((f32[32,16,256]{2,1,0:T(8,128)}), f32[32,16,256]{2,1,0:T(8,128)S(1)}, u32[]{:S(2)}, u32[]{:S(2)}) async-start(f32[32,16,256]{2,1,0:T(8,128)} %bitcast.2), calls=%async_computation | async-start | bytes 1048576 | tf_op jit(solution)/shard_map/all_to_all | solution.py:33
  62.9 11.1 %all-to-all-done = f32[32,16,256]{2,1,0:T(8,128)S(1)} async-done(((f32[32,16,256]{2,1,0:T(8,128)}), f32[32,16,256]{2,1,0:T(8,128)S(1)}, u32[]{:S(2)}, u32[]{:S(2)}) %all-to-all-start) | async-done | bytes 524320 | tf_op jit(solution)/shard_map/all_to_all | solution.py:33
  75.0 1.1 broadcast_in_dim.12
  76.1 4.7 %all-to-all-start.1 = ((f32[32,16,512]{2,1,0:T(8,128)}), f32[32,16,512]{2,1,0:T(8,128)S(1)}, u32[]{:S(2)}, u32[]{:S(2)}) async-start(f32[32,16,512]{2,1,0:T(8,128)} %broadcast_in_dim.12), calls=%async_computation.1 | async-start | bytes 2097152 | tf_op jit(solution)/shard_map/all_to_all | solution.py:33
  80.8 16.6 %all-to-all-done.1 = f32[32,16,512]{2,1,0:T(8,128)S(1)} async-done(((f32[32,16,512]{2,1,0:T(8,128)}), f32[32,16,512]{2,1,0:T(8,128)S(1)}, u32[]{:S(2)}, u32[]{:S(2)}) %all-to-all-start.1) | async-done | bytes 1048608 | tf_op jit(solution)/shard_map/all_to_all | solution.py:33
  97.4 1.1 fusion.11
  98.6 2.1 convolution_add_fusion
  100.6 1.2 slice.14
  103.2 18.0 %all_to_all.53 = f32[16,1,512]{2,1,0:T(1,128)S(1)} all-to-all(f32[16,1,512]{2,1,0:T(1,128)S(1)} %copy.9), channel_id=1, replica_groups=mesh['z'=16,'core'=2,'x'=4,'y'=4] {'z'}, dimensions={0} | all-to-all | bytes 65536 | tf_op jit(solution)/shard_map/all_to_all | solution.py:33
  121.3 14.3 %all_to_all.54 = f32[16,1,512]{2,1,0:T(1,128)S(1)} all-to-all(f32[16,1,512]{2,1,0:T(1,128)S(1)} %reshape.75), channel_id=1, replica_groups=mesh['z'=16,'core'=2,'x'=4,'y'=4] {'z'}, dimensions={0} | all-to-all | bytes 65536 | tf_op jit(solution)/shard_map/all_to_all | solution.py:33
  136.7 7.4 %all-to-all-start.4 = ((f32[32,16,512]{2,1,0:T(8,128)}), f32[32,16,512]{2,1,0:T(8,128)S(1)}, u32[]{:S(2)}, u32[]{:S(2)}) async-start(f32[32,16,512]{2,1,0:T(8,128)} %broadcast_in_dim.14), calls=%async_computation.4 | async-start | bytes 2097152 | tf_op jit(solution)/shard_map/all_to_all | solution.py:33
  144.1 16.6 %all-to-all-done.4 = f32[32,16,512]{2,1,0:T(8,128)S(1)} async-done(((f32[32,16,512]{2,1,0:T(8,128)}), f32[32,16,512]{2,1,0:T(8,128)S(1)}, u32[]{:S(2)}, u32[]{:S(2)}) %all-to-all-start.4) | async-done | bytes 1048608 | tf_op jit(solution)/shard_map/all_to_all | solution.py:33
  161.7 24.1 %inverse_factor.1 = f32[512,512]{1,0:T(8,128)} custom-call(f32[512,512]{1,0:T(8,128)} %bitcast.43), custom_call_target="tpu_custom_call" | custom-call | flops 200000000 | bytes 2097152 | tf_op jit(solution)/shard_map/inverse_factor/pallas_call | solution.py:125
  185.8 2.3 fusion.4
  188.1 25.8 %all_gather.7 = f32[256,896]{1,0:T(8,128)S(1)} all-gather(f32[16,896]{1,0:T(8,128)} %reduce-scatter.2.cloned.1.call-done), channel_id=1, replica_groups=mesh['z'=16,'core'=2,'x'=4,'y'=4] {'z'}, dimensions={0}, use_global_device_ids=true | all-gather | bytes 974848 | tf_op jit(solution)/shard_map/all_gather | solution.py:182
  214.1 12.9 %all_to_all.55 = f32[2,256,896]{2,1,0:T(8,128)S(1)} all-to-all(f32[2,256,896]{2,1,0:T(8,128)S(1)} %broadcast_in_dim.15), channel_id=1, replica_groups=mesh['z'=16,'core'=2,'x'=4,'y'=4] {'core'}, dimensions={0} | all-to-all | bytes 3670016 | tf_op jit(solution)/shard_map/all_to_all | solution.py:33
  227.0 3.6 %multiply_reduce_fusion = (f32[512]{0:T(512)S(1)}, f32[512,896]{1,0:T(8,128)S(1)}) fusion(f32[512,512]{1,0:T(8,128)S(1)} %copy-done, f32[512,896]{1,0:T(8,128)S(1)} %bitcast.42), kind=kOutput, calls=%fused_computation | convolution fusion | flops 2819489280 | bytes 4720640 | tf_op jit(solution)/shard_map/dot_general | solution.py:23
  231.2 3.5 %all-to-all-start.6 = ((f32[16,4,128]{2,1,0:T(4,128)}), f32[16,4,128]{2,1,0:T(4,128)S(1)}, u32[]{:S(2)}, u32[]{:S(2)}) async-start(f32[16,4,128]{2,1,0:T(4,128)} %broadcast_in_dim.17), calls=%async_computation.7 | async-start | bytes 65536 | tf_op jit(solution)/shard_map/all_to_all | solution.py:33
  234.7 2.8 %fusion = f32[256,896]{1,0:T(8,128)} fusion(f32[256,896]{1,0:T(8,128)S(1)} %convert_add_fusion, f32[256,512]{1,0:T(8,128)S(1)} %fusion.4, f32[512,896]{1,0:T(8,128)S(1)} %get-tuple-element.4), kind=kOutput, calls=%fused_computation.2 | convolution fusion | flops 1409744896 | bytes 4194304 | tf_op jit(solution)/shard_map/dot_general | solution.py:23
  237.5 3.6 %all-to-all-done.6 = f32[16,4,128]{2,1,0:T(4,128)S(1)} async-done(((f32[16,4,128]{2,1,0:T(4,128)}), f32[16,4,128]{2,1,0:T(4,128)S(1)}, u32[]{:S(2)}, u32[]{:S(2)}) %all-to-all-start.6) | async-done | bytes 32800 | tf_op jit(solution)/shard_map/all_to_all | solution.py:33
  241.2 3.7 %fusion.2 = bf16[256,896]{1,0:T(8,128)(2,1)} fusion(f32[512,896]{1,0:T(8,128)S(1)} %get-tuple-element.4, bf16[256,896]{1,0:T(8,128)(2,1)} %param.4, f32[256,512]{1,0:T(8,128)S(1)} %fusion.4, f32[512]{0:T(512)S(1)} %rsqrt_bitcast_fusion), kind=kOutput, calls=%fused_computation.6 | convolution fusion | flops 1410334720 | bytes 3278848 | tf_op jit(solution)/shard_map/dot_general | solution.py:23
  (31 shorter events, 8.4 us)
Async XLA Ops:
  7.2 10.2 %copy-start.2 = (f32[16,896]{1,0:T(8,128)S(1)}, f32[16,896]{1,0:T(8,128)}, u32[]{:S(2)}) copy-start(f32[16,896]{1,0:T(8,128)} %param.7) | copy-start | bytes 172036
  8.6 38.9 %collective-permute-start = (f32[256,896]{1,0:T(8,128)S(1)}, f32[256,896]{1,0:T(8,128)S(1)}, u32[]{:S(2)}, u32[]{:S(2)}) collective-permute-start(f32[256,896]{1,0:T(8,128)S(1)} %convert_add_fusion), channel_id=1, source_target_pairs={{0,16},{16,0},{1,17},{17,1},{2,18},{18,2},{3,19},{19,3},{4,20},{20... | collective-permute-start | bytes 2752520 | tf_op jit(solution)/shard_map/ppermute | solution.py:152
  49.3 24.7 %all-to-all-start = ((f32[32,16,256]{2,1,0:T(8,128)}), f32[32,16,256]{2,1,0:T(8,128)S(1)}, u32[]{:S(2)}, u32[]{:S(2)}) async-start(f32[32,16,256]{2,1,0:T(8,128)} %bitcast.2), calls=%async_computation | async-start | bytes 1048576 | tf_op jit(solution)/shard_map/all_to_all | solution.py:33
  76.1 21.3 %all-to-all-start.1 = ((f32[32,16,512]{2,1,0:T(8,128)}), f32[32,16,512]{2,1,0:T(8,128)S(1)}, u32[]{:S(2)}, u32[]{:S(2)}) async-start(f32[32,16,512]{2,1,0:T(8,128)} %broadcast_in_dim.12), calls=%async_computation.1 | async-start | bytes 2097152 | tf_op jit(solution)/shard_map/all_to_all | solution.py:33
  80.8 107.4 %reduce-scatter.2.cloned.1.call-start = ((), (), s32[]{:S(2)}) async-start(), calls=%async_computation.8 | async-start | bytes 974848 | tf_op jit(solution)/shard_map/reduce_scatter | solution.py:174
  136.7 24.0 %all-to-all-start.4 = ((f32[32,16,512]{2,1,0:T(8,128)}), f32[32,16,512]{2,1,0:T(8,128)S(1)}, u32[]{:S(2)}, u32[]{:S(2)}) async-start(f32[32,16,512]{2,1,0:T(8,128)} %broadcast_in_dim.14), calls=%async_computation.4 | async-start | bytes 2097152 | tf_op jit(solution)/shard_map/all_to_all | solution.py:33
  160.7 1.0 copy-start.1
  214.0 12.9 %copy-start = (f32[512,512]{1,0:T(8,128)S(1)}, f32[512,512]{1,0:T(8,128)}, u32[]{:S(2)}) copy-start(f32[512,512]{1,0:T(8,128)} %inverse_factor.1) | copy-start | bytes 3145732
  231.2 9.9 %all-to-all-start.6 = ((f32[16,4,128]{2,1,0:T(4,128)}), f32[16,4,128]{2,1,0:T(4,128)S(1)}, u32[]{:S(2)}, u32[]{:S(2)}) async-start(f32[16,4,128]{2,1,0:T(4,128)} %broadcast_in_dim.17), calls=%async_computation.7 | async-start | bytes 65536 | tf_op jit(solution)/shard_map/all_to_all | solution.py:33
Sparse Core Ops, SparseCore 0:
  100.8 53.3 reduce-scatter.1

commit v3 on v2

--- a/solution.py
+++ b/solution.py
@@ -14,8 +14,10 @@
 step_size = 2.0
 epsilon = 1e-06
 
-PLANE = ("core", "x", "y")
+DEPTH = ("far", "near")
+PLANE = ("x", "y", "core")
 COLUMN_BLOCKS = ("x", "y")
+HIGH = lax.Precision.HIGH
 SWAP = [(0, 1), (1, 0)]
 
 
@@ -134,66 +136,77 @@
         cost_estimate=pl.CostEstimate(
             flops=200_000_000, bytes_accessed=4 * size * size * 2, transcendentals=size
         ),
+        compiler_params=pltpu.CompilerParams(vmem_limit_bytes=8 * 2**20),
         name="inverse_factor",
     )(gram)
+
+
+def total(array, count):
+    return jnp.sum(array.reshape((count, array.shape[0] // count) + array.shape[1:]), axis=0)
+
+
+def by_core(core, own, other, axis):
+    return jnp.where(
+        core == 0, jnp.concatenate([own, other], axis), jnp.concatenate([other, own], axis)
+    )
 
 
 def on_device(weights, momentum, gradient, warm_basis):
     rows, columns = momentum.shape
     owned = warm_basis.shape[0]
-    depth = lax.axis_size("z")
+    depth = lax.axis_size(DEPTH)
     plane = lax.axis_size(PLANE)
     blocks = lax.axis_size(COLUMN_BLOCKS)
+    far, near = lax.axis_size("far"), lax.axis_size("near")
     rank = owned * depth * 2
+    half = rank // 2
     core = lax.axis_index("core")
-    place = lax.axis_index("z")
+    place = lax.axis_index(DEPTH)
 
     blended = momentum + gradient.astype(jnp.float32)
     partner = lax.ppermute(blended, "core", SWAP)
-    basis = lax.all_gather(warm_basis, "z", axis=0, tiled=True)
-    mine = dot(blended, basis, 1, 1)
-    theirs = dot(partner, basis, 1, 1)
-    partial = jnp.where(
-        core == 0, jnp.stack([mine, theirs]), jnp.stack([theirs, mine])
-    ).reshape(2 * rows, rank // 2)
-    pieces = exchange(partial, PLANE).reshape(2, blocks, 2 * rows // plane, rank // 2)
-    pieces = jnp.sum(pieces, axis=1)
-    gathered = lax.broadcasted_iota(jnp.int32, (rank // 2, rank), 0)
-    ranks = lax.broadcasted_iota(jnp.int32, (rank // 2, rank), 1)
-    even = gathered // owned * (2 * owned) + gathered % owned
-    part = dot(pieces[0], (ranks == even).astype(jnp.float32), 1, 0) + dot(
-        pieces[1], (ranks == even + owned).astype(jnp.float32), 1, 0
-    )
-    projected = spread(part, PLANE, plane)
-
-    half = lax.dynamic_slice_in_dim(projected, core * (rank // 2), rank // 2, 1)
-    own_rows = lax.dynamic_slice_in_dim(half, core * rows, rows, 0)
-    partner_rows = lax.dynamic_slice_in_dim(half, (1 - core) * rows, rows, 0)
-    moved = dot(own_rows, blended, 0, 0) + dot(partner_rows, partner, 0, 0)
-    tie = moved[0, 0] * 0.0
-    moved = lax.psum_scatter(moved, "z", scatter_dimension=0, tiled=True)
-    share = rank // plane
-    mine_at = lax.axis_index(PLANE) * share
-    gram_part = dot(lax.dynamic_slice_in_dim(projected, mine_at, share, 1), projected, 0, 0) + tie
-    gram_row = jnp.sum(exchange(gram_part, "z").reshape(depth, share // depth, rank), axis=0)
-    gram_share = spread(gram_row, "z", depth)
-    gram = spread(gram_share, PLANE, plane)
-
-    moved = lax.all_gather(moved, "z", axis=0, tiled=True)
+    basis = lax.all_gather(warm_basis, DEPTH, axis=0, tiled=True)
+    partial = jnp.concatenate([dot(blended, basis, 1, 1), dot(partner, basis, 1, 1)])
+    part = total(exchange(partial, COLUMN_BLOCKS), blocks)
+    projected = spread(part, COLUMN_BLOCKS, blocks)
+    others = lax.ppermute(projected, "core", SWAP)
+    others = jnp.concatenate([others[rows:], others[:rows]])
+
+    def natural(first, count):
+        kept = lax.broadcasted_iota(jnp.int32, (rank, count), 0)
+        ranks = lax.broadcasted_iota(jnp.int32, (rank, count), 1) + first
+        source = ranks // owned % 2 * half + ranks // (2 * owned) * owned + ranks % owned
+        return (kept == source).astype(jnp.float32)
+
+    order = natural(0, rank)
+    joined = by_core(core, projected, others, 1)
+    mine = dot(joined, natural(core * half, half), 1, 0)
+    moved = dot(mine[:rows], blended, 0, 0, HIGH) + dot(mine[rows:], partner, 0, 0, HIGH)
+    moved = lax.psum_scatter(moved, DEPTH, scatter_dimension=0, tiled=True)
+
+    share = half // blocks
+    picked = lax.dynamic_slice_in_dim(
+        projected, lax.axis_index(COLUMN_BLOCKS) * share, share, 1
+    )
+    same = dot(picked, projected, 0, 0)
+    cross = dot(picked, others, 0, 0)
+    gram = dot(by_core(core, same, cross, 1), order, 1, 0)
+    gram = total(spread(gram, "far", far), far)
+    gram = total(spread(gram, "near", near), near)
+    gram = spread(gram, PLANE, plane)
+    inverse = inverse_factor(gram)
+
+    moved = lax.all_gather(moved, DEPTH, axis=0, tiled=True)
     moved = spread(moved, "core", 2)
-
-    inverse = inverse_factor(gram)
-    own_projected = lax.dynamic_slice_in_dim(projected, core * rows, rows, 0)
-    orthonormal = dot(own_projected, inverse, 1, 1)
-    coefficients = dot(inverse, moved, 1, 0)
+    own_projected = dot(joined[:rows], order, 1, 0)
+    orthonormal = dot(own_projected, inverse, 1, 1, HIGH)
+    coefficients = dot(inverse, moved, 1, 0, HIGH)
     energy = jnp.sum(coefficients * coefficients, axis=1).reshape(rank // 128, 128)
-    energy = jnp.sum(
-        spread(energy, COLUMN_BLOCKS, blocks).reshape(blocks, rank // 128, 128), axis=0
-    ).reshape(rank)
+    energy = total(spread(energy, COLUMN_BLOCKS, blocks), blocks).reshape(rank)
     scale = lax.rsqrt(energy / FF + epsilon)
-    feedback = dot(orthonormal, coefficients, 1, 0)
+    feedback = dot(orthonormal, coefficients, 1, 0, HIGH)
     new_momentum = blended - (1.0 - momentum_decay) * feedback
-    update = dot(orthonormal * scale[None, :], coefficients, 1, 0)
+    update = dot(orthonormal * scale[None, :], coefficients, 1, 0, HIGH)
     first = (place * 2 + core) * owned
     new_basis = (
         lax.dynamic_slice_in_dim(coefficients, first, owned, 0)
@@ -208,10 +221,10 @@
 def solution(mesh):
     devices = mesh.devices
     split = Mesh(
-        devices.reshape(devices.shape[0] // 2, 2, 4, devices.shape[1] // 4),
-        ("z", "core", "x", "y"),
-    )
-    spec = P(("z", "core"), ("x", "y"))
+        devices.reshape(4, devices.shape[0] // 8, 2, 4, devices.shape[1] // 4),
+        ("far", "near", "core", "x", "y"),
+    )
+    spec = P(("far", "near", "core"), ("x", "y"))
     return jax.shard_map(
         on_device, mesh=split, in_specs=(spec,) * 4, out_specs=(spec,) * 3, check_vma=False
     )

time: 253 us -> 236 us (0.933)
  blocking collectives: 100 us -> 80 us
  starting transfers between devices: 37.9 us -> 50.1 us
  matrix products: 19.3 us -> 15 us
    all_to_all x3 -> x2, blocking collectives: 45.2 us -> 24.4 us  [exchange(): return lax.all_to_all(array, axes, 0, 0, tiled=True)]
    ppermute x0 -> x1, starting transfers between devices: none -> 10.9 us  [on_device(): others = lax.ppermute(projected, 'core', SWAP)]
    dot_general x11 -> x13, matrix products: 19.3 us -> 15 us  [dot(): lax.dot_general(left_side, right_side, (((contract_left,), (contract_righ...]
    all_to_all x4 -> x5, starting transfers between devices: 29.1 us -> 30.5 us  [exchange(): return lax.all_to_all(array, axes, 0, 0, tiled=True)]
    all_to_all x4 -> x5, waiting for transfers between devices: 47.9 us -> 46.5 us  [exchange(): return lax.all_to_all(array, axes, 0, 0, tiled=True)]
  transfers between devices with their start and end apart: 6 -> 8, of which waited for: 4 -> 6; matrix products, arithmetic and copies ran while one was open for 4% -> 4% of each run, Pallas kernels for 10% -> 9%
where the time goes in v3:
time: 236 us
  blocking collectives  80 us (34%)
  starting transfers between devices  50.1 us (21%)
  waiting for transfers between devices  47.4 us (20%)
  Pallas kernels  21.9 us (9%)
  matrix products  15 us (6%)
  between operations  14.3 us (6%)
  local copies, waits for them, and re-layouts  3.51 us (1%)
  other arithmetic  3.28 us (1%)
    all_to_all x5, waiting for transfers between devices, exchange(): return lax.all_to_all(array, axes, 0, 0, tiled=True)  46.5 us
    all_to_all x5, starting transfers between devices, exchange(): return lax.all_to_all(array, axes, 0, 0, tiled=True)  30.5 us
    all_gather x1, blocking collectives, on_device(): basis = lax.all_gather(warm_basis, DEPTH, axis=0, tiled=True)  29 us
    all_gather x1, blocking collectives, on_device(): moved = lax.all_gather(moved, DEPTH, axis=0, tiled=True)  26.5 us
    all_to_all x2, blocking collectives, exchange(): return lax.all_to_all(array, axes, 0, 0, tiled=True)  24.4 us
    pallas_call x1, Pallas kernels, inverse_factor(): pl.pallas_call(inverse_factor_kernel, out_shape=jax.ShapeDtypeStruct((siz...  21.9 us
    dot_general x13, matrix products, dot(): lax.dot_general(left_side, right_side, (((contract_left,), (contract_righ...  15 us
    ppermute x1, starting transfers between devices, on_device(): others = lax.ppermute(projected, 'core', SWAP)  10.9 us
  transfers between devices with their start and end apart: 8, of which 6 were waited for; matrix products, arithmetic and copies ran while one was open for 4% of the time, Pallas kernels for 9%

profile of v3, /device:TPU:1, one launch (start us, length us, event | category | flops | bytes accessed | tf_op | source)
XLA Modules:
  0.0 235.5 jit_solution(12595791884810272359)
XLA Ops:
  7.2 1.4 convert_add_fusion
  8.6 8.8 %collective-permute-start = (f32[256,896]{1,0:T(8,128)S(1)}, f32[256,896]{1,0:T(8,128)S(1)}, u32[]{:S(2)}, u32[]{:S(2)}) collective-permute-start(f32[256,896]{1,0:T(8,128)S(1)} %convert_add_fusion), channel_id=1, source_target_pairs={{0,16},{16,0},{1,17},{17,1},{2,18},{18,2},{3,19},{19,3},{4,20},{20... | collective-permute-start | bytes 2752520 | tf_op jit(solution)/shard_map/ppermute | solution.py:167
  17.4 29.0 %all_gather.6 = f32[256,896]{1,0:T(8,128)S(1)} all-gather(f32[16,896]{1,0:T(8,128)S(1)} %copy-done.2), channel_id=1, replica_groups=mesh['far'=4,'near'=4,'core'=2,'x'=4,'y'=4] {'far','near'}, dimensions={0}, use_global_device_ids=true | all-gather | bytes 974848 | tf_op jit(solution)/shard_map/all_gather | solution.py:168
  47.5 1.0 fusion.76
  49.3 6.8 %all-to-all-start = ((f32[16,32,256]{2,1,0:T(8,128)}), f32[16,32,256]{2,1,0:T(8,128)S(1)}, u32[]{:S(2)}, u32[]{:S(2)}) async-start(f32[16,32,256]{2,1,0:T(8,128)} %bitcast), calls=%async_computation | async-start | bytes 1048576 | tf_op jit(solution)/shard_map/all_to_all | solution.py:35
  56.1 8.9 %all-to-all-done = f32[16,32,256]{2,1,0:T(8,128)S(1)} async-done(((f32[16,32,256]{2,1,0:T(8,128)}), f32[16,32,256]{2,1,0:T(8,128)S(1)}, u32[]{:S(2)}, u32[]{:S(2)}) %all-to-all-start) | async-done | bytes 524320 | tf_op jit(solution)/shard_map/all_to_all | solution.py:35
  65.9 3.6 %all-to-all-start.1 = ((f32[16,32,256]{2,1,0:T(8,128)}), f32[16,32,256]{2,1,0:T(8,128)S(1)}, u32[]{:S(2)}, u32[]{:S(2)}) async-start(f32[16,32,256]{2,1,0:T(8,128)} %broadcast_in_dim.14), calls=%async_computation.1 | async-start | bytes 1048576 | tf_op jit(solution)/shard_map/all_to_all | solution.py:35
  69.6 8.8 %all-to-all-done.1 = f32[16,32,256]{2,1,0:T(8,128)S(1)} async-done(((f32[16,32,256]{2,1,0:T(8,128)}), f32[16,32,256]{2,1,0:T(8,128)S(1)}, u32[]{:S(2)}, u32[]{:S(2)}) %all-to-all-start.1) | async-done | bytes 524320 | tf_op jit(solution)/shard_map/all_to_all | solution.py:35
  78.4 10.9 %collective-permute-start.1 = (f32[512,256]{1,0:T(8,128)S(1)}, f32[512,256]{1,0:T(8,128)S(1)}, u32[]{:S(2)}, u32[]{:S(2)}) collective-permute-start(f32[512,256]{1,0:T(8,128)S(1)} %bitcast.24), channel_id=1, source_target_pairs={{0,16},{16,0},{1,17},{17,1},{2,18},{18,2},{3,19},{19,3},{4,20},{20... | collective-permute-start | bytes 1572872 | tf_op jit(solution)/shard_map/ppermute | solution.py:172
  92.8 6.5 %all-to-all-start.2 = ((f32[4,16,512]{2,1,0:T(8,128)}), f32[4,16,512]{2,1,0:T(8,128)S(1)}, u32[]{:S(2)}, u32[]{:S(2)}) async-start(f32[4,16,512]{2,1,0:T(8,128)} %broadcast_in_dim.15), calls=%async_computation.2 | async-start | bytes 262144 | tf_op jit(solution)/shard_map/all_to_all | solution.py:35
  100.7 1.5 convolution_add_fusion
  102.2 9.2 %all-to-all-done.2 = f32[4,16,512]{2,1,0:T(8,128)S(1)} async-done(((f32[4,16,512]{2,1,0:T(8,128)}), f32[4,16,512]{2,1,0:T(8,128)S(1)}, u32[]{:S(2)}, u32[]{:S(2)}) %all-to-all-start.2) | async-done | bytes 131104 | tf_op jit(solution)/shard_map/all_to_all | solution.py:35
  111.5 8.7 %all_to_all.53 = f32[4,16,512]{2,1,0:T(8,128)S(1)} all-to-all(f32[4,16,512]{2,1,0:T(8,128)S(1)} %broadcast_in_dim.16), channel_id=1, replica_groups=mesh['far'=4,'near'=4,'core'=2,'x'=4,'y'=4] {'near'}, dimensions={0} | all-to-all | bytes 262144 | tf_op jit(solution)/shard_map/all_to_all | solution.py:35
  120.2 1.1 broadcast_in_dim.17
  121.3 7.8 %all-to-all-start.4 = ((f32[32,16,512]{2,1,0:T(8,128)}), f32[32,16,512]{2,1,0:T(8,128)S(1)}, u32[]{:S(2)}, u32[]{:S(2)}) async-start(f32[32,16,512]{2,1,0:T(8,128)} %broadcast_in_dim.17), calls=%async_computation.4 | async-start | bytes 2097152 | tf_op jit(solution)/shard_map/all_to_all | solution.py:35
  129.8 16.3 %all-to-all-done.4 = f32[32,16,512]{2,1,0:T(8,128)S(1)} async-done(((f32[32,16,512]{2,1,0:T(8,128)}), f32[32,16,512]{2,1,0:T(8,128)S(1)}, u32[]{:S(2)}, u32[]{:S(2)}) %all-to-all-start.4) | async-done | bytes 1048608 | tf_op jit(solution)/shard_map/all_to_all | solution.py:35
  146.1 21.9 %inverse_factor.1 = f32[512,512]{1,0:T(8,128)S(1)} custom-call(f32[512,512]{1,0:T(8,128)S(1)} %bitcast.22), custom_call_target="tpu_custom_call" | custom-call | flops 200000000 | bytes 2097152 | tf_op jit(solution)/shard_map/inverse_factor/pallas_call | solution.py:127
  168.7 26.5 %all_gather.7 = f32[256,896]{1,0:T(8,128)S(1)} all-gather(f32[16,896]{1,0:T(8,128)} %reduce-scatter.2.cloned.1.call-done), channel_id=1, replica_groups=mesh['far'=4,'near'=4,'core'=2,'x'=4,'y'=4] {'far','near'}, dimensions={0}, use_global_device_ids=true | all-gather | bytes 974848 | tf_op jit(solution)/shard_map/all_gather | solution.py:199
  195.3 15.7 %all_to_all.54 = f32[2,256,896]{2,1,0:T(8,128)S(1)} all-to-all(f32[2,256,896]{2,1,0:T(8,128)S(1)} %broadcast_in_dim.18), channel_id=1, replica_groups=mesh['far'=4,'near'=4,'core'=2,'x'=4,'y'=4] {'core'}, dimensions={0} | all-to-all | bytes 3670016 | tf_op jit(solution)/shard_map/all_to_all | solution.py:35
  211.1 2.0 multiply_reduce_fusion
  213.7 5.8 %all-to-all-start.6 = ((f32[16,4,128]{2,1,0:T(4,128)}), f32[16,4,128]{2,1,0:T(4,128)S(1)}, u32[]{:S(2)}, u32[]{:S(2)}) async-start(f32[16,4,128]{2,1,0:T(4,128)} %broadcast_in_dim.20), calls=%async_computation.7 | async-start | bytes 65536 | tf_op jit(solution)/shard_map/all_to_all | solution.py:35
  219.6 3.2 %fusion = f32[256,896]{1,0:T(8,128)} fusion(f32[256,896]{1,0:T(8,128)} %copy-done, f32[256,512]{1,0:T(8,128)S(1)} %fusion.77, f32[512,896]{1,0:T(8,128)S(1)} %get-tuple-element.6), kind=kOutput, calls=%fused_computation.7 | convolution fusion | flops 705101824 | bytes 4194304 | tf_op jit(solution)/shard_map/dot_general | solution.py:25
  222.8 3.3 %all-to-all-done.6 = f32[16,4,128]{2,1,0:T(4,128)S(1)} async-done(((f32[16,4,128]{2,1,0:T(4,128)}), f32[16,4,128]{2,1,0:T(4,128)S(1)}, u32[]{:S(2)}, u32[]{:S(2)}) %all-to-all-start.6) | async-done | bytes 32800 | tf_op jit(solution)/shard_map/all_to_all | solution.py:35
  226.1 1.8 fusion.2
  (44 shorter events, 10.5 us)
Async XLA Ops:
  7.2 10.2 %copy-start.2 = (f32[16,896]{1,0:T(8,128)S(1)}, f32[16,896]{1,0:T(8,128)}, u32[]{:S(2)}) copy-start(f32[16,896]{1,0:T(8,128)} %param.7) | copy-start | bytes 172036
  8.6 91.4 %copy-start = (f32[256,896]{1,0:T(8,128)}, f32[256,896]{1,0:T(8,128)S(1)}, u32[]{:S(2)}) copy-start(f32[256,896]{1,0:T(8,128)S(1)} %convert_add_fusion) | copy-start | bytes 2752516
  8.6 38.9 %collective-permute-start = (f32[256,896]{1,0:T(8,128)S(1)}, f32[256,896]{1,0:T(8,128)S(1)}, u32[]{:S(2)}, u32[]{:S(2)}) collective-permute-start(f32[256,896]{1,0:T(8,128)S(1)} %convert_add_fusion), channel_id=1, source_target_pairs={{0,16},{16,0},{1,17},{17,1},{2,18},{18,2},{3,19},{19,3},{4,20},{20... | collective-permute-start | bytes 2752520 | tf_op jit(solution)/shard_map/ppermute | solution.py:167
  49.3 15.7 %all-to-all-start = ((f32[16,32,256]{2,1,0:T(8,128)}), f32[16,32,256]{2,1,0:T(8,128)S(1)}, u32[]{:S(2)}, u32[]{:S(2)}) async-start(f32[16,32,256]{2,1,0:T(8,128)} %bitcast), calls=%async_computation | async-start | bytes 1048576 | tf_op jit(solution)/shard_map/all_to_all | solution.py:35
  65.9 12.5 %all-to-all-start.1 = ((f32[16,32,256]{2,1,0:T(8,128)}), f32[16,32,256]{2,1,0:T(8,128)S(1)}, u32[]{:S(2)}, u32[]{:S(2)}) async-start(f32[16,32,256]{2,1,0:T(8,128)} %broadcast_in_dim.14), calls=%async_computation.1 | async-start | bytes 1048576 | tf_op jit(solution)/shard_map/all_to_all | solution.py:35
  78.4 12.4 %collective-permute-start.1 = (f32[512,256]{1,0:T(8,128)S(1)}, f32[512,256]{1,0:T(8,128)S(1)}, u32[]{:S(2)}, u32[]{:S(2)}) collective-permute-start(f32[512,256]{1,0:T(8,128)S(1)} %bitcast.24), channel_id=1, source_target_pairs={{0,16},{16,0},{1,17},{17,1},{2,18},{18,2},{3,19},{19,3},{4,20},{20... | collective-permute-start | bytes 1572872 | tf_op jit(solution)/shard_map/ppermute | solution.py:172
  92.8 18.7 %all-to-all-start.2 = ((f32[4,16,512]{2,1,0:T(8,128)}), f32[4,16,512]{2,1,0:T(8,128)S(1)}, u32[]{:S(2)}, u32[]{:S(2)}) async-start(f32[4,16,512]{2,1,0:T(8,128)} %broadcast_in_dim.15), calls=%async_computation.2 | async-start | bytes 262144 | tf_op jit(solution)/shard_map/all_to_all | solution.py:35
  99.3 69.4 %reduce-scatter.2.cloned.1.call-start = ((), (), s32[]{:S(2)}) async-start(), calls=%async_computation.8 | async-start | bytes 974848 | tf_op jit(solution)/shard_map/reduce_scatter | solution.py:185
  121.3 24.8 %all-to-all-start.4 = ((f32[32,16,512]{2,1,0:T(8,128)}), f32[32,16,512]{2,1,0:T(8,128)S(1)}, u32[]{:S(2)}, u32[]{:S(2)}) async-start(f32[32,16,512]{2,1,0:T(8,128)} %broadcast_in_dim.17), calls=%async_computation.4 | async-start | bytes 2097152 | tf_op jit(solution)/shard_map/all_to_all | solution.py:35
  213.7 12.3 %all-to-all-start.6 = ((f32[16,4,128]{2,1,0:T(4,128)}), f32[16,4,128]{2,1,0:T(4,128)S(1)}, u32[]{:S(2)}, u32[]{:S(2)}) async-start(f32[16,4,128]{2,1,0:T(4,128)} %broadcast_in_dim.20), calls=%async_computation.7 | async-start | bytes 65536 | tf_op jit(solution)/shard_map/all_to_all | solution.py:35
  219.5 6.5 %copy-start.1 = (bf16[256,896]{1,0:T(8,128)(2,1)S(1)}, bf16[256,896]{1,0:T(8,128)(2,1)}, u32[]{:S(2)}) copy-start(bf16[256,896]{1,0:T(8,128)(2,1)} %param.4) | copy-start | bytes 1376260
Sparse Core Ops, SparseCore 0:
  103.5 57.8 reduce-scatter.1

commit v4 on v3

--- a/solution.py
+++ b/solution.py
@@ -1,3 +1,4 @@
+import functools
 import math
 
 import jax
@@ -15,7 +16,6 @@
 epsilon = 1e-06
 
 DEPTH = ("far", "near")
-PLANE = ("x", "y", "core")
 COLUMN_BLOCKS = ("x", "y")
 HIGH = lax.Precision.HIGH
 SWAP = [(0, 1), (1, 0)]
@@ -48,11 +48,10 @@
 TILE = 128
 
 
-def factor_step(work, wide, at):
+def factor_step(work, wide, at, block):
     lane = lax.broadcasted_iota(jnp.int32,(SUB,TILE),1)
     sub = lax.broadcasted_iota(jnp.int32,(SUB,TILE),0)
     own = (lane>=at)&(lane<at+SUB)
-    block = work[at:at+SUB,:]
     for j in range(SUB):
         wide[j] = jnp.broadcast_to(block[:,at+j:at+j+1],(SUB,TILE))
     work[at:at+SUB,:] = jnp.where(own, jnp.where(lane-at==sub,1.0,0.0), block)
@@ -76,8 +75,9 @@
     for i in range(SUB-1):
         out = jnp.where(sub==i, rows[i], out)
     work[at:at+SUB,:] = out
-    nxt = at+SUB
-    if nxt < TILE:
+    far = at+SUB*4
+    ahead = None
+    for nxt in range(at+SUB, min(far,TILE), SUB):
         block = work[nxt:nxt+SUB,:]
         left=[]
         total = jnp.where(own,0.0,block)
@@ -87,23 +87,33 @@
                 col = col - left[m]*low[j][m]
             left.append(col*inv[j])
             total = total - left[j]*rows[j]
-        work[nxt:nxt+SUB,:] = total
-    far = nxt+SUB
+        if nxt == at+SUB:
+            ahead = total
+        else:
+            work[nxt:nxt+SUB,:] = total
     if far < TILE:
         prod = dot(out,out,0,0)
         rest = work[far:,:]
         lanes = lax.broadcasted_iota(jnp.int32,rest.shape,1)
         work[far:,:] = jnp.where((lanes>=at)&(lanes<at+SUB),0.0,rest) - prod[far:,:]
-
-
-def inverse_factor_kernel(gram_ref, out_ref, work, wide):
-    n = gram_ref.shape[0]; tiles = n//TILE
-    out_ref[...] = gram_ref[...]
+    return ahead
+
+
+def inverse_factor_kernel(core_ref, own_ref, other_ref, out_ref, work, wide, *, owned):
+    n = out_ref.shape[0]
+    tiles = n//TILE
+    core = core_ref[0]
+    for t in range(n // (2 * owned)):
+        first = pl.multiple_of(2 * t * owned + core * owned, owned)
+        second = pl.multiple_of(2 * t * owned + (1 - core) * owned, owned)
+        out_ref[pl.ds(first, owned), :] = own_ref[t*owned:(t+1)*owned, :]
+        out_ref[pl.ds(second, owned), :] = other_ref[t*owned:(t+1)*owned, :]
     def panel(p, carry):
         at = pl.multiple_of(p*TILE,TILE)
         work[...] = out_ref[pl.ds(at,TILE),pl.ds(at,TILE)]
+        block = work[0:SUB,:]
         for k in range(TILE//SUB):
-            factor_step(work, wide.at[k%2], k*SUB)
+            block = factor_step(work, wide.at[k%2], k*SUB, block)
         r = lax.broadcasted_iota(jnp.int32,(TILE,TILE),0); c = lax.broadcasted_iota(jnp.int32,(TILE,TILE),1)
         inverse = jnp.where(r>=c, work[...], 0.0)
         out_ref[pl.ds(at,TILE),pl.ds(at,TILE)] = jnp.where(r==c,1.0,0.0)
@@ -113,22 +123,20 @@
             @pl.when(q>p)
             def _():
                 out_ref[q*TILE:(q+1)*TILE,pl.ds(at,TILE)] = jnp.zeros((TILE,TILE),jnp.float32)
-                out_ref[q*TILE:(q+1)*TILE,:] = out_ref[q*TILE:(q+1)*TILE,:] - dot(
-                    new[:,q*TILE:(q+1)*TILE],new,0,0
-                )
+                out_ref[q*TILE:(q+1)*TILE,:] = out_ref[q*TILE:(q+1)*TILE,:] - dot(new[:,q*TILE:(q+1)*TILE],new,0,0)
         return carry
     lax.fori_loop(0,tiles,panel,0)
     for q in range(tiles-1):
         out_ref[q*TILE:(q+1)*TILE,(q+1)*TILE:] = jnp.zeros((TILE,n-(q+1)*TILE),jnp.float32)
 
-
-def inverse_factor(gram):
-    size = gram.shape[0]
+def inverse_factor(core, own, other, owned):
+    size = own.shape[1]
+    whole = pl.BlockSpec(memory_space=pltpu.VMEM)
     return pl.pallas_call(
-        inverse_factor_kernel,
+        functools.partial(inverse_factor_kernel, owned=owned),
         out_shape=jax.ShapeDtypeStruct((size, size), jnp.float32),
-        in_specs=[pl.BlockSpec(memory_space=pltpu.VMEM)],
-        out_specs=pl.BlockSpec(memory_space=pltpu.VMEM),
+        in_specs=[pl.BlockSpec(memory_space=pltpu.SMEM), whole, whole],
+        out_specs=whole,
         scratch_shapes=[
             pltpu.VMEM((TILE, TILE), jnp.float32),
             pltpu.VMEM((2, SUB, SUB, TILE), jnp.float32),
@@ -138,7 +146,7 @@
         ),
         compiler_params=pltpu.CompilerParams(vmem_limit_bytes=8 * 2**20),
         name="inverse_factor",
-    )(gram)
+    )(core.reshape(1), own, other)
 
 
 def total(array, count):
@@ -149,13 +157,19 @@
     return jnp.where(
         core == 0, jnp.concatenate([own, other], axis), jnp.concatenate([other, own], axis)
     )
+
+
+def one_side(rank, owned, core):
+    ranks = lax.broadcasted_iota(jnp.int32, (rank, rank // 2), 0)
+    kept = lax.broadcasted_iota(jnp.int32, (rank, rank // 2), 1)
+    source = (kept // owned * 2 + core) * owned + kept % owned
+    return (ranks == source).astype(jnp.float32)
 
 
 def on_device(weights, momentum, gradient, warm_basis):
     rows, columns = momentum.shape
     owned = warm_basis.shape[0]
     depth = lax.axis_size(DEPTH)
-    plane = lax.axis_size(PLANE)
     blocks = lax.axis_size(COLUMN_BLOCKS)
     far, near = lax.axis_size("far"), lax.axis_size("near")
     rank = owned * depth * 2
@@ -172,17 +186,15 @@
     others = lax.ppermute(projected, "core", SWAP)
     others = jnp.concatenate([others[rows:], others[:rows]])
 
-    def natural(first, count):
-        kept = lax.broadcasted_iota(jnp.int32, (rank, count), 0)
-        ranks = lax.broadcasted_iota(jnp.int32, (rank, count), 1) + first
-        source = ranks // owned % 2 * half + ranks // (2 * owned) * owned + ranks % owned
-        return (kept == source).astype(jnp.float32)
-
-    order = natural(0, rank)
-    joined = by_core(core, projected, others, 1)
-    mine = dot(joined, natural(core * half, half), 1, 0)
-    moved = dot(mine[:rows], blended, 0, 0, HIGH) + dot(mine[rows:], partner, 0, 0, HIGH)
+    moved = dot(projected[:rows], blended, 0, 0, HIGH) + dot(
+        projected[rows:], partner, 0, 0, HIGH
+    )
     moved = lax.psum_scatter(moved, DEPTH, scatter_dimension=0, tiled=True)
+
+    kept = lax.broadcasted_iota(jnp.int32, (rank, rank), 0)
+    ranks = lax.broadcasted_iota(jnp.int32, (rank, rank), 1)
+    source = ranks // owned % 2 * half + ranks // (2 * owned) * owned + ranks % owned
+    order = (kept == source).astype(jnp.float32)
 
     share = half // blocks
     picked = lax.dynamic_slice_in_dim(
@@ -193,14 +205,17 @@
     gram = dot(by_core(core, same, cross, 1), order, 1, 0)
     gram = total(spread(gram, "far", far), far)
     gram = total(spread(gram, "near", near), near)
-    gram = spread(gram, PLANE, plane)
-    inverse = inverse_factor(gram)
-
-    moved = lax.all_gather(moved, DEPTH, axis=0, tiled=True)
-    moved = spread(moved, "core", 2)
-    own_projected = dot(joined[:rows], order, 1, 0)
+    gram = spread(gram, COLUMN_BLOCKS, blocks)
+    inverse = inverse_factor(core, gram, lax.ppermute(gram, "core", SWAP), owned)
+
+    moved = lax.all_gather(moved + inverse[0, rank - 1], DEPTH, axis=0, tiled=True)
+    handed = lax.ppermute(moved, "core", SWAP)
+    joined = by_core(core, projected[:rows], others[:rows], 1)
+    own_projected = dot(joined, order, 1, 0)
     orthonormal = dot(own_projected, inverse, 1, 1, HIGH)
-    coefficients = dot(inverse, moved, 1, 0, HIGH)
+    coefficients = dot(
+        dot(inverse, one_side(rank, owned, core), 1, 0, HIGH), moved, 1, 0, HIGH
+    ) + dot(dot(inverse, one_side(rank, owned, 1 - core), 1, 0, HIGH), handed, 1, 0, HIGH)
     energy = jnp.sum(coefficients * coefficients, axis=1).reshape(rank // 128, 128)
     energy = total(spread(energy, COLUMN_BLOCKS, blocks), blocks).reshape(rank)
     scale = lax.rsqrt(energy / FF + epsilon)

time: 236 us -> 224 us (0.949)
  waiting for transfers between devices: 47.4 us -> 22.1 us
  blocking collectives: 80 us -> 100 us
  starting transfers between devices: 50.1 us -> 45.6 us
  Pallas kernels: 21.9 us -> 17.9 us
    all_to_all x5 -> x3, waiting for transfers between devices: 46.5 us -> 22.1 us  [exchange(): return lax.all_to_all(array, axes, 0, 0, tiled=True)]
    all_to_all x2 -> x3, blocking collectives: 24.4 us -> 44.7 us  [exchange(): return lax.all_to_all(array, axes, 0, 0, tiled=True)]
    all_to_all x5 -> x3, starting transfers between devices: 30.5 us -> 10.6 us  [exchange(): return lax.all_to_all(array, axes, 0, 0, tiled=True)]
    ppermute x0 -> x2, starting transfers between devices: none -> 15.2 us  [the longest x1 8.91 us: on_device(): handed = lax.ppermute(moved, 'core', SWAP)]
    pallas_call x1, Pallas kernels: 21.9 us -> 17.9 us  [inverse_factor(): pl.pallas_call(functools.partial(inverse_factor_kernel, owned=owned), out...]
    dot_general x13 -> x15, matrix products: 15 us -> 16.1 us  [dot(): lax.dot_general(left_side, right_side, (((contract_left,), (contract_righ...]
  transfers between devices with their start and end apart: 8 -> 8, of which waited for: 6 -> 3; matrix products, arithmetic and copies ran while one was open for 4% -> 6% of each run, Pallas kernels for 9% -> 8%
where the time goes in v4:
time: 224 us; the launch traced here: 223 us
  blocking collectives  100 us (45%)
  starting transfers between devices  45.6 us (20%)
  waiting for transfers between devices  22.1 us (10%)
  Pallas kernels  17.9 us (8%)
  matrix products  16.1 us (7%)
  between operations  14.3 us (6%)
  other arithmetic  3.73 us (2%)
  local copies, waits for them, and re-layouts  3.1 us (1%)
    all_to_all x3, blocking collectives, exchange(): return lax.all_to_all(array, axes, 0, 0, tiled=True)  44.7 us
    all_gather x1, blocking collectives, on_device(): basis = lax.all_gather(warm_basis, DEPTH, axis=0, tiled=True)  29 us
    all_gather x1, blocking collectives, on_device(): lax.all_gather(moved + inverse[0, rank - 1], DEPTH, axis=0, tiled=True)  26.2 us
    all_to_all x3, waiting for transfers between devices, exchange(): return lax.all_to_all(array, axes, 0, 0, tiled=True)  22.1 us
    pallas_call x1, Pallas kernels, inverse_factor(): pl.pallas_call(functools.partial(inverse_factor_kernel, owned=owned), out...  17.9 us
    dot_general x15, matrix products, dot(): lax.dot_general(left_side, right_side, (((contract_left,), (contract_righ...  16.1 us
    ppermute x1, starting transfers between devices, on_device(): others = lax.ppermute(projected, 'core', SWAP)  10.9 us
    all_to_all x3, starting transfers between devices, exchange(): return lax.all_to_all(array, axes, 0, 0, tiled=True)  10.6 us
  transfers between devices with their start and end apart: 8, of which 3 were waited for; matrix products, arithmetic and copies ran while one was open for 6% of the time, Pallas kernels for 8%

profile of v4, /device:TPU:1, one launch (start us, length us, event | category | flops | bytes accessed | tf_op | source)
XLA Modules:
  0.0 222.8 jit_solution(16993575573263652274)
XLA Ops:
  7.2 1.4 convert_add_fusion
  8.6 8.8 %collective-permute-start = (f32[256,896]{1,0:T(8,128)S(1)}, f32[256,896]{1,0:T(8,128)S(1)}, u32[]{:S(2)}, u32[]{:S(2)}) collective-permute-start(f32[256,896]{1,0:T(8,128)S(1)} %convert_add_fusion), channel_id=1, source_target_pairs={{0,16},{16,0},{1,17},{17,1},{2,18},{18,2},{3,19},{19,3},{4,20},{20... | collective-permute-start | bytes 2752520 | tf_op jit(solution)/shard_map/ppermute | solution.py:181
  17.4 29.0 %all_gather.6 = f32[256,896]{1,0:T(8,128)S(1)} all-gather(f32[16,896]{1,0:T(8,128)S(1)} %copy-done.1), channel_id=1, replica_groups=mesh['far'=4,'near'=4,'core'=2,'x'=4,'y'=4] {'far','near'}, dimensions={0}, use_global_device_ids=true | all-gather | bytes 974848 | tf_op jit(solution)/shard_map/all_gather | solution.py:182
  47.4 1.0 fusion.79
  48.5 15.5 %all_to_all.44 = f32[16,32,256]{2,1,0:T(8,128)S(1)} all-to-all(f32[16,32,256]{2,1,0:T(8,128)S(1)} %bitcast.35), channel_id=1, replica_groups=mesh['far'=4,'near'=4,'core'=2,'x'=4,'y'=4] {'x','y'}, dimensions={0} | all-to-all | bytes 1048576 | tf_op jit(solution)/shard_map/all_to_all | solution.py:35
  64.9 3.6 %all-to-all-start.1 = ((f32[16,32,256]{2,1,0:T(8,128)}), f32[16,32,256]{2,1,0:T(8,128)S(1)}, u32[]{:S(2)}, u32[]{:S(2)}) async-start(f32[16,32,256]{2,1,0:T(8,128)} %broadcast_in_dim.12), calls=%async_computation.1 | async-start | bytes 1048576 | tf_op jit(solution)/shard_map/all_to_all | solution.py:35
  68.6 8.8 %all-to-all-done.1 = f32[16,32,256]{2,1,0:T(8,128)S(1)} async-done(((f32[16,32,256]{2,1,0:T(8,128)}), f32[16,32,256]{2,1,0:T(8,128)S(1)}, u32[]{:S(2)}, u32[]{:S(2)}) %all-to-all-start.1) | async-done | bytes 524320 | tf_op jit(solution)/shard_map/all_to_all | solution.py:35
  77.4 10.9 %collective-permute-start.1 = (f32[512,256]{1,0:T(8,128)S(1)}, f32[512,256]{1,0:T(8,128)S(1)}, u32[]{:S(2)}, u32[]{:S(2)}) collective-permute-start(f32[512,256]{1,0:T(8,128)S(1)} %bitcast.32), channel_id=1, source_target_pairs={{0,16},{16,0},{1,17},{17,1},{2,18},{18,2},{3,19},{19,3},{4,20},{20... | collective-permute-start | bytes 1572872 | tf_op jit(solution)/shard_map/ppermute | solution.py:186
  89.0 1.5 convolution_add_fusion.1
  92.4 21.3 %all_to_all.45 = f32[4,16,512]{2,1,0:T(8,128)S(1)} all-to-all(f32[4,16,512]{2,1,0:T(8,128)S(1)} %broadcast_in_dim.13), channel_id=1, replica_groups=mesh['far'=4,'near'=4,'core'=2,'x'=4,'y'=4] {'far'}, dimensions={0} | all-to-all | bytes 262144 | tf_op jit(solution)/shard_map/all_to_all | solution.py:35
  113.7 7.9 %all_to_all.46 = f32[4,16,512]{2,1,0:T(8,128)S(1)} all-to-all(f32[4,16,512]{2,1,0:T(8,128)S(1)} %broadcast_in_dim.14), channel_id=1, replica_groups=mesh['far'=4,'near'=4,'core'=2,'x'=4,'y'=4] {'near'}, dimensions={0} | all-to-all | bytes 262144 | tf_op jit(solution)/shard_map/all_to_all | solution.py:35
  122.5 3.6 %all-to-all-start.4 = ((f32[16,16,512]{2,1,0:T(8,128)}), f32[16,16,512]{2,1,0:T(8,128)S(1)}, u32[]{:S(2)}, u32[]{:S(2)}) async-start(f32[16,16,512]{2,1,0:T(8,128)} %broadcast_in_dim.15), calls=%async_computation.4 | async-start | bytes 1048576 | tf_op jit(solution)/shard_map/all_to_all | solution.py:35
  126.1 8.9 %all-to-all-done.4 = f32[16,16,512]{2,1,0:T(8,128)S(1)} async-done(((f32[16,16,512]{2,1,0:T(8,128)}), f32[16,16,512]{2,1,0:T(8,128)S(1)}, u32[]{:S(2)}, u32[]{:S(2)}) %all-to-all-start.4) | async-done | bytes 524320 | tf_op jit(solution)/shard_map/all_to_all | solution.py:35
  135.0 6.3 %collective-permute-start.2 = (f32[256,512]{1,0:T(8,128)S(1)}, f32[256,512]{1,0:T(8,128)S(1)}, u32[]{:S(2)}, u32[]{:S(2)}) collective-permute-start(f32[256,512]{1,0:T(8,128)S(1)} %bitcast.30), channel_id=1, source_target_pairs={{0,16},{16,0},{1,17},{17,1},{2,18},{18,2},{3,19},{19,3},{4,20},{20... | collective-permute-start | bytes 1572872 | tf_op jit(solution)/shard_map/ppermute | solution.py:209
  141.3 1.5 fusion.10
  142.8 17.9 %inverse_factor.1 = f32[512,512]{1,0:T(8,128)S(1)} custom-call(s32[1]{0:T(128)} %bitcast.3.core_ref, f32[256,512]{1,0:T(8,128)S(1)} %bitcast.31, f32[256,512]{1,0:T(8,128)S(1)} %collective-permute-done.2.other_ref), custom_call_target="tpu_custom_call" | custom-call | flops 200000000 | bytes 2097152 | tf_op jit(solution)/shard_map/inverse_factor/pallas_call | solution.py:135
  161.3 1.5 broadcast_add_fusion
  162.8 26.2 %all_gather.7 = f32[256,896]{1,0:T(8,128)S(1)} all-gather(f32[16,896]{1,0:T(8,128)S(1)} %broadcast_add_fusion), channel_id=1, replica_groups=mesh['far'=4,'near'=4,'core'=2,'x'=4,'y'=4] {'far','near'}, dimensions={0}, use_global_device_ids=true | all-gather | bytes 974848 | tf_op jit(solution)/shard_map/all_gather | solution.py:211
  189.0 8.9 %collective-permute-start.3 = (f32[256,896]{1,0:T(8,128)S(1)}, f32[256,896]{1,0:T(8,128)S(1)}, u32[]{:S(2)}, u32[]{:S(2)}) collective-permute-start(f32[256,896]{1,0:T(8,128)S(1)} %all_gather.7), channel_id=1, source_target_pairs={{0,16},{16,0},{1,17},{17,1},{2,18},{18,2},{3,19},{19,3},{4,20},{20... | collective-permute-start | bytes 2752520 | tf_op jit(solution)/shard_map/ppermute | solution.py:212
  200.5 1.2 multiply_reduce_fusion
  202.4 3.5 %all-to-all-start.5 = ((f32[16,4,128]{2,1,0:T(4,128)}), f32[16,4,128]{2,1,0:T(4,128)S(1)}, u32[]{:S(2)}, u32[]{:S(2)}) async-start(f32[16,4,128]{2,1,0:T(4,128)} %broadcast_in_dim.17), calls=%async_computation.6 | async-start | bytes 65536 | tf_op jit(solution)/shard_map/all_to_all | solution.py:35
  205.9 2.0 fusion
  207.8 4.4 %all-to-all-done.5 = f32[16,4,128]{2,1,0:T(4,128)S(1)} async-done(((f32[16,4,128]{2,1,0:T(4,128)}), f32[16,4,128]{2,1,0:T(4,128)S(1)}, u32[]{:S(2)}, u32[]{:S(2)}) %all-to-all-start.5) | async-done | bytes 32800 | tf_op jit(solution)/shard_map/all_to_all | solution.py:35
  212.3 2.8 %fusion.2 = bf16[256,896]{1,0:T(8,128)(2,1)} fusion(f32[512,896]{1,0:T(8,128)S(1)} %get-tuple-element.8, bf16[256,896]{1,0:T(8,128)(2,1)} %param.4, f32[256,512]{1,0:T(8,128)S(1)} %fusion.80, f32[512]{0:T(512)S(1)} %rsqrt_bitcast_fusion), kind=kOutput, calls=%fused_computation.12 | convolution fusion | flops 705691648 | bytes 3278848 | tf_op jit(solution)/shard_map/dot_general | solution.py:25
  (44 shorter events, 10.0 us)
Async XLA Ops:
  7.2 10.2 %copy-start.1 = (f32[16,896]{1,0:T(8,128)S(1)}, f32[16,896]{1,0:T(8,128)}, u32[]{:S(2)}) copy-start(f32[16,896]{1,0:T(8,128)} %param.7) | copy-start | bytes 172036
  8.6 38.9 %collective-permute-start = (f32[256,896]{1,0:T(8,128)S(1)}, f32[256,896]{1,0:T(8,128)S(1)}, u32[]{:S(2)}, u32[]{:S(2)}) collective-permute-start(f32[256,896]{1,0:T(8,128)S(1)} %convert_add_fusion), channel_id=1, source_target_pairs={{0,16},{16,0},{1,17},{17,1},{2,18},{18,2},{3,19},{19,3},{4,20},{20... | collective-permute-start | bytes 2752520 | tf_op jit(solution)/shard_map/ppermute | solution.py:181
  64.9 12.5 %all-to-all-start.1 = ((f32[16,32,256]{2,1,0:T(8,128)}), f32[16,32,256]{2,1,0:T(8,128)S(1)}, u32[]{:S(2)}, u32[]{:S(2)}) async-start(f32[16,32,256]{2,1,0:T(8,128)} %broadcast_in_dim.12), calls=%async_computation.1 | async-start | bytes 1048576 | tf_op jit(solution)/shard_map/all_to_all | solution.py:35
  68.5 92.8 %reduce-scatter.2.cloned.1.call-start = ((), (), s32[]{:S(2)}) async-start(), calls=%async_computation.7 | async-start | bytes 974848 | tf_op jit(solution)/shard_map/reduce_scatter | solution.py:192
  77.4 13.8 %collective-permute-start.1 = (f32[512,256]{1,0:T(8,128)S(1)}, f32[512,256]{1,0:T(8,128)S(1)}, u32[]{:S(2)}, u32[]{:S(2)}) collective-permute-start(f32[512,256]{1,0:T(8,128)S(1)} %bitcast.32), channel_id=1, source_target_pairs={{0,16},{16,0},{1,17},{17,1},{2,18},{18,2},{3,19},{19,3},{4,20},{20... | collective-permute-start | bytes 1572872 | tf_op jit(solution)/shard_map/ppermute | solution.py:186
  122.5 12.5 %all-to-all-start.4 = ((f32[16,16,512]{2,1,0:T(8,128)}), f32[16,16,512]{2,1,0:T(8,128)S(1)}, u32[]{:S(2)}, u32[]{:S(2)}) async-start(f32[16,16,512]{2,1,0:T(8,128)} %broadcast_in_dim.15), calls=%async_computation.4 | async-start | bytes 1048576 | tf_op jit(solution)/shard_map/all_to_all | solution.py:35
  135.0 7.8 %collective-permute-start.2 = (f32[256,512]{1,0:T(8,128)S(1)}, f32[256,512]{1,0:T(8,128)S(1)}, u32[]{:S(2)}, u32[]{:S(2)}) collective-permute-start(f32[256,512]{1,0:T(8,128)S(1)} %bitcast.30), channel_id=1, source_target_pairs={{0,16},{16,0},{1,17},{17,1},{2,18},{18,2},{3,19},{19,3},{4,20},{20... | collective-permute-start | bytes 1572872 | tf_op jit(solution)/shard_map/ppermute | solution.py:209
  162.8 36.1 %copy-start = (f32[256,512]{1,0:T(8,128)S(1)}, f32[256,512]{1,0:T(8,128)}, u32[]{:S(2)}) copy-start(f32[256,512]{1,0:T(8,128)} %fusion.10) | copy-start | bytes 1572868
  189.0 11.5 %collective-permute-start.3 = (f32[256,896]{1,0:T(8,128)S(1)}, f32[256,896]{1,0:T(8,128)S(1)}, u32[]{:S(2)}, u32[]{:S(2)}) collective-permute-start(f32[256,896]{1,0:T(8,128)S(1)} %all_gather.7), channel_id=1, source_target_pairs={{0,16},{16,0},{1,17},{17,1},{2,18},{18,2},{3,19},{19,3},{4,20},{20... | collective-permute-start | bytes 2752520 | tf_op jit(solution)/shard_map/ppermute | solution.py:212
  202.4 9.9 %all-to-all-start.5 = ((f32[16,4,128]{2,1,0:T(4,128)}), f32[16,4,128]{2,1,0:T(4,128)S(1)}, u32[]{:S(2)}, u32[]{:S(2)}) async-start(f32[16,4,128]{2,1,0:T(4,128)} %broadcast_in_dim.17), calls=%async_computation.6 | async-start | bytes 65536 | tf_op jit(solution)/shard_map/all_to_all | solution.py:35
Sparse Core Ops, SparseCore 0:
  90.7 54.9 reduce-scatter.1

commit v5 on v4

--- a/solution.py
+++ b/solution.py
@@ -142,7 +142,7 @@
             pltpu.VMEM((2, SUB, SUB, TILE), jnp.float32),
         ],
         cost_estimate=pl.CostEstimate(
-            flops=200_000_000, bytes_accessed=4 * size * size * 2, transcendentals=size
+            flops=8_000_000_000, bytes_accessed=4 * size * size * 2, transcendentals=size
         ),
         compiler_params=pltpu.CompilerParams(vmem_limit_bytes=8 * 2**20),
         name="inverse_factor",
@@ -171,7 +171,6 @@
     owned = warm_basis.shape[0]
     depth = lax.axis_size(DEPTH)
     blocks = lax.axis_size(COLUMN_BLOCKS)
-    far, near = lax.axis_size("far"), lax.axis_size("near")
     rank = owned * depth * 2
     half = rank // 2
     core = lax.axis_index("core")
@@ -189,7 +188,7 @@
     moved = dot(projected[:rows], blended, 0, 0, HIGH) + dot(
         projected[rows:], partner, 0, 0, HIGH
     )
-    moved = lax.psum_scatter(moved, DEPTH, scatter_dimension=0, tiled=True)
+    moved = total(exchange(moved, DEPTH), depth)
 
     kept = lax.broadcasted_iota(jnp.int32, (rank, rank), 0)
     ranks = lax.broadcasted_iota(jnp.int32, (rank, rank), 1)
@@ -203,12 +202,10 @@
     same = dot(picked, projected, 0, 0)
     cross = dot(picked, others, 0, 0)
     gram = dot(by_core(core, same, cross, 1), order, 1, 0)
-    gram = total(spread(gram, "far", far), far)
-    gram = total(spread(gram, "near", near), near)
-    gram = spread(gram, COLUMN_BLOCKS, blocks)
+    gram = total(lax.all_gather(gram, DEPTH, axis=0, tiled=True), depth)
+    gram = spread(gram + moved[0, 0] * 0.0, COLUMN_BLOCKS, blocks)
+    moved = spread(moved + gram[0, 0] * 0.0, DEPTH, depth)
     inverse = inverse_factor(core, gram, lax.ppermute(gram, "core", SWAP), owned)
-
-    moved = lax.all_gather(moved + inverse[0, rank - 1], DEPTH, axis=0, tiled=True)
     handed = lax.ppermute(moved, "core", SWAP)
     joined = by_core(core, projected[:rows], others[:rows], 1)
     own_projected = dot(joined, order, 1, 0)

time: 224 us -> 231 us (1.031)
  starting transfers between devices: 45.6 us -> 66.3 us
  waiting for transfers between devices: 22.1 us -> 5.26 us
  blocking collectives: 100 us -> 116 us
  between operations: 14.3 us -> 2.26 us
    all_gather x1, blocking collectives: 26.2 us -> 47.3 us  [on_device(): gram = total(lax.all_gather(gram, DEPTH, axis=0, tiled=True), depth)]
    all_to_all x3, waiting for transfers between devices: 22.1 us -> 4.43 us  [exchange(): return lax.all_to_all(array, axes, 0, 0, tiled=True)]
    ppermute x1, starting transfers between devices: 6.31 us -> 13.8 us  [on_device(): lax.ppermute(gram, 'core', SWAP)]
    all_to_all x3, starting transfers between devices: 10.6 us -> 17.6 us  [exchange(): return lax.all_to_all(array, axes, 0, 0, tiled=True)]
    ppermute x1, starting transfers between devices: 8.91 us -> 14.3 us  [on_device(): handed = lax.ppermute(moved, 'core', SWAP)]
    all_to_all x3, blocking collectives: 44.7 us -> 39.3 us  [exchange(): return lax.all_to_all(array, axes, 0, 0, tiled=True)]
  transfers between devices with their start and end apart: 8 -> 7, of which waited for: 3 -> 2; matrix products, arithmetic and copies ran while one was open for 6% -> 4% of each run, Pallas kernels for 8% -> 8%
where the time goes in v5:
time: 231 us; the launch traced here: 230 us
  blocking collectives  116 us (50%)
  starting transfers between devices  66.3 us (29%)
  Pallas kernels  17.9 us (8%)
  matrix products  17.3 us (7%)
  waiting for transfers between devices  5.26 us (2%)
  local copies, waits for them, and re-layouts  2.89 us (1%)
  other arithmetic  2.34 us (1%)
    all_gather x1, blocking collectives, on_device(): gram = total(lax.all_gather(gram, DEPTH, axis=0, tiled=True), depth)  47.3 us
    all_to_all x3, blocking collectives, exchange(): return lax.all_to_all(array, axes, 0, 0, tiled=True)  39.3 us
    all_gather x1, blocking collectives, on_device(): basis = lax.all_gather(warm_basis, DEPTH, axis=0, tiled=True)  29 us
    pallas_call x1, Pallas kernels, inverse_factor(): pl.pallas_call(functools.partial(inverse_factor_kernel, owned=owned), out...  17.9 us
    all_to_all x3, starting transfers between devices, exchange(): return lax.all_to_all(array, axes, 0, 0, tiled=True)  17.6 us
    dot_general x15, matrix products, dot(): lax.dot_general(left_side, right_side, (((contract_left,), (contract_righ...  17.3 us
    ppermute x1, starting transfers between devices, on_device(): handed = lax.ppermute(moved, 'core', SWAP)  14.3 us
    ppermute x1, starting transfers between devices, on_device(): lax.ppermute(gram, 'core', SWAP)  13.8 us
  transfers between devices with their start and end apart: 7, of which 2 were waited for; matrix products, arithmetic and copies ran while one was open for 4% of the time, Pallas kernels for 8%

profile of v5, /device:TPU:1, one launch (start us, length us, event | category | flops | bytes accessed | tf_op | source)
XLA Modules:
  0.0 229.9 jit_solution(10484569822340377880)
XLA Ops:
  0.6 1.4 convert_add_fusion
  2.0 8.8 %collective-permute-start = (f32[256,896]{1,0:T(8,128)S(1)}, f32[256,896]{1,0:T(8,128)S(1)}, u32[]{:S(2)}, u32[]{:S(2)}) collective-permute-start(f32[256,896]{1,0:T(8,128)S(1)} %convert_add_fusion), channel_id=1, source_target_pairs={{0,16},{16,0},{1,17},{17,1},{2,18},{18,2},{3,19},{19,3},{4,20},{20... | collective-permute-start | bytes 2752520 | tf_op jit(solution)/shard_map/ppermute | solution.py:180
  10.8 29.0 %all_gather.6 = f32[256,896]{1,0:T(8,128)S(1)} all-gather(f32[16,896]{1,0:T(8,128)S(1)} %copy-done.1), channel_id=1, replica_groups=mesh['far'=4,'near'=4,'core'=2,'x'=4,'y'=4] {'far','near'}, dimensions={0}, use_global_device_ids=true | all-gather | bytes 974848 | tf_op jit(solution)/shard_map/all_gather | solution.py:181
  39.9 1.0 fusion.78
  40.9 1.0 fusion.79
  42.0 15.5 %all_to_all.50 = f32[16,32,256]{2,1,0:T(8,128)S(1)} all-to-all(f32[16,32,256]{2,1,0:T(8,128)S(1)} %bitcast.42), channel_id=1, replica_groups=mesh['far'=4,'near'=4,'core'=2,'x'=4,'y'=4] {'x','y'}, dimensions={0} | all-to-all | bytes 1048576 | tf_op jit(solution)/shard_map/all_to_all | solution.py:35
  57.6 11.9 %all_to_all.51 = f32[16,32,256]{2,1,0:T(8,128)S(1)} all-to-all(f32[16,32,256]{2,1,0:T(8,128)S(1)} %broadcast_in_dim.10), channel_id=1, replica_groups=mesh['far'=4,'near'=4,'core'=2,'x'=4,'y'=4] {'x','y'}, dimensions={0} | all-to-all | bytes 1048576 | tf_op jit(solution)/shard_map/all_to_all | solution.py:35
  70.2 1.6 convolution_add_fusion.1
  71.7 6.3 %all-to-all-start.2 = ((f32[16,16,896]{2,1,0:T(8,128)}), f32[16,16,896]{2,1,0:T(8,128)S(1)}, u32[]{:S(2)}, u32[]{:S(2)}) async-start(f32[16,16,896]{2,1,0:T(8,128)} %bitcast.40), calls=%async_computation.2 | async-start | bytes 1835008 | tf_op jit(solution)/shard_map/all_to_all | solution.py:35
  78.0 11.8 %collective-permute-start.1 = (f32[512,256]{1,0:T(8,128)S(1)}, f32[512,256]{1,0:T(8,128)S(1)}, u32[]{:S(2)}, u32[]{:S(2)}) collective-permute-start(f32[512,256]{1,0:T(8,128)S(1)} %bitcast.37), channel_id=1, source_target_pairs={{0,16},{16,0},{1,17},{17,1},{2,18},{18,2},{3,19},{19,3},{4,20},{20... | collective-permute-start | bytes 1572872 | tf_op jit(solution)/shard_map/ppermute | solution.py:185
  92.5 47.3 %all_gather.7 = f32[256,512]{1,0:T(8,128)S(1)} all-gather(f32[16,512]{1,0:T(8,128)S(1)} %fusion.48), channel_id=1, replica_groups=mesh['far'=4,'near'=4,'core'=2,'x'=4,'y'=4] {'far','near'}, dimensions={0}, use_global_device_ids=true | all-gather | bytes 557056 | tf_op jit(solution)/shard_map/all_gather | solution.py:205
  141.2 11.9 %all_to_all.52 = f32[16,16,512]{2,1,0:T(8,128)S(1)} all-to-all(f32[16,16,512]{2,1,0:T(8,128)S(1)} %broadcast_in_dim.11), channel_id=1, replica_groups=mesh['far'=4,'near'=4,'core'=2,'x'=4,'y'=4] {'x','y'}, dimensions={0} | all-to-all | bytes 1048576 | tf_op jit(solution)/shard_map/all_to_all | solution.py:35
  154.3 1.0 broadcast_in_dim.12
  155.2 7.9 %all-to-all-start.4 = ((f32[16,16,896]{2,1,0:T(8,128)}), f32[16,16,896]{2,1,0:T(8,128)}, u32[]{:S(2)}, u32[]{:S(2)}) async-start(f32[16,16,896]{2,1,0:T(8,128)} %broadcast_in_dim.12), calls=%async_computation.4 | async-start | bytes 1835008 | tf_op jit(solution)/shard_map/all_to_all | solution.py:35
  163.1 13.8 %collective-permute-start.2 = (f32[256,512]{1,0:T(8,128)S(1)}, f32[256,512]{1,0:T(8,128)S(1)}, u32[]{:S(2)}, u32[]{:S(2)}) collective-permute-start(f32[256,512]{1,0:T(8,128)S(1)} %bitcast.35), channel_id=1, source_target_pairs={{0,16},{16,0},{1,17},{17,1},{2,18},{18,2},{3,19},{19,3},{4,20},{20... | collective-permute-start | bytes 1572872 | tf_op jit(solution)/shard_map/ppermute | solution.py:208
  176.9 1.5 fusion.10
  178.5 17.9 %inverse_factor.1 = f32[512,512]{1,0:T(8,128)S(1)} custom-call(s32[1]{0:T(128)} %bitcast.3.core_ref, f32[256,512]{1,0:T(8,128)S(1)} %bitcast.36, f32[256,512]{1,0:T(8,128)S(1)} %collective-permute-done.2.other_ref), custom_call_target="tpu_custom_call" | custom-call | flops 8000000000 | bytes 2097152 | tf_op jit(solution)/shard_map/inverse_factor/pallas_call | solution.py:135
  196.4 14.3 %collective-permute-start.3 = (f32[256,896]{1,0:T(8,128)}, f32[256,896]{1,0:T(8,128)S(1)}, u32[]{:S(2)}, u32[]{:S(2)}) collective-permute-start(f32[256,896]{1,0:T(8,128)} %bitcast.10), channel_id=1, source_target_pairs={{0,16},{16,0},{1,17},{17,1},{2,18},{18,2},{3,19},{19,3},{4,20},{20... | collective-permute-start | bytes 2752520 | tf_op jit(solution)/shard_map/ppermute | solution.py:209
  212.3 2.2 fusion.82
  214.5 1.2 multiply_reduce_fusion
  216.4 3.5 %all-to-all-start.5 = ((f32[16,4,128]{2,1,0:T(4,128)}), f32[16,4,128]{2,1,0:T(4,128)S(1)}, u32[]{:S(2)}, u32[]{:S(2)}) async-start(f32[16,4,128]{2,1,0:T(4,128)} %broadcast_in_dim.14), calls=%async_computation.5 | async-start | bytes 65536 | tf_op jit(solution)/shard_map/all_to_all | solution.py:35
  219.9 2.0 fusion
  221.9 4.4 %all-to-all-done.5 = f32[16,4,128]{2,1,0:T(4,128)S(1)} async-done(((f32[16,4,128]{2,1,0:T(4,128)}), f32[16,4,128]{2,1,0:T(4,128)S(1)}, u32[]{:S(2)}, u32[]{:S(2)}) %all-to-all-start.5) | async-done | bytes 32800 | tf_op jit(solution)/shard_map/all_to_all | solution.py:35
  226.3 2.9 %fusion.2 = bf16[256,896]{1,0:T(8,128)(2,1)} fusion(f32[512,896]{1,0:T(8,128)S(1)} %get-tuple-element.8, bf16[256,896]{1,0:T(8,128)(2,1)} %param.4, f32[256,512]{1,0:T(8,128)S(1)} %fusion.81, f32[512]{0:T(512)S(1)} %rsqrt_bitcast_fusion), kind=kOutput, calls=%fused_computation.12 | convolution fusion | flops 705691648 | bytes 3278848 | tf_op jit(solution)/shard_map/dot_general | solution.py:25
  (42 shorter events, 7.6 us)
Async XLA Ops:
  0.6 10.2 %copy-start.1 = (f32[16,896]{1,0:T(8,128)S(1)}, f32[16,896]{1,0:T(8,128)}, u32[]{:S(2)}) copy-start(f32[16,896]{1,0:T(8,128)} %param.7) | copy-start | bytes 172036
  2.0 38.9 %collective-permute-start = (f32[256,896]{1,0:T(8,128)S(1)}, f32[256,896]{1,0:T(8,128)S(1)}, u32[]{:S(2)}, u32[]{:S(2)}) collective-permute-start(f32[256,896]{1,0:T(8,128)S(1)} %convert_add_fusion), channel_id=1, source_target_pairs={{0,16},{16,0},{1,17},{17,1},{2,18},{18,2},{3,19},{19,3},{4,20},{20... | collective-permute-start | bytes 2752520 | tf_op jit(solution)/shard_map/ppermute | solution.py:180
  71.7 68.1 %all-to-all-start.2 = ((f32[16,16,896]{2,1,0:T(8,128)}), f32[16,16,896]{2,1,0:T(8,128)S(1)}, u32[]{:S(2)}, u32[]{:S(2)}) async-start(f32[16,16,896]{2,1,0:T(8,128)} %bitcast.40), calls=%async_computation.2 | async-start | bytes 1835008 | tf_op jit(solution)/shard_map/all_to_all | solution.py:35
  78.0 13.3 %collective-permute-start.1 = (f32[512,256]{1,0:T(8,128)S(1)}, f32[512,256]{1,0:T(8,128)S(1)}, u32[]{:S(2)}, u32[]{:S(2)}) collective-permute-start(f32[512,256]{1,0:T(8,128)S(1)} %bitcast.37), channel_id=1, source_target_pairs={{0,16},{16,0},{1,17},{17,1},{2,18},{18,2},{3,19},{19,3},{4,20},{20... | collective-permute-start | bytes 1572872 | tf_op jit(solution)/shard_map/ppermute | solution.py:185
  155.2 41.1 %all-to-all-start.4 = ((f32[16,16,896]{2,1,0:T(8,128)}), f32[16,16,896]{2,1,0:T(8,128)}, u32[]{:S(2)}, u32[]{:S(2)}) async-start(f32[16,16,896]{2,1,0:T(8,128)} %broadcast_in_dim.12), calls=%async_computation.4 | async-start | bytes 1835008 | tf_op jit(solution)/shard_map/all_to_all | solution.py:35
  163.1 15.3 %collective-permute-start.2 = (f32[256,512]{1,0:T(8,128)S(1)}, f32[256,512]{1,0:T(8,128)S(1)}, u32[]{:S(2)}, u32[]{:S(2)}) collective-permute-start(f32[256,512]{1,0:T(8,128)S(1)} %bitcast.35), channel_id=1, source_target_pairs={{0,16},{16,0},{1,17},{17,1},{2,18},{18,2},{3,19},{19,3},{4,20},{20... | collective-permute-start | bytes 1572872 | tf_op jit(solution)/shard_map/ppermute | solution.py:208
  196.4 15.3 %copy-start = (f32[256,512]{1,0:T(8,128)S(1)}, f32[256,512]{1,0:T(8,128)}, u32[]{:S(2)}) copy-start(f32[256,512]{1,0:T(8,128)} %fusion.10) | copy-start | bytes 1572868
  196.4 18.1 %collective-permute-start.3 = (f32[256,896]{1,0:T(8,128)}, f32[256,896]{1,0:T(8,128)S(1)}, u32[]{:S(2)}, u32[]{:S(2)}) collective-permute-start(f32[256,896]{1,0:T(8,128)} %bitcast.10), channel_id=1, source_target_pairs={{0,16},{16,0},{1,17},{17,1},{2,18},{18,2},{3,19},{19,3},{4,20},{20... | collective-permute-start | bytes 2752520 | tf_op jit(solution)/shard_map/ppermute | solution.py:209
  216.4 9.9 %all-to-all-start.5 = ((f32[16,4,128]{2,1,0:T(4,128)}), f32[16,4,128]{2,1,0:T(4,128)S(1)}, u32[]{:S(2)}, u32[]{:S(2)}) async-start(f32[16,4,128]{2,1,0:T(4,128)} %broadcast_in_dim.14), calls=%async_computation.5 | async-start | bytes 65536 | tf_op jit(solution)/shard_map/all_to_all | solution.py:35

commit v6 on v4

--- a/solution.py
+++ b/solution.py
@@ -46,6 +46,7 @@
 
 SUB = 8
 TILE = 128
+GROUP = 32
 
 
 def factor_step(work, wide, at, block):
@@ -75,7 +76,7 @@
     for i in range(SUB-1):
         out = jnp.where(sub==i, rows[i], out)
     work[at:at+SUB,:] = out
-    far = at+SUB*4
+    far = (at//GROUP+2)*GROUP
     ahead = None
     for nxt in range(at+SUB, min(far,TILE), SUB):
         block = work[nxt:nxt+SUB,:]
@@ -91,15 +92,25 @@
             ahead = total
         else:
             work[nxt:nxt+SUB,:] = total
+    return ahead
+
+
+def group_step(work, at):
+    far = at+2*GROUP
     if far < TILE:
-        prod = dot(out,out,0,0)
+        rows = work[at:at+GROUP,:]
+        lane = lax.broadcasted_iota(jnp.int32,(GROUP,TILE),1)-at
+        sub = lax.broadcasted_iota(jnp.int32,(GROUP,TILE),0)
+        clean = jnp.where((lane>=sub//SUB*SUB+SUB)&(lane<GROUP),0.0,rows)
+        prod = dot(rows,clean,0,0)
         rest = work[far:,:]
         lanes = lax.broadcasted_iota(jnp.int32,rest.shape,1)
-        work[far:,:] = jnp.where((lanes>=at)&(lanes<at+SUB),0.0,rest) - prod[far:,:]
-    return ahead
-
-
-def inverse_factor_kernel(core_ref, own_ref, other_ref, out_ref, work, wide, *, owned):
+        work[far:,:] = jnp.where((lanes>=at)&(lanes<at+GROUP),0.0,rest) - prod[far:,:]
+
+
+def inverse_factor_kernel(
+    core_ref, own_ref, other_ref, out_ref, zero_ref, work, wide, *, owned
+):
     n = out_ref.shape[0]
     tiles = n//TILE
     core = core_ref[0]
@@ -114,6 +125,8 @@
         block = work[0:SUB,:]
         for k in range(TILE//SUB):
             block = factor_step(work, wide.at[k%2], k*SUB, block)
+            if (k+1)*SUB%GROUP==0:
+                group_step(work,(k+1)*SUB-GROUP)
         r = lax.broadcasted_iota(jnp.int32,(TILE,TILE),0); c = lax.broadcasted_iota(jnp.int32,(TILE,TILE),1)
         inverse = jnp.where(r>=c, work[...], 0.0)
         out_ref[pl.ds(at,TILE),pl.ds(at,TILE)] = jnp.where(r==c,1.0,0.0)
@@ -128,15 +141,19 @@
     lax.fori_loop(0,tiles,panel,0)
     for q in range(tiles-1):
         out_ref[q*TILE:(q+1)*TILE,(q+1)*TILE:] = jnp.zeros((TILE,n-(q+1)*TILE),jnp.float32)
-
-def inverse_factor(core, own, other, owned):
+    zero_ref[...] = jnp.zeros_like(zero_ref)
+
+def inverse_factor(core, own, other, owned, columns):
     size = own.shape[1]
     whole = pl.BlockSpec(memory_space=pltpu.VMEM)
     return pl.pallas_call(
         functools.partial(inverse_factor_kernel, owned=owned),
-        out_shape=jax.ShapeDtypeStruct((size, size), jnp.float32),
+        out_shape=(
+            jax.ShapeDtypeStruct((size, size), jnp.float32),
+            jax.ShapeDtypeStruct((owned, columns), jnp.float32),
+        ),
         in_specs=[pl.BlockSpec(memory_space=pltpu.SMEM), whole, whole],
-        out_specs=whole,
+        out_specs=(whole, whole),
         scratch_shapes=[
             pltpu.VMEM((TILE, TILE), jnp.float32),
             pltpu.VMEM((2, SUB, SUB, TILE), jnp.float32),
@@ -206,9 +223,11 @@
     gram = total(spread(gram, "far", far), far)
     gram = total(spread(gram, "near", near), near)
     gram = spread(gram, COLUMN_BLOCKS, blocks)
-    inverse = inverse_factor(core, gram, lax.ppermute(gram, "core", SWAP), owned)
-
-    moved = lax.all_gather(moved + inverse[0, rank - 1], DEPTH, axis=0, tiled=True)
+    inverse, zero = inverse_factor(
+        core, gram, lax.ppermute(gram, "core", SWAP), owned, columns
+    )
+
+    moved = lax.all_gather(moved + zero, DEPTH, axis=0, tiled=True)
     handed = lax.ppermute(moved, "core", SWAP)
     joined = by_core(core, projected[:rows], others[:rows], 1)
     own_projected = dot(joined, order, 1, 0)

time: 224 us -> 223 us (level)
  blocking collectives: 100 us -> 111 us
  waiting for transfers between devices: 22.1 us -> 14.8 us
  Pallas kernels: 17.9 us -> 15.6 us
    all_to_all x3 -> x4, blocking collectives: 44.7 us -> 56.3 us  [exchange(): return lax.all_to_all(array, axes, 0, 0, tiled=True)]
    all_to_all x3 -> x2, waiting for transfers between devices: 22.1 us -> 13.3 us  [exchange(): return lax.all_to_all(array, axes, 0, 0, tiled=True)]
    pallas_call x1, Pallas kernels: 17.9 us -> 15.6 us  [inverse_factor(): pl.pallas_call(functools.partial(inverse_factor_kernel, owned=owned), out...]
    all_to_all x3 -> x2, starting transfers between devices: 10.6 us -> 8.42 us  [exchange(): return lax.all_to_all(array, axes, 0, 0, tiled=True)]
  transfers between devices with their start and end apart: 8 -> 7, of which waited for: 3 -> 3; matrix products, arithmetic and copies ran while one was open for 6% -> 5% of each run, Pallas kernels for 8% -> 7%
where the time goes in v6:
time: 223 us; the launch traced here: 222 us
  blocking collectives  111 us (50%)
  starting transfers between devices  44 us (20%)
  matrix products  17.3 us (8%)
  Pallas kernels  15.6 us (7%)
  waiting for transfers between devices  14.8 us (7%)
  between operations  14.3 us (6%)
  other arithmetic  3.09 us (1%)
  local copies, waits for them, and re-layouts  2.42 us (1%)
    all_to_all x4, blocking collectives, exchange(): return lax.all_to_all(array, axes, 0, 0, tiled=True)  56.3 us
    all_gather x1, blocking collectives, on_device(): basis = lax.all_gather(warm_basis, DEPTH, axis=0, tiled=True)  29 us
    all_gather x1, blocking collectives, on_device(): moved = lax.all_gather(moved + zero, DEPTH, axis=0, tiled=True)  25.6 us
    dot_general x15, matrix products, dot(): lax.dot_general(left_side, right_side, (((contract_left,), (contract_righ...  17.3 us
    pallas_call x1, Pallas kernels, inverse_factor(): pl.pallas_call(functools.partial(inverse_factor_kernel, owned=owned), out...  15.6 us
    all_to_all x2, waiting for transfers between devices, exchange(): return lax.all_to_all(array, axes, 0, 0, tiled=True)  13.3 us
    ppermute x1, starting transfers between devices, on_device(): others = lax.ppermute(projected, 'core', SWAP)  10.9 us
    ppermute x1, starting transfers between devices, on_device(): handed = lax.ppermute(moved, 'core', SWAP)  9.37 us
  transfers between devices with their start and end apart: 7, of which 3 were waited for; matrix products, arithmetic and copies ran while one was open for 5% of the time, Pallas kernels for 7%

profile of v6, /device:TPU:1, one launch (start us, length us, event | category | flops | bytes accessed | tf_op | source)
XLA Modules:
  0.0 222.4 jit_solution(2733860905538014240)
XLA Ops:
  7.2 1.4 convert_add_fusion
  8.6 8.8 %collective-permute-start = (f32[256,896]{1,0:T(8,128)S(1)}, f32[256,896]{1,0:T(8,128)S(1)}, u32[]{:S(2)}, u32[]{:S(2)}) collective-permute-start(f32[256,896]{1,0:T(8,128)S(1)} %convert_add_fusion), channel_id=1, source_target_pairs={{0,16},{16,0},{1,17},{17,1},{2,18},{18,2},{3,19},{19,3},{4,20},{20... | collective-permute-start | bytes 2752520 | tf_op jit(solution)/shard_map/ppermute | solution.py:198
  17.4 29.0 %all_gather.6 = f32[256,896]{1,0:T(8,128)S(1)} all-gather(f32[16,896]{1,0:T(8,128)S(1)} %copy-done), channel_id=1, replica_groups=mesh['far'=4,'near'=4,'core'=2,'x'=4,'y'=4] {'far','near'}, dimensions={0}, use_global_device_ids=true | all-gather | bytes 974848 | tf_op jit(solution)/shard_map/all_gather | solution.py:199
  47.4 1.0 fusion.79
  48.5 15.5 %all_to_all.44 = f32[16,32,256]{2,1,0:T(8,128)S(1)} all-to-all(f32[16,32,256]{2,1,0:T(8,128)S(1)} %bitcast.34), channel_id=1, replica_groups=mesh['far'=4,'near'=4,'core'=2,'x'=4,'y'=4] {'x','y'}, dimensions={0} | all-to-all | bytes 1048576 | tf_op jit(solution)/shard_map/all_to_all | solution.py:35
  64.9 3.6 %all-to-all-start.1 = ((f32[16,32,256]{2,1,0:T(8,128)}), f32[16,32,256]{2,1,0:T(8,128)S(1)}, u32[]{:S(2)}, u32[]{:S(2)}) async-start(f32[16,32,256]{2,1,0:T(8,128)} %broadcast_in_dim.12), calls=%async_computation.1 | async-start | bytes 1048576 | tf_op jit(solution)/shard_map/all_to_all | solution.py:35
  68.6 8.8 %all-to-all-done.1 = f32[16,32,256]{2,1,0:T(8,128)S(1)} async-done(((f32[16,32,256]{2,1,0:T(8,128)}), f32[16,32,256]{2,1,0:T(8,128)S(1)}, u32[]{:S(2)}, u32[]{:S(2)}) %all-to-all-start.1) | async-done | bytes 524320 | tf_op jit(solution)/shard_map/all_to_all | solution.py:35
  77.4 10.9 %collective-permute-start.1 = (f32[512,256]{1,0:T(8,128)S(1)}, f32[512,256]{1,0:T(8,128)S(1)}, u32[]{:S(2)}, u32[]{:S(2)}) collective-permute-start(f32[512,256]{1,0:T(8,128)S(1)} %bitcast.31), channel_id=1, source_target_pairs={{0,16},{16,0},{1,17},{17,1},{2,18},{18,2},{3,19},{19,3},{4,20},{20... | collective-permute-start | bytes 1572872 | tf_op jit(solution)/shard_map/ppermute | solution.py:203
  89.0 1.6 fusion.81
  90.6 1.6 convolution_add_fusion.1
  94.0 21.3 %all_to_all.45 = f32[4,16,512]{2,1,0:T(8,128)S(1)} all-to-all(f32[4,16,512]{2,1,0:T(8,128)S(1)} %broadcast_in_dim.13), channel_id=1, replica_groups=mesh['far'=4,'near'=4,'core'=2,'x'=4,'y'=4] {'far'}, dimensions={0} | all-to-all | bytes 262144 | tf_op jit(solution)/shard_map/all_to_all | solution.py:35
  115.3 7.9 %all_to_all.46 = f32[4,16,512]{2,1,0:T(8,128)S(1)} all-to-all(f32[4,16,512]{2,1,0:T(8,128)S(1)} %broadcast_in_dim.14), channel_id=1, replica_groups=mesh['far'=4,'near'=4,'core'=2,'x'=4,'y'=4] {'near'}, dimensions={0} | all-to-all | bytes 262144 | tf_op jit(solution)/shard_map/all_to_all | solution.py:35
  123.4 11.6 %all_to_all.47 = f32[16,16,512]{2,1,0:T(8,128)S(1)} all-to-all(f32[16,16,512]{2,1,0:T(8,128)S(1)} %broadcast_in_dim.15), channel_id=1, replica_groups=mesh['far'=4,'near'=4,'core'=2,'x'=4,'y'=4] {'x','y'}, dimensions={0} | all-to-all | bytes 1048576 | tf_op jit(solution)/shard_map/all_to_all | solution.py:35
  134.9 6.5 %collective-permute-start.2 = (f32[256,512]{1,0:T(8,128)S(1)}, f32[256,512]{1,0:T(8,128)S(1)}, u32[]{:S(2)}, u32[]{:S(2)}) collective-permute-start(f32[256,512]{1,0:T(8,128)S(1)} %bitcast.29), channel_id=1, source_target_pairs={{0,16},{16,0},{1,17},{17,1},{2,18},{18,2},{3,19},{19,3},{4,20},{20... | collective-permute-start | bytes 1572872 | tf_op jit(solution)/shard_map/ppermute | solution.py:227
  141.5 1.5 collective-permute-done.2.other_ref
  142.9 15.6 %inverse_factor.1 = (f32[512,512]{1,0:T(8,128)S(1)}, f32[16,896]{1,0:T(8,128)S(1)}) custom-call(s32[1]{0:T(128)} %bitcast.3.core_ref, f32[256,512]{1,0:T(8,128)S(1)} %bitcast.30, f32[256,512]{1,0:T(8,128)S(1)} %collective-permute-done.2.other_ref), custom_call_target="tpu_custom_call" | custom-call | flops 200000000 | bytes 2097152 | tf_op jit(solution)/shard_map/inverse_factor/pallas_call | solution.py:149
  159.4 25.6 %all_gather.7 = f32[256,896]{1,0:T(8,128)S(1)} all-gather(f32[16,896]{1,0:T(8,128)S(1)} %add.113), channel_id=1, replica_groups=mesh['far'=4,'near'=4,'core'=2,'x'=4,'y'=4] {'far','near'}, dimensions={0}, use_global_device_ids=true | all-gather | bytes 974848 | tf_op jit(solution)/shard_map/all_gather | solution.py:230
  185.0 9.4 %collective-permute-start.3 = (f32[256,896]{1,0:T(8,128)S(1)}, f32[256,896]{1,0:T(8,128)S(1)}, u32[]{:S(2)}, u32[]{:S(2)}) collective-permute-start(f32[256,896]{1,0:T(8,128)S(1)} %all_gather.7), channel_id=1, source_target_pairs={{0,16},{16,0},{1,17},{17,1},{2,18},{18,2},{3,19},{19,3},{4,20},{20... | collective-permute-start | bytes 2752520 | tf_op jit(solution)/shard_map/ppermute | solution.py:231
  194.3 1.7 fusion.10
  198.7 1.2 multiply_reduce_fusion
  200.5 4.8 %all-to-all-start.5 = ((f32[16,4,128]{2,1,0:T(4,128)}), f32[16,4,128]{2,1,0:T(4,128)S(1)}, u32[]{:S(2)}, u32[]{:S(2)}) async-start(f32[16,4,128]{2,1,0:T(4,128)} %broadcast_in_dim.17), calls=%async_computation.6 | async-start | bytes 65536 | tf_op jit(solution)/shard_map/all_to_all | solution.py:35
  205.4 2.0 fusion
  207.4 4.5 %all-to-all-done.5 = f32[16,4,128]{2,1,0:T(4,128)S(1)} async-done(((f32[16,4,128]{2,1,0:T(4,128)}), f32[16,4,128]{2,1,0:T(4,128)S(1)}, u32[]{:S(2)}, u32[]{:S(2)}) %all-to-all-start.5) | async-done | bytes 32800 | tf_op jit(solution)/shard_map/all_to_all | solution.py:35
  211.9 2.8 %fusion.2 = bf16[256,896]{1,0:T(8,128)(2,1)} fusion(f32[512,896]{1,0:T(8,128)S(1)} %get-tuple-element.12, bf16[256,896]{1,0:T(8,128)(2,1)} %param.4, f32[256,512]{1,0:T(8,128)S(1)} %fusion.80, f32[512]{0:T(512)S(1)} %rsqrt_bitcast_fusion), kind=kOutput, calls=%fused_computation.12 | convolution fusion | flops 705691648 | bytes 3278848 | tf_op jit(solution)/shard_map/dot_general | solution.py:25
  (40 shorter events, 9.6 us)
Async XLA Ops:
  7.2 10.2 %copy-start = (f32[16,896]{1,0:T(8,128)S(1)}, f32[16,896]{1,0:T(8,128)}, u32[]{:S(2)}) copy-start(f32[16,896]{1,0:T(8,128)} %param.7) | copy-start | bytes 172036
  8.6 38.9 %collective-permute-start = (f32[256,896]{1,0:T(8,128)S(1)}, f32[256,896]{1,0:T(8,128)S(1)}, u32[]{:S(2)}, u32[]{:S(2)}) collective-permute-start(f32[256,896]{1,0:T(8,128)S(1)} %convert_add_fusion), channel_id=1, source_target_pairs={{0,16},{16,0},{1,17},{17,1},{2,18},{18,2},{3,19},{19,3},{4,20},{20... | collective-permute-start | bytes 2752520 | tf_op jit(solution)/shard_map/ppermute | solution.py:198
  64.9 12.5 %all-to-all-start.1 = ((f32[16,32,256]{2,1,0:T(8,128)}), f32[16,32,256]{2,1,0:T(8,128)S(1)}, u32[]{:S(2)}, u32[]{:S(2)}) async-start(f32[16,32,256]{2,1,0:T(8,128)} %broadcast_in_dim.12), calls=%async_computation.1 | async-start | bytes 1048576 | tf_op jit(solution)/shard_map/all_to_all | solution.py:35
  68.5 90.1 %reduce-scatter.2.cloned.1.call-start = ((), (), s32[]{:S(2)}) async-start(), calls=%async_computation.7 | async-start | bytes 974848 | tf_op jit(solution)/shard_map/reduce_scatter | solution.py:209
  77.4 15.5 %collective-permute-start.1 = (f32[512,256]{1,0:T(8,128)S(1)}, f32[512,256]{1,0:T(8,128)S(1)}, u32[]{:S(2)}, u32[]{:S(2)}) collective-permute-start(f32[512,256]{1,0:T(8,128)S(1)} %bitcast.31), channel_id=1, source_target_pairs={{0,16},{16,0},{1,17},{17,1},{2,18},{18,2},{3,19},{19,3},{4,20},{20... | collective-permute-start | bytes 1572872 | tf_op jit(solution)/shard_map/ppermute | solution.py:203
  134.9 8.0 %collective-permute-start.2 = (f32[256,512]{1,0:T(8,128)S(1)}, f32[256,512]{1,0:T(8,128)S(1)}, u32[]{:S(2)}, u32[]{:S(2)}) collective-permute-start(f32[256,512]{1,0:T(8,128)S(1)} %bitcast.29), channel_id=1, source_target_pairs={{0,16},{16,0},{1,17},{17,1},{2,18},{18,2},{3,19},{19,3},{4,20},{20... | collective-permute-start | bytes 1572872 | tf_op jit(solution)/shard_map/ppermute | solution.py:227
  185.0 12.7 %collective-permute-start.3 = (f32[256,896]{1,0:T(8,128)S(1)}, f32[256,896]{1,0:T(8,128)S(1)}, u32[]{:S(2)}, u32[]{:S(2)}) collective-permute-start(f32[256,896]{1,0:T(8,128)S(1)} %all_gather.7), channel_id=1, source_target_pairs={{0,16},{16,0},{1,17},{17,1},{2,18},{18,2},{3,19},{19,3},{4,20},{20... | collective-permute-start | bytes 2752520 | tf_op jit(solution)/shard_map/ppermute | solution.py:231
  200.5 11.3 %all-to-all-start.5 = ((f32[16,4,128]{2,1,0:T(4,128)}), f32[16,4,128]{2,1,0:T(4,128)S(1)}, u32[]{:S(2)}, u32[]{:S(2)}) async-start(f32[16,4,128]{2,1,0:T(4,128)} %broadcast_in_dim.17), calls=%async_computation.6 | async-start | bytes 65536 | tf_op jit(solution)/shard_map/all_to_all | solution.py:35
Sparse Core Ops, SparseCore 0:
  92.3 55.3 reduce-scatter.1

commit v7 on v6

--- a/solution.py
+++ b/solution.py
@@ -229,12 +229,12 @@
 
     moved = lax.all_gather(moved + zero, DEPTH, axis=0, tiled=True)
     handed = lax.ppermute(moved, "core", SWAP)
-    joined = by_core(core, projected[:rows], others[:rows], 1)
-    own_projected = dot(joined, order, 1, 0)
-    orthonormal = dot(own_projected, inverse, 1, 1, HIGH)
-    coefficients = dot(
-        dot(inverse, one_side(rank, owned, core), 1, 0, HIGH), moved, 1, 0, HIGH
-    ) + dot(dot(inverse, one_side(rank, owned, 1 - core), 1, 0, HIGH), handed, 1, 0, HIGH)
+    inverse_own = dot(inverse, one_side(rank, owned, core), 1, 0, HIGH)
+    inverse_other = dot(inverse, one_side(rank, owned, 1 - core), 1, 0, HIGH)
+    orthonormal = dot(projected[:rows], inverse_own, 1, 1, HIGH) + dot(
+        others[:rows], inverse_other, 1, 1, HIGH
+    )
+    coefficients = dot(inverse_own, moved, 1, 0, HIGH) + dot(inverse_other, handed, 1, 0, HIGH)
     energy = jnp.sum(coefficients * coefficients, axis=1).reshape(rank // 128, 128)
     energy = total(spread(energy, COLUMN_BLOCKS, blocks), blocks).reshape(rank)
     scale = lax.rsqrt(energy / FF + epsilon)

time: 223 us -> 220 us (0.987)
  matrix products: 17.3 us -> 14.8 us
    dot_general x15, matrix products: 17.3 us -> 14.8 us  [dot(): lax.dot_general(left_side, right_side, (((contract_left,), (contract_righ...]
  transfers between devices with their start and end apart: 7 -> 7, of which waited for: 3 -> 3; matrix products, arithmetic and copies ran while one was open for 5% -> 4% of each run, Pallas kernels for 7% -> 7%
where the time goes in v7:
time: 220 us; the launch traced here: 219 us
  blocking collectives  111 us (50%)
  starting transfers between devices  43.4 us (20%)
  Pallas kernels  15.6 us (7%)
  matrix products  14.8 us (7%)
  waiting for transfers between devices  14.8 us (7%)
  between operations  14.3 us (6%)
  other arithmetic  3.09 us (1%)
    all_to_all x4, blocking collectives, exchange(): return lax.all_to_all(array, axes, 0, 0, tiled=True)  56.3 us
    all_gather x1, blocking collectives, on_device(): basis = lax.all_gather(warm_basis, DEPTH, axis=0, tiled=True)  29 us
    all_gather x1, blocking collectives, on_device(): moved = lax.all_gather(moved + zero, DEPTH, axis=0, tiled=True)  26.1 us
    pallas_call x1, Pallas kernels, inverse_factor(): pl.pallas_call(functools.partial(inverse_factor_kernel, owned=owned), out...  15.6 us
    dot_general x15, matrix products, dot(): lax.dot_general(left_side, right_side, (((contract_left,), (contract_righ...  14.8 us
    all_to_all x2, waiting for transfers between devices, exchange(): return lax.all_to_all(array, axes, 0, 0, tiled=True)  13.3 us
    ppermute x1, starting transfers between devices, on_device(): others = lax.ppermute(projected, 'core', SWAP)  10.9 us
    ppermute x1, starting transfers between devices, on_device(): handed = lax.ppermute(moved, 'core', SWAP)  8.8 us
  transfers between devices with their start and end apart: 7, of which 3 were waited for; matrix products, arithmetic and copies ran while one was open for 4% of the time, Pallas kernels for 7%

profile of v7, /device:TPU:1, one launch (start us, length us, event | category | flops | bytes accessed | tf_op | source)
XLA Modules:
  0.0 219.4 jit_solution(10088386228791679851)
XLA Ops:
  7.2 1.4 convert_add_fusion
  8.6 8.8 %collective-permute-start = (f32[256,896]{1,0:T(8,128)S(1)}, f32[256,896]{1,0:T(8,128)S(1)}, u32[]{:S(2)}, u32[]{:S(2)}) collective-permute-start(f32[256,896]{1,0:T(8,128)S(1)} %convert_add_fusion), channel_id=1, source_target_pairs={{0,16},{16,0},{1,17},{17,1},{2,18},{18,2},{3,19},{19,3},{4,20},{20... | collective-permute-start | bytes 2752520 | tf_op jit(solution)/shard_map/ppermute | solution.py:198
  17.4 29.0 %all_gather.6 = f32[256,896]{1,0:T(8,128)S(1)} all-gather(f32[16,896]{1,0:T(8,128)S(1)} %copy-done.2), channel_id=1, replica_groups=mesh['far'=4,'near'=4,'core'=2,'x'=4,'y'=4] {'far','near'}, dimensions={0}, use_global_device_ids=true | all-gather | bytes 974848 | tf_op jit(solution)/shard_map/all_gather | solution.py:199
  46.4 1.0 fusion.89
  47.4 1.0 fusion.90
  48.5 15.5 %all_to_all.44 = f32[16,32,256]{2,1,0:T(8,128)S(1)} all-to-all(f32[16,32,256]{2,1,0:T(8,128)S(1)} %bitcast.37), channel_id=1, replica_groups=mesh['far'=4,'near'=4,'core'=2,'x'=4,'y'=4] {'x','y'}, dimensions={0} | all-to-all | bytes 1048576 | tf_op jit(solution)/shard_map/all_to_all | solution.py:35
  64.9 3.6 %all-to-all-start.1 = ((f32[16,32,256]{2,1,0:T(8,128)}), f32[16,32,256]{2,1,0:T(8,128)S(1)}, u32[]{:S(2)}, u32[]{:S(2)}) async-start(f32[16,32,256]{2,1,0:T(8,128)} %broadcast_in_dim.12), calls=%async_computation.1 | async-start | bytes 1048576 | tf_op jit(solution)/shard_map/all_to_all | solution.py:35
  68.6 8.8 %all-to-all-done.1 = f32[16,32,256]{2,1,0:T(8,128)S(1)} async-done(((f32[16,32,256]{2,1,0:T(8,128)}), f32[16,32,256]{2,1,0:T(8,128)S(1)}, u32[]{:S(2)}, u32[]{:S(2)}) %all-to-all-start.1) | async-done | bytes 524320 | tf_op jit(solution)/shard_map/all_to_all | solution.py:35
  77.4 10.9 %collective-permute-start.1 = (f32[512,256]{1,0:T(8,128)S(1)}, f32[512,256]{1,0:T(8,128)S(1)}, u32[]{:S(2)}, u32[]{:S(2)}) collective-permute-start(f32[512,256]{1,0:T(8,128)S(1)} %bitcast.32), channel_id=1, source_target_pairs={{0,16},{16,0},{1,17},{17,1},{2,18},{18,2},{3,19},{19,3},{4,20},{20... | collective-permute-start | bytes 1572872 | tf_op jit(solution)/shard_map/ppermute | solution.py:203
  89.0 1.5 convolution_add_fusion.1
  92.4 21.3 %all_to_all.45 = f32[4,16,512]{2,1,0:T(8,128)S(1)} all-to-all(f32[4,16,512]{2,1,0:T(8,128)S(1)} %broadcast_in_dim.13), channel_id=1, replica_groups=mesh['far'=4,'near'=4,'core'=2,'x'=4,'y'=4] {'far'}, dimensions={0} | all-to-all | bytes 262144 | tf_op jit(solution)/shard_map/all_to_all | solution.py:35
  113.7 8.0 %all_to_all.46 = f32[4,16,512]{2,1,0:T(8,128)S(1)} all-to-all(f32[4,16,512]{2,1,0:T(8,128)S(1)} %broadcast_in_dim.14), channel_id=1, replica_groups=mesh['far'=4,'near'=4,'core'=2,'x'=4,'y'=4] {'near'}, dimensions={0} | all-to-all | bytes 262144 | tf_op jit(solution)/shard_map/all_to_all | solution.py:35
  121.8 11.6 %all_to_all.47 = f32[16,16,512]{2,1,0:T(8,128)S(1)} all-to-all(f32[16,16,512]{2,1,0:T(8,128)S(1)} %broadcast_in_dim.15), channel_id=1, replica_groups=mesh['far'=4,'near'=4,'core'=2,'x'=4,'y'=4] {'x','y'}, dimensions={0} | all-to-all | bytes 1048576 | tf_op jit(solution)/shard_map/all_to_all | solution.py:35
  133.3 6.4 %collective-permute-start.2 = (f32[256,512]{1,0:T(8,128)S(1)}, f32[256,512]{1,0:T(8,128)S(1)}, u32[]{:S(2)}, u32[]{:S(2)}) collective-permute-start(f32[256,512]{1,0:T(8,128)S(1)} %bitcast.30), channel_id=1, source_target_pairs={{0,16},{16,0},{1,17},{17,1},{2,18},{18,2},{3,19},{19,3},{4,20},{20... | collective-permute-start | bytes 1572872 | tf_op jit(solution)/shard_map/ppermute | solution.py:227
  139.8 1.5 collective-permute-done.2.other_ref
  141.3 15.6 %inverse_factor.1 = (f32[512,512]{1,0:T(8,128)S(1)}, f32[16,896]{1,0:T(8,128)S(1)}) custom-call(s32[1]{0:T(128)} %bitcast.2.core_ref, f32[256,512]{1,0:T(8,128)S(1)} %bitcast.31, f32[256,512]{1,0:T(8,128)S(1)} %collective-permute-done.2.other_ref), custom_call_target="tpu_custom_call" | custom-call | flops 200000000 | bytes 2097152 | tf_op jit(solution)/shard_map/inverse_factor/pallas_call | solution.py:149
  157.7 26.1 %all_gather.7 = f32[256,896]{1,0:T(8,128)S(1)} all-gather(f32[16,896]{1,0:T(8,128)S(1)} %add.112), channel_id=1, replica_groups=mesh['far'=4,'near'=4,'core'=2,'x'=4,'y'=4] {'far','near'}, dimensions={0}, use_global_device_ids=true | all-gather | bytes 974848 | tf_op jit(solution)/shard_map/all_gather | solution.py:230
  183.9 8.8 %collective-permute-start.3 = (f32[256,896]{1,0:T(8,128)S(1)}, f32[256,896]{1,0:T(8,128)S(1)}, u32[]{:S(2)}, u32[]{:S(2)}) collective-permute-start(f32[256,896]{1,0:T(8,128)S(1)} %all_gather.7), channel_id=1, source_target_pairs={{0,16},{16,0},{1,17},{17,1},{2,18},{18,2},{3,19},{19,3},{4,20},{20... | collective-permute-start | bytes 2752520 | tf_op jit(solution)/shard_map/ppermute | solution.py:231
  194.6 1.0 fusion.93
  195.6 1.2 multiply_reduce_fusion
  197.5 5.0 %all-to-all-start.5 = ((f32[16,4,128]{2,1,0:T(4,128)}), f32[16,4,128]{2,1,0:T(4,128)S(1)}, u32[]{:S(2)}, u32[]{:S(2)}) async-start(f32[16,4,128]{2,1,0:T(4,128)} %broadcast_in_dim.17), calls=%async_computation.6 | async-start | bytes 65536 | tf_op jit(solution)/shard_map/all_to_all | solution.py:35
  202.4 2.0 fusion
  204.4 4.5 %all-to-all-done.5 = f32[16,4,128]{2,1,0:T(4,128)S(1)} async-done(((f32[16,4,128]{2,1,0:T(4,128)}), f32[16,4,128]{2,1,0:T(4,128)S(1)}, u32[]{:S(2)}, u32[]{:S(2)}) %all-to-all-start.5) | async-done | bytes 32800 | tf_op jit(solution)/shard_map/all_to_all | solution.py:35
  209.0 2.8 %fusion.2 = bf16[256,896]{1,0:T(8,128)(2,1)} fusion(f32[512,896]{1,0:T(8,128)S(1)} %get-tuple-element.12, bf16[256,896]{1,0:T(8,128)(2,1)} %param.4, f32[256,512]{1,0:T(8,128)S(1)} %convolution_add_fusion.2, f32[512]{0:T(512)S(1)} %rsqrt_bitcast_fusion), kind=kOutput, calls=%fused_computation.12 | convolution fusion | flops 705691648 | bytes 3278848 | tf_op jit(solution)/shard_map/dot_general | solution.py:25
  (44 shorter events, 7.8 us)
Async XLA Ops:
  7.2 10.2 %copy-start.2 = (f32[16,896]{1,0:T(8,128)S(1)}, f32[16,896]{1,0:T(8,128)}, u32[]{:S(2)}) copy-start(f32[16,896]{1,0:T(8,128)} %param.7) | copy-start | bytes 172036
  8.6 38.9 %collective-permute-start = (f32[256,896]{1,0:T(8,128)S(1)}, f32[256,896]{1,0:T(8,128)S(1)}, u32[]{:S(2)}, u32[]{:S(2)}) collective-permute-start(f32[256,896]{1,0:T(8,128)S(1)} %convert_add_fusion), channel_id=1, source_target_pairs={{0,16},{16,0},{1,17},{17,1},{2,18},{18,2},{3,19},{19,3},{4,20},{20... | collective-permute-start | bytes 2752520 | tf_op jit(solution)/shard_map/ppermute | solution.py:198
  64.9 12.5 %all-to-all-start.1 = ((f32[16,32,256]{2,1,0:T(8,128)}), f32[16,32,256]{2,1,0:T(8,128)S(1)}, u32[]{:S(2)}, u32[]{:S(2)}) async-start(f32[16,32,256]{2,1,0:T(8,128)} %broadcast_in_dim.12), calls=%async_computation.1 | async-start | bytes 1048576 | tf_op jit(solution)/shard_map/all_to_all | solution.py:35
  68.5 88.4 %reduce-scatter.2.cloned.1.call-start = ((), (), s32[]{:S(2)}) async-start(), calls=%async_computation.7 | async-start | bytes 974848 | tf_op jit(solution)/shard_map/reduce_scatter | solution.py:209
  77.4 13.8 %collective-permute-start.1 = (f32[512,256]{1,0:T(8,128)S(1)}, f32[512,256]{1,0:T(8,128)S(1)}, u32[]{:S(2)}, u32[]{:S(2)}) collective-permute-start(f32[512,256]{1,0:T(8,128)S(1)} %bitcast.32), channel_id=1, source_target_pairs={{0,16},{16,0},{1,17},{17,1},{2,18},{18,2},{3,19},{19,3},{4,20},{20... | collective-permute-start | bytes 1572872 | tf_op jit(solution)/shard_map/ppermute | solution.py:203
  91.2 1.2 copy-start
  133.3 7.9 %collective-permute-start.2 = (f32[256,512]{1,0:T(8,128)S(1)}, f32[256,512]{1,0:T(8,128)S(1)}, u32[]{:S(2)}, u32[]{:S(2)}) collective-permute-start(f32[256,512]{1,0:T(8,128)S(1)} %bitcast.30), channel_id=1, source_target_pairs={{0,16},{16,0},{1,17},{17,1},{2,18},{18,2},{3,19},{19,3},{4,20},{20... | collective-permute-start | bytes 1572872 | tf_op jit(solution)/shard_map/ppermute | solution.py:227
  183.9 10.8 %collective-permute-start.3 = (f32[256,896]{1,0:T(8,128)S(1)}, f32[256,896]{1,0:T(8,128)S(1)}, u32[]{:S(2)}, u32[]{:S(2)}) collective-permute-start(f32[256,896]{1,0:T(8,128)S(1)} %all_gather.7), channel_id=1, source_target_pairs={{0,16},{16,0},{1,17},{17,1},{2,18},{18,2},{3,19},{19,3},{4,20},{20... | collective-permute-start | bytes 2752520 | tf_op jit(solution)/shard_map/ppermute | solution.py:231
  193.1 1.0 copy-start.1
  197.5 11.4 %all-to-all-start.5 = ((f32[16,4,128]{2,1,0:T(4,128)}), f32[16,4,128]{2,1,0:T(4,128)S(1)}, u32[]{:S(2)}, u32[]{:S(2)}) async-start(f32[16,4,128]{2,1,0:T(4,128)} %broadcast_in_dim.17), calls=%async_computation.6 | async-start | bytes 65536 | tf_op jit(solution)/shard_map/all_to_all | solution.py:35
Sparse Core Ops, SparseCore 0:
  90.7 55.0 reduce-scatter.1

commit v8 on v7

--- a/solution.py
+++ b/solution.py
@@ -183,6 +183,45 @@
     return (ranks == source).astype(jnp.float32)
 
 
+def finish_kernel(
+    first_ref, energy_ref, orthonormal_ref, coefficients_ref, weights_ref, out_ref, basis_ref
+):
+    owned = basis_ref.shape[0]
+    energy = jnp.sum(energy_ref[...], axis=0)
+    scale = lax.rsqrt(energy / FF + epsilon)
+    scale = jnp.concatenate([scale[i : i + 1] for i in range(scale.shape[0])], axis=1)
+    coefficients = coefficients_ref[...]
+    row = lax.broadcasted_iota(jnp.int32, (owned, scale.shape[1]), 0) + first_ref[0]
+    column = lax.broadcasted_iota(jnp.int32, (owned, scale.shape[1]), 1)
+    own = jnp.sum(jnp.where(row == column, scale, 0.0), axis=1, keepdims=True)
+    basis_ref[...] = coefficients_ref[pl.ds(pl.multiple_of(first_ref[0], owned), owned), :] * own
+    update = dot(orthonormal_ref[...] * scale, coefficients, 1, 0, HIGH)
+    out_ref[...] = (
+        weights_ref[...].astype(jnp.float32) - step_size * math.sqrt(D / FF) * update
+    ).astype(jnp.bfloat16)
+
+
+def finish(first, energy, orthonormal, coefficients, weights, owned):
+    whole = pl.BlockSpec(memory_space=pltpu.VMEM)
+    rows, columns = weights.shape
+    return pl.pallas_call(
+        finish_kernel,
+        out_shape=(
+            jax.ShapeDtypeStruct((rows, columns), jnp.bfloat16),
+            jax.ShapeDtypeStruct((owned, columns), jnp.float32),
+        ),
+        in_specs=[pl.BlockSpec(memory_space=pltpu.SMEM), whole, whole, whole, whole],
+        out_specs=(whole, whole),
+        cost_estimate=pl.CostEstimate(
+            flops=6 * rows * columns * coefficients.shape[0],
+            bytes_accessed=4 * rows * columns,
+            transcendentals=512,
+        ),
+        compiler_params=pltpu.CompilerParams(vmem_limit_bytes=24 * 2**20),
+        name="finish",
+    )(first.reshape(1), energy, orthonormal, coefficients, weights)
+
+
 def on_device(weights, momentum, gradient, warm_basis):
     rows, columns = momentum.shape
     owned = warm_basis.shape[0]
@@ -236,19 +275,11 @@
     )
     coefficients = dot(inverse_own, moved, 1, 0, HIGH) + dot(inverse_other, handed, 1, 0, HIGH)
     energy = jnp.sum(coefficients * coefficients, axis=1).reshape(rank // 128, 128)
-    energy = total(spread(energy, COLUMN_BLOCKS, blocks), blocks).reshape(rank)
-    scale = lax.rsqrt(energy / FF + epsilon)
+    energy = spread(energy, COLUMN_BLOCKS, blocks).reshape(blocks, rank // 128, 128)
     feedback = dot(orthonormal, coefficients, 1, 0, HIGH)
     new_momentum = blended - (1.0 - momentum_decay) * feedback
-    update = dot(orthonormal * scale[None, :], coefficients, 1, 0, HIGH)
     first = (place * 2 + core) * owned
-    new_basis = (
-        lax.dynamic_slice_in_dim(coefficients, first, owned, 0)
-        * lax.dynamic_slice_in_dim(scale, first, owned, 0)[:, None]
-    )
-    new_weights = (weights.astype(jnp.float32) - step_size * math.sqrt(D / FF) * update).astype(
-        jnp.bfloat16
-    )
+    new_weights, new_basis = finish(first, energy, orthonormal, coefficients, weights, owned)
     return (new_weights, new_momentum, new_basis)
 
 

time: 220 us -> 218 us (level)
    dot_general x15 -> x14, matrix products: 14.8 us -> 13.2 us  [dot(): lax.dot_general(left_side, right_side, (((contract_left,), (contract_righ...]
  transfers between devices with their start and end apart: 7 -> 7, of which waited for: 3 -> 4; matrix products, arithmetic and copies ran while one was open for 4% -> 5% of each run, Pallas kernels for 7% -> 7%
where the time goes in v8:
time: 218 us; the launch traced here: 217 us
  blocking collectives  111 us (51%)
  starting transfers between devices  44.1 us (20%)
  Pallas kernels  17.4 us (8%)
  between operations  14.3 us (7%)
  waiting for transfers between devices  13.7 us (6%)
  matrix products  13.2 us (6%)
  other arithmetic  2.36 us (1%)
    all_to_all x4, blocking collectives, exchange(): return lax.all_to_all(array, axes, 0, 0, tiled=True)  56.3 us
    all_gather x1, blocking collectives, on_device(): basis = lax.all_gather(warm_basis, DEPTH, axis=0, tiled=True)  29 us
    all_gather x1, blocking collectives, on_device(): moved = lax.all_gather(moved + zero, DEPTH, axis=0, tiled=True)  25.3 us
    pallas_call x1, Pallas kernels, inverse_factor(): pl.pallas_call(functools.partial(inverse_factor_kernel, owned=owned), out...  15.6 us
    dot_general x14, matrix products, dot(): lax.dot_general(left_side, right_side, (((contract_left,), (contract_righ...  13.2 us
    all_to_all x2, waiting for transfers between devices, exchange(): return lax.all_to_all(array, axes, 0, 0, tiled=True)  12.1 us
    ppermute x1, starting transfers between devices, on_device(): others = lax.ppermute(projected, 'core', SWAP)  10.9 us
    ppermute x1, starting transfers between devices, on_device(): handed = lax.ppermute(moved, 'core', SWAP)  9.63 us
  transfers between devices with their start and end apart: 7, of which 4 were waited for; matrix products, arithmetic and copies ran while one was open for 5% of the time, Pallas kernels for 7%

profile of v8, /device:TPU:1, one launch (start us, length us, event | category | flops | bytes accessed | tf_op | source)
XLA Modules:
  0.0 217.3 jit_solution(7837164865016502636)
XLA Ops:
  7.2 1.4 convert_add_fusion
  8.6 8.8 %collective-permute-start = (f32[256,896]{1,0:T(8,128)S(1)}, f32[256,896]{1,0:T(8,128)S(1)}, u32[]{:S(2)}, u32[]{:S(2)}) collective-permute-start(f32[256,896]{1,0:T(8,128)S(1)} %convert_add_fusion), channel_id=1, source_target_pairs={{0,16},{16,0},{1,17},{17,1},{2,18},{18,2},{3,19},{19,3},{4,20},{20... | collective-permute-start | bytes 2752520 | tf_op jit(solution)/shard_map/ppermute | solution.py:237
  17.4 29.0 %all_gather.6 = f32[256,896]{1,0:T(8,128)S(1)} all-gather(f32[16,896]{1,0:T(8,128)S(1)} %copy-done.2), channel_id=1, replica_groups=mesh['far'=4,'near'=4,'core'=2,'x'=4,'y'=4] {'far','near'}, dimensions={0}, use_global_device_ids=true | all-gather | bytes 974848 | tf_op jit(solution)/shard_map/all_gather | solution.py:238
  46.4 1.0 fusion.85
  47.5 1.0 fusion.86
  48.5 15.5 %all_to_all.44 = f32[16,32,256]{2,1,0:T(8,128)S(1)} all-to-all(f32[16,32,256]{2,1,0:T(8,128)S(1)} %bitcast.35), channel_id=1, replica_groups=mesh['far'=4,'near'=4,'core'=2,'x'=4,'y'=4] {'x','y'}, dimensions={0} | all-to-all | bytes 1048576 | tf_op jit(solution)/shard_map/all_to_all | solution.py:35
  64.9 3.6 %all-to-all-start.1 = ((f32[16,32,256]{2,1,0:T(8,128)}), f32[16,32,256]{2,1,0:T(8,128)S(1)}, u32[]{:S(2)}, u32[]{:S(2)}) async-start(f32[16,32,256]{2,1,0:T(8,128)} %broadcast_in_dim.12), calls=%async_computation.1 | async-start | bytes 1048576 | tf_op jit(solution)/shard_map/all_to_all | solution.py:35
  68.6 8.8 %all-to-all-done.1 = f32[16,32,256]{2,1,0:T(8,128)S(1)} async-done(((f32[16,32,256]{2,1,0:T(8,128)}), f32[16,32,256]{2,1,0:T(8,128)S(1)}, u32[]{:S(2)}, u32[]{:S(2)}) %all-to-all-start.1) | async-done | bytes 524320 | tf_op jit(solution)/shard_map/all_to_all | solution.py:35
  77.4 10.9 %collective-permute-start.1 = (f32[512,256]{1,0:T(8,128)S(1)}, f32[512,256]{1,0:T(8,128)S(1)}, u32[]{:S(2)}, u32[]{:S(2)}) collective-permute-start(f32[512,256]{1,0:T(8,128)S(1)} %bitcast.30), channel_id=1, source_target_pairs={{0,16},{16,0},{1,17},{17,1},{2,18},{18,2},{3,19},{19,3},{4,20},{20... | collective-permute-start | bytes 1572872 | tf_op jit(solution)/shard_map/ppermute | solution.py:242
  89.0 1.6 convolution_add_fusion.1
  92.4 21.3 %all_to_all.45 = f32[4,16,512]{2,1,0:T(8,128)S(1)} all-to-all(f32[4,16,512]{2,1,0:T(8,128)S(1)} %broadcast_in_dim.13), channel_id=1, replica_groups=mesh['far'=4,'near'=4,'core'=2,'x'=4,'y'=4] {'far'}, dimensions={0} | all-to-all | bytes 262144 | tf_op jit(solution)/shard_map/all_to_all | solution.py:35
  113.7 7.8 %all_to_all.46 = f32[4,16,512]{2,1,0:T(8,128)S(1)} all-to-all(f32[4,16,512]{2,1,0:T(8,128)S(1)} %broadcast_in_dim.14), channel_id=1, replica_groups=mesh['far'=4,'near'=4,'core'=2,'x'=4,'y'=4] {'near'}, dimensions={0} | all-to-all | bytes 262144 | tf_op jit(solution)/shard_map/all_to_all | solution.py:35
  121.6 11.7 %all_to_all.47 = f32[16,16,512]{2,1,0:T(8,128)S(1)} all-to-all(f32[16,16,512]{2,1,0:T(8,128)S(1)} %broadcast_in_dim.15), channel_id=1, replica_groups=mesh['far'=4,'near'=4,'core'=2,'x'=4,'y'=4] {'x','y'}, dimensions={0} | all-to-all | bytes 1048576 | tf_op jit(solution)/shard_map/all_to_all | solution.py:35
  133.3 6.5 %collective-permute-start.2 = (f32[256,512]{1,0:T(8,128)S(1)}, f32[256,512]{1,0:T(8,128)S(1)}, u32[]{:S(2)}, u32[]{:S(2)}) collective-permute-start(f32[256,512]{1,0:T(8,128)S(1)} %bitcast.28), channel_id=1, source_target_pairs={{0,16},{16,0},{1,17},{17,1},{2,18},{18,2},{3,19},{19,3},{4,20},{20... | collective-permute-start | bytes 1572872 | tf_op jit(solution)/shard_map/ppermute | solution.py:266
  139.8 1.5 collective-permute-done.2.other_ref
  141.3 15.6 %inverse_factor.1 = (f32[512,512]{1,0:T(8,128)S(1)}, f32[16,896]{1,0:T(8,128)S(1)}) custom-call(s32[1]{0:T(128)} %bitcast.1.core_ref, f32[256,512]{1,0:T(8,128)S(1)} %bitcast.29, f32[256,512]{1,0:T(8,128)S(1)} %collective-permute-done.2.other_ref), custom_call_target="tpu_custom_call" | custom-call | flops 200000000 | bytes 2097152 | tf_op jit(solution)/shard_map/inverse_factor/pallas_call | solution.py:149
  157.7 25.3 %all_gather.7 = f32[256,896]{1,0:T(8,128)S(1)} all-gather(f32[16,896]{1,0:T(8,128)S(1)} %add.95), channel_id=1, replica_groups=mesh['far'=4,'near'=4,'core'=2,'x'=4,'y'=4] {'far','near'}, dimensions={0}, use_global_device_ids=true | all-gather | bytes 974848 | tf_op jit(solution)/shard_map/all_gather | solution.py:269
  183.0 9.6 %collective-permute-start.3 = (f32[256,896]{1,0:T(8,128)S(1)}, f32[256,896]{1,0:T(8,128)S(1)}, u32[]{:S(2)}, u32[]{:S(2)}) collective-permute-start(f32[256,896]{1,0:T(8,128)S(1)} %all_gather.7), channel_id=1, source_target_pairs={{0,16},{16,0},{1,17},{17,1},{2,18},{18,2},{3,19},{19,3},{4,20},{20... | collective-permute-start | bytes 2752520 | tf_op jit(solution)/shard_map/ppermute | solution.py:270
  194.6 1.0 fusion.88
  195.6 1.2 multiply_reduce_fusion
  197.4 4.7 %all-to-all-start.5 = ((f32[16,4,128]{2,1,0:T(4,128)}), f32[16,4,128]{2,1,0:T(4,128)S(1)}, u32[]{:S(2)}, u32[]{:S(2)}) async-start(f32[16,4,128]{2,1,0:T(4,128)} %broadcast_in_dim.17), calls=%async_computation.6 | async-start | bytes 65536 | tf_op jit(solution)/shard_map/all_to_all | solution.py:35
  202.1 3.2 %fusion = f32[256,896]{1,0:T(8,128)} fusion(f32[256,896]{1,0:T(8,128)} %copy-done.1, f32[256,512]{1,0:T(8,128)S(1)} %convolution_add_fusion.2.orthonormal_ref, f32[512,896]{1,0:T(8,128)S(1)} %get-tuple-element.16.coefficients_ref), kind=kOutput, calls=%fused_computation.8 | convolution fusion | flops 705101824 | bytes 4194304 | tf_op jit(solution)/shard_map/dot_general | solution.py:25
  205.3 3.3 %all-to-all-done.5.energy_ref = f32[16,4,128]{2,1,0:T(4,128)S(1)} async-done(((f32[16,4,128]{2,1,0:T(4,128)}), f32[16,4,128]{2,1,0:T(4,128)S(1)}, u32[]{:S(2)}, u32[]{:S(2)}) %all-to-all-start.5) | async-done | bytes 32800 | tf_op jit(solution)/shard_map/all_to_all | solution.py:35
  208.6 1.9 finish.1
  (40 shorter events, 6.9 us)
Async XLA Ops:
  7.2 10.2 %copy-start.2 = (f32[16,896]{1,0:T(8,128)S(1)}, f32[16,896]{1,0:T(8,128)}, u32[]{:S(2)}) copy-start(f32[16,896]{1,0:T(8,128)} %param.7) | copy-start | bytes 172036
  8.6 79.8 %copy-start.1 = (f32[256,896]{1,0:T(8,128)}, f32[256,896]{1,0:T(8,128)S(1)}, u32[]{:S(2)}) copy-start(f32[256,896]{1,0:T(8,128)S(1)} %convert_add_fusion) | copy-start | bytes 2752516
  8.6 38.9 %collective-permute-start = (f32[256,896]{1,0:T(8,128)S(1)}, f32[256,896]{1,0:T(8,128)S(1)}, u32[]{:S(2)}, u32[]{:S(2)}) collective-permute-start(f32[256,896]{1,0:T(8,128)S(1)} %convert_add_fusion), channel_id=1, source_target_pairs={{0,16},{16,0},{1,17},{17,1},{2,18},{18,2},{3,19},{19,3},{4,20},{20... | collective-permute-start | bytes 2752520 | tf_op jit(solution)/shard_map/ppermute | solution.py:237
  64.9 12.5 %all-to-all-start.1 = ((f32[16,32,256]{2,1,0:T(8,128)}), f32[16,32,256]{2,1,0:T(8,128)S(1)}, u32[]{:S(2)}, u32[]{:S(2)}) async-start(f32[16,32,256]{2,1,0:T(8,128)} %broadcast_in_dim.12), calls=%async_computation.1 | async-start | bytes 1048576 | tf_op jit(solution)/shard_map/all_to_all | solution.py:35
  68.5 88.4 %reduce-scatter.2.cloned.1.call-start = ((), (), s32[]{:S(2)}) async-start(), calls=%async_computation.7 | async-start | bytes 974848 | tf_op jit(solution)/shard_map/reduce_scatter | solution.py:248
  77.4 13.8 %collective-permute-start.1 = (f32[512,256]{1,0:T(8,128)S(1)}, f32[512,256]{1,0:T(8,128)S(1)}, u32[]{:S(2)}, u32[]{:S(2)}) collective-permute-start(f32[512,256]{1,0:T(8,128)S(1)} %bitcast.30), channel_id=1, source_target_pairs={{0,16},{16,0},{1,17},{17,1},{2,18},{18,2},{3,19},{19,3},{4,20},{20... | collective-permute-start | bytes 1572872 | tf_op jit(solution)/shard_map/ppermute | solution.py:242
  133.3 8.0 %collective-permute-start.2 = (f32[256,512]{1,0:T(8,128)S(1)}, f32[256,512]{1,0:T(8,128)S(1)}, u32[]{:S(2)}, u32[]{:S(2)}) collective-permute-start(f32[256,512]{1,0:T(8,128)S(1)} %bitcast.28), channel_id=1, source_target_pairs={{0,16},{16,0},{1,17},{17,1},{2,18},{18,2},{3,19},{19,3},{4,20},{20... | collective-permute-start | bytes 1572872 | tf_op jit(solution)/shard_map/ppermute | solution.py:266
  183.0 11.5 %collective-permute-start.3 = (f32[256,896]{1,0:T(8,128)S(1)}, f32[256,896]{1,0:T(8,128)S(1)}, u32[]{:S(2)}, u32[]{:S(2)}) collective-permute-start(f32[256,896]{1,0:T(8,128)S(1)} %all_gather.7), channel_id=1, source_target_pairs={{0,16},{16,0},{1,17},{17,1},{2,18},{18,2},{3,19},{19,3},{4,20},{20... | collective-permute-start | bytes 2752520 | tf_op jit(solution)/shard_map/ppermute | solution.py:270
  197.4 11.2 %all-to-all-start.5 = ((f32[16,4,128]{2,1,0:T(4,128)}), f32[16,4,128]{2,1,0:T(4,128)S(1)}, u32[]{:S(2)}, u32[]{:S(2)}) async-start(f32[16,4,128]{2,1,0:T(4,128)} %broadcast_in_dim.17), calls=%async_computation.6 | async-start | bytes 65536 | tf_op jit(solution)/shard_map/all_to_all | solution.py:35
  202.1 6.5 %copy-start = (bf16[256,896]{1,0:T(8,128)(2,1)S(1)}, bf16[256,896]{1,0:T(8,128)(2,1)}, u32[]{:S(2)}) copy-start(bf16[256,896]{1,0:T(8,128)(2,1)} %weights_ref.1) | copy-start | bytes 1376260
Sparse Core Ops, SparseCore 0:
  90.7 55.2 reduce-scatter.1

commit v9 on v8

--- a/solution.py
+++ b/solution.py
@@ -184,7 +184,15 @@
 
 
 def finish_kernel(
-    first_ref, energy_ref, orthonormal_ref, coefficients_ref, weights_ref, out_ref, basis_ref
+    first_ref,
+    energy_ref,
+    orthonormal_ref,
+    coefficients_ref,
+    weights_ref,
+    blended_ref,
+    out_ref,
+    basis_ref,
+    momentum_ref,
 ):
     owned = basis_ref.shape[0]
     energy = jnp.sum(energy_ref[...], axis=0)
@@ -195,13 +203,17 @@
     column = lax.broadcasted_iota(jnp.int32, (owned, scale.shape[1]), 1)
     own = jnp.sum(jnp.where(row == column, scale, 0.0), axis=1, keepdims=True)
     basis_ref[...] = coefficients_ref[pl.ds(pl.multiple_of(first_ref[0], owned), owned), :] * own
-    update = dot(orthonormal_ref[...] * scale, coefficients, 1, 0, HIGH)
+    orthonormal = orthonormal_ref[...]
+    rows = orthonormal.shape[0]
+    both = dot(jnp.concatenate([orthonormal * scale, orthonormal]), coefficients, 1, 0, HIGH)
+    update = both[:rows]
+    momentum_ref[...] = blended_ref[...] - (1.0 - momentum_decay) * both[rows:]
     out_ref[...] = (
         weights_ref[...].astype(jnp.float32) - step_size * math.sqrt(D / FF) * update
     ).astype(jnp.bfloat16)
 
 
-def finish(first, energy, orthonormal, coefficients, weights, owned):
+def finish(first, energy, orthonormal, coefficients, weights, blended, owned):
     whole = pl.BlockSpec(memory_space=pltpu.VMEM)
     rows, columns = weights.shape
     return pl.pallas_call(
@@ -209,9 +221,10 @@
         out_shape=(
             jax.ShapeDtypeStruct((rows, columns), jnp.bfloat16),
             jax.ShapeDtypeStruct((owned, columns), jnp.float32),
-        ),
-        in_specs=[pl.BlockSpec(memory_space=pltpu.SMEM), whole, whole, whole, whole],
-        out_specs=(whole, whole),
+            jax.ShapeDtypeStruct((rows, columns), jnp.float32),
+        ),
+        in_specs=[pl.BlockSpec(memory_space=pltpu.SMEM)] + [whole] * 5,
+        out_specs=(whole,) * 3,
         cost_estimate=pl.CostEstimate(
             flops=6 * rows * columns * coefficients.shape[0],
             bytes_accessed=4 * rows * columns,
@@ -219,7 +232,7 @@
         ),
         compiler_params=pltpu.CompilerParams(vmem_limit_bytes=24 * 2**20),
         name="finish",
-    )(first.reshape(1), energy, orthonormal, coefficients, weights)
+    )(first.reshape(1), energy, orthonormal, coefficients, weights, blended)
 
 
 def on_device(weights, momentum, gradient, warm_basis):
@@ -276,10 +289,10 @@
     coefficients = dot(inverse_own, moved, 1, 0, HIGH) + dot(inverse_other, handed, 1, 0, HIGH)
     energy = jnp.sum(coefficients * coefficients, axis=1).reshape(rank // 128, 128)
     energy = spread(energy, COLUMN_BLOCKS, blocks).reshape(blocks, rank // 128, 128)
-    feedback = dot(orthonormal, coefficients, 1, 0, HIGH)
-    new_momentum = blended - (1.0 - momentum_decay) * feedback
     first = (place * 2 + core) * owned
-    new_weights, new_basis = finish(first, energy, orthonormal, coefficients, weights, owned)
+    new_weights, new_basis, new_momentum = finish(
+        first, energy, orthonormal, coefficients, weights, blended, owned
+    )
     return (new_weights, new_momentum, new_basis)
 
 

time: 218 us -> 223 us (1.023)
    dot_general x14 -> x13, matrix products: 13.2 us -> 13.3 us  [dot(): lax.dot_general(left_side, right_side, (((contract_left,), (contract_righ...]
  transfers between devices with their start and end apart: 7 -> 7, of which waited for: 4 -> 3; matrix products, arithmetic and copies ran while one was open for 5% -> 4% of each run, Pallas kernels for 7% -> 7%
where the time goes in v9:
time: 223 us; the launch traced here: 222 us
  blocking collectives  111 us (50%)
  starting transfers between devices  43.8 us (20%)
  Pallas kernels  18.5 us (8%)
  waiting for transfers between devices  15.1 us (7%)
  between operations  14.3 us (6%)
  matrix products  13.3 us (6%)
  local copies, waits for them, and re-layouts  3.45 us (2%)
  other arithmetic  2.36 us (1%)
    all_to_all x4, blocking collectives, exchange(): return lax.all_to_all(array, axes, 0, 0, tiled=True)  56.5 us
    all_gather x1, blocking collectives, on_device(): basis = lax.all_gather(warm_basis, DEPTH, axis=0, tiled=True)  29 us
    all_gather x1, blocking collectives, on_device(): moved = lax.all_gather(moved + zero, DEPTH, axis=0, tiled=True)  25.5 us
    pallas_call x1, Pallas kernels, inverse_factor(): pl.pallas_call(functools.partial(inverse_factor_kernel, owned=owned), out...  15.6 us
    all_to_all x2, waiting for transfers between devices, exchange(): return lax.all_to_all(array, axes, 0, 0, tiled=True)  13.6 us
    dot_general x13, matrix products, dot(): lax.dot_general(left_side, right_side, (((contract_left,), (contract_righ...  13.3 us
    ppermute x1, starting transfers between devices, on_device(): others = lax.ppermute(projected, 'core', SWAP)  10.9 us
    ppermute x1, starting transfers between devices, on_device(): handed = lax.ppermute(moved, 'core', SWAP)  9.44 us
  transfers between devices with their start and end apart: 7, of which 3 were waited for; matrix products, arithmetic and copies ran while one was open for 4% of the time, Pallas kernels for 7%

profile of v9, /device:TPU:1, one launch (start us, length us, event | category | flops | bytes accessed | tf_op | source)
XLA Modules:
  0.0 221.9 jit_solution(3124793313081749201)
XLA Ops:
  7.2 1.4 convert_add_fusion.blended_ref
  8.6 8.8 %collective-permute-start = (f32[256,896]{1,0:T(8,128)S(1)}, f32[256,896]{1,0:T(8,128)S(1)}, u32[]{:S(2)}, u32[]{:S(2)}) collective-permute-start(f32[256,896]{1,0:T(8,128)S(1)} %convert_add_fusion.blended_ref), channel_id=1, source_target_pairs={{0,16},{16,0},{1,17},{17,1},{2,18},{18,2},{3,19},{19,3},{4,20},{20... | collective-permute-start | bytes 2752520 | tf_op jit(solution)/shard_map/ppermute | solution.py:250
  17.4 29.0 %all_gather.6 = f32[256,896]{1,0:T(8,128)S(1)} all-gather(f32[16,896]{1,0:T(8,128)S(1)} %copy-done.5), channel_id=1, replica_groups=mesh['far'=4,'near'=4,'core'=2,'x'=4,'y'=4] {'far','near'}, dimensions={0}, use_global_device_ids=true | all-gather | bytes 974848 | tf_op jit(solution)/shard_map/all_gather | solution.py:251
  47.4 1.0 fusion.85
  48.5 15.5 %all_to_all.44 = f32[16,32,256]{2,1,0:T(8,128)S(1)} all-to-all(f32[16,32,256]{2,1,0:T(8,128)S(1)} %bitcast.33), channel_id=1, replica_groups=mesh['far'=4,'near'=4,'core'=2,'x'=4,'y'=4] {'x','y'}, dimensions={0} | all-to-all | bytes 1048576 | tf_op jit(solution)/shard_map/all_to_all | solution.py:35
  64.9 3.6 %all-to-all-start.1 = ((f32[16,32,256]{2,1,0:T(8,128)}), f32[16,32,256]{2,1,0:T(8,128)S(1)}, u32[]{:S(2)}, u32[]{:S(2)}) async-start(f32[16,32,256]{2,1,0:T(8,128)} %broadcast_in_dim.12), calls=%async_computation.1 | async-start | bytes 1048576 | tf_op jit(solution)/shard_map/all_to_all | solution.py:35
  68.6 8.8 %all-to-all-done.1 = f32[16,32,256]{2,1,0:T(8,128)S(1)} async-done(((f32[16,32,256]{2,1,0:T(8,128)}), f32[16,32,256]{2,1,0:T(8,128)S(1)}, u32[]{:S(2)}, u32[]{:S(2)}) %all-to-all-start.1) | async-done | bytes 524320 | tf_op jit(solution)/shard_map/all_to_all | solution.py:35
  77.4 10.9 %collective-permute-start.1 = (f32[512,256]{1,0:T(8,128)S(1)}, f32[512,256]{1,0:T(8,128)S(1)}, u32[]{:S(2)}, u32[]{:S(2)}) collective-permute-start(f32[512,256]{1,0:T(8,128)S(1)} %bitcast.28), channel_id=1, source_target_pairs={{0,16},{16,0},{1,17},{17,1},{2,18},{18,2},{3,19},{19,3},{4,20},{20... | collective-permute-start | bytes 1572872 | tf_op jit(solution)/shard_map/ppermute | solution.py:255
  89.0 1.5 convolution_add_fusion.1
  92.4 21.3 %all_to_all.45 = f32[4,16,512]{2,1,0:T(8,128)S(1)} all-to-all(f32[4,16,512]{2,1,0:T(8,128)S(1)} %broadcast_in_dim.13), channel_id=1, replica_groups=mesh['far'=4,'near'=4,'core'=2,'x'=4,'y'=4] {'far'}, dimensions={0} | all-to-all | bytes 262144 | tf_op jit(solution)/shard_map/all_to_all | solution.py:35
  113.7 8.1 %all_to_all.46 = f32[4,16,512]{2,1,0:T(8,128)S(1)} all-to-all(f32[4,16,512]{2,1,0:T(8,128)S(1)} %broadcast_in_dim.14), channel_id=1, replica_groups=mesh['far'=4,'near'=4,'core'=2,'x'=4,'y'=4] {'near'}, dimensions={0} | all-to-all | bytes 262144 | tf_op jit(solution)/shard_map/all_to_all | solution.py:35
  121.9 11.6 %all_to_all.47 = f32[16,16,512]{2,1,0:T(8,128)S(1)} all-to-all(f32[16,16,512]{2,1,0:T(8,128)S(1)} %broadcast_in_dim.15), channel_id=1, replica_groups=mesh['far'=4,'near'=4,'core'=2,'x'=4,'y'=4] {'x','y'}, dimensions={0} | all-to-all | bytes 1048576 | tf_op jit(solution)/shard_map/all_to_all | solution.py:35
  133.5 6.3 %collective-permute-start.2 = (f32[256,512]{1,0:T(8,128)S(1)}, f32[256,512]{1,0:T(8,128)S(1)}, u32[]{:S(2)}, u32[]{:S(2)}) collective-permute-start(f32[256,512]{1,0:T(8,128)S(1)} %bitcast.26), channel_id=1, source_target_pairs={{0,16},{16,0},{1,17},{17,1},{2,18},{18,2},{3,19},{19,3},{4,20},{20... | collective-permute-start | bytes 1572872 | tf_op jit(solution)/shard_map/ppermute | solution.py:279
  139.8 1.5 collective-permute-done.2.other_ref
  141.3 15.6 %inverse_factor.1 = (f32[512,512]{1,0:T(8,128)S(1)}, f32[16,896]{1,0:T(8,128)S(1)}) custom-call(s32[1]{0:T(128)} %bitcast.1.core_ref, f32[256,512]{1,0:T(8,128)S(1)} %bitcast.27, f32[256,512]{1,0:T(8,128)S(1)} %collective-permute-done.2.other_ref), custom_call_target="tpu_custom_call" | custom-call | flops 200000000 | bytes 2097152 | tf_op jit(solution)/shard_map/inverse_factor/pallas_call | solution.py:149
  157.7 25.5 %all_gather.7 = f32[256,896]{1,0:T(8,128)S(1)} all-gather(f32[16,896]{1,0:T(8,128)S(1)} %add.95), channel_id=1, replica_groups=mesh['far'=4,'near'=4,'core'=2,'x'=4,'y'=4] {'far','near'}, dimensions={0}, use_global_device_ids=true | all-gather | bytes 974848 | tf_op jit(solution)/shard_map/all_gather | solution.py:282
  183.2 9.4 %collective-permute-start.3 = (f32[256,896]{1,0:T(8,128)S(1)}, f32[256,896]{1,0:T(8,128)}, u32[]{:S(2)}, u32[]{:S(2)}) collective-permute-start(f32[256,896]{1,0:T(8,128)S(1)} %all_gather.7), channel_id=1, source_target_pairs={{0,16},{16,0},{1,17},{17,1},{2,18},{18,2},{3,19},{19,3},{4,20},{20... | collective-permute-start | bytes 2752520 | tf_op jit(solution)/shard_map/ppermute | solution.py:283
  193.2 1.2 fusion.88
  195.7 2.3 %fusion.87 = f32[512,896]{1,0:T(8,128)S(1)} fusion(f32[512,256]{1,0:T(8,128)S(1)} %fusion.24, f32[256,896]{1,0:T(8,128)} %collective-permute-done.3), kind=kOutput, calls=%fused_computation.112 | convolution fusion | flops 704643072 | bytes 3276800 | tf_op jit(solution)/shard_map/dot_general | solution.py:25
  198.0 1.2 multiply_reduce_fusion
  199.8 4.9 %all-to-all-start.5 = ((f32[16,4,128]{2,1,0:T(4,128)}), f32[16,4,128]{2,1,0:T(4,128)S(1)}, u32[]{:S(2)}, u32[]{:S(2)}) async-start(f32[16,4,128]{2,1,0:T(4,128)} %broadcast_in_dim.17), calls=%async_computation.6 | async-start | bytes 65536 | tf_op jit(solution)/shard_map/all_to_all | solution.py:35
  204.7 1.7 convolution_add_fusion.2.orthonormal_ref
  206.4 4.8 %all-to-all-done.5.energy_ref = f32[16,4,128]{2,1,0:T(4,128)S(1)} async-done(((f32[16,4,128]{2,1,0:T(4,128)}), f32[16,4,128]{2,1,0:T(4,128)S(1)}, u32[]{:S(2)}, u32[]{:S(2)}) %all-to-all-start.5) | async-done | bytes 32800 | tf_op jit(solution)/shard_map/all_to_all | solution.py:35
  212.2 2.9 %finish.1 = (bf16[256,896]{1,0:T(8,128)(2,1)}, f32[16,896]{1,0:T(8,128)}, f32[256,896]{1,0:T(8,128)}) custom-call(s32[1]{0:T(128)} %bitcast.first_ref, f32[16,4,128]{2,1,0:T(4,128)S(1)} %all-to-all-done.5.energy_ref, f32[256,512]{1,0:T(8,128)S(1)} %convolution_add_fusion.2.orthonormal_ref, f32[512,896]{1,0:T(8,128)S(1)} %get-tuple-element.18.coefficients_ref, ...), custom_call_target="tpu_custom_call" | custom-call | flops 704643072 | bytes 917504 | tf_op jit(solution)/shard_map/finish/pallas_call | solution.py:219
  (45 shorter events, 8.8 us)
Async XLA Ops:
  7.2 10.2 %copy-start.5 = (f32[16,896]{1,0:T(8,128)S(1)}, f32[16,896]{1,0:T(8,128)}, u32[]{:S(2)}) copy-start(f32[16,896]{1,0:T(8,128)} %param.7) | copy-start | bytes 172036
  8.6 38.9 %collective-permute-start = (f32[256,896]{1,0:T(8,128)S(1)}, f32[256,896]{1,0:T(8,128)S(1)}, u32[]{:S(2)}, u32[]{:S(2)}) collective-permute-start(f32[256,896]{1,0:T(8,128)S(1)} %convert_add_fusion.blended_ref), channel_id=1, source_target_pairs={{0,16},{16,0},{1,17},{17,1},{2,18},{18,2},{3,19},{19,3},{4,20},{20... | collective-permute-start | bytes 2752520 | tf_op jit(solution)/shard_map/ppermute | solution.py:250
  64.9 12.5 %all-to-all-start.1 = ((f32[16,32,256]{2,1,0:T(8,128)}), f32[16,32,256]{2,1,0:T(8,128)S(1)}, u32[]{:S(2)}, u32[]{:S(2)}) async-start(f32[16,32,256]{2,1,0:T(8,128)} %broadcast_in_dim.12), calls=%async_computation.1 | async-start | bytes 1048576 | tf_op jit(solution)/shard_map/all_to_all | solution.py:35
  68.5 88.4 %reduce-scatter.2.cloned.1.call-start = ((), (), s32[]{:S(2)}) async-start(), calls=%async_computation.7 | async-start | bytes 974848 | tf_op jit(solution)/shard_map/reduce_scatter | solution.py:261
  77.4 13.8 %collective-permute-start.1 = (f32[512,256]{1,0:T(8,128)S(1)}, f32[512,256]{1,0:T(8,128)S(1)}, u32[]{:S(2)}, u32[]{:S(2)}) collective-permute-start(f32[512,256]{1,0:T(8,128)S(1)} %bitcast.28), channel_id=1, source_target_pairs={{0,16},{16,0},{1,17},{17,1},{2,18},{18,2},{3,19},{19,3},{4,20},{20... | collective-permute-start | bytes 1572872 | tf_op jit(solution)/shard_map/ppermute | solution.py:255
  91.2 1.2 copy-start.4
  133.5 7.8 %collective-permute-start.2 = (f32[256,512]{1,0:T(8,128)S(1)}, f32[256,512]{1,0:T(8,128)S(1)}, u32[]{:S(2)}, u32[]{:S(2)}) collective-permute-start(f32[256,512]{1,0:T(8,128)S(1)} %bitcast.26), channel_id=1, source_target_pairs={{0,16},{16,0},{1,17},{17,1},{2,18},{18,2},{3,19},{19,3},{4,20},{20... | collective-permute-start | bytes 1572872 | tf_op jit(solution)/shard_map/ppermute | solution.py:279
  183.2 11.7 %copy-start.2 = (f32[256,896]{1,0:T(8,128)}, f32[256,896]{1,0:T(8,128)S(1)}, u32[]{:S(2)}) copy-start(f32[256,896]{1,0:T(8,128)S(1)} %all_gather.7) | copy-start | bytes 2752516
  183.2 11.7 %collective-permute-start.3 = (f32[256,896]{1,0:T(8,128)S(1)}, f32[256,896]{1,0:T(8,128)}, u32[]{:S(2)}, u32[]{:S(2)}) collective-permute-start(f32[256,896]{1,0:T(8,128)S(1)} %all_gather.7), channel_id=1, source_target_pairs={{0,16},{16,0},{1,17},{17,1},{2,18},{18,2},{3,19},{19,3},{4,20},{20... | collective-permute-start | bytes 2752520 | tf_op jit(solution)/shard_map/ppermute | solution.py:283
  194.9 0.8 copy-start.1
  195.7 2.3 %copy-start.3 = (f32[256,896]{1,0:T(8,128)S(1)}, f32[256,896]{1,0:T(8,128)}, u32[]{:S(2)}) copy-start(f32[256,896]{1,0:T(8,128)} %copy-done.2) | copy-start | bytes 2752516
  199.8 11.3 %all-to-all-start.5 = ((f32[16,4,128]{2,1,0:T(4,128)}), f32[16,4,128]{2,1,0:T(4,128)S(1)}, u32[]{:S(2)}, u32[]{:S(2)}) async-start(f32[16,4,128]{2,1,0:T(4,128)} %broadcast_in_dim.17), calls=%async_computation.6 | async-start | bytes 65536 | tf_op jit(solution)/shard_map/all_to_all | solution.py:35
  211.2 1.0 copy-start
Sparse Core Ops, SparseCore 0:
  90.7 55.0 reduce-scatter.1
